TPU v7x, 256 devices: a whole 4x4x8 slice. The times are simulated.
256 devices in a mesh: blk: 8 (over x, y_lo), rep: 32 (over y_hi, z, core).
Axes of the slice: x: 4, y: 4 (y_hi: 2, y_lo: 2; y = y_hi * 2 + y_lo), z: 8, core: 2. Of those that a mesh axis runs over, the one named last changes fastest.
Arguments:
- tokens: bfloat16 [65536, 4096], P(('blk', 'rep'))
- grad_attended: bfloat16 [65536, 1024], P(('blk', 'rep'))
- doc_ids: int32 [256, 256], P(('blk', 'rep')), may hold values from 0 to 3, never falling along the last dimension, each value on 1 to 128 neighbouring positions
- w_qkv: bfloat16 [4096, 1280], P('blk')
Outputs:
- d_tokens: bfloat16 [65536, 4096], P(('blk', 'rep'))
- grad_qkv: bfloat16 [4096, 1280], P('blk')
Inputs may be any that keep to these rules, and one draw needn't show every extreme that they name: `doc_ids`: along each row ids never fall; every document holds 1 to 128 tokens.
All inputs are finite; a program needn't handle non-finite values.
Results may differ from a plain program's by a relative error of at most 0.035.
Values may be sent and summed in bfloat16 or wider, within the bound.
No kernel may reach another device: no remote copies, remote signals or barrier semaphores. Data moves between devices by JAX's collectives and lax.ppermute only.
A program may use at most 128 MiB of HBM per device.

v0:
```python
import jax
import jax.numpy as jnp
from jax import lax
from jax.experimental import pallas as pl
from jax.experimental.pallas import tpu as pltpu
from jax.sharding import Mesh
from jax.sharding import PartitionSpec as P

D = 4096
HD = 128
QH = 8
QKV = 1280
TOK = 256
BLK = D // 8
HALF = BLK // 2
QUART = HALF // 2
PIECE = QUART // 8
COLS = QKV // 2
OUTW = QH * HD
LOW = COLS // HD

AXES = ("x", "y_lo", "y_hi", "z", "core")
SIZES = (4, 2, 2, 8, 2)
target_rms = 0.5
rope_base = 500000.0
F32 = jnp.float32
BF16 = jnp.bfloat16


def place():
    x, y_lo, y_hi, z, c = (lax.axis_index(axis) for axis in AXES)
    return x, y_hi * 2 + y_lo, z, c


def flat(x, y, z, c):
    return (x * 2 + y % 2) * 32 + (y // 2) * 16 + z * 2 + c


def swap(value, partner):
    pairs = []
    for x in range(4):
        for y in range(4):
            for z in range(8):
                for c in range(2):
                    pairs.append((flat(x, y, z, c), flat(*partner(x, y, z, c))))
    return lax.ppermute(value, AXES, pairs)


def near(c):
    return 1 if c == 0 else 3


def other_core(x, y, z, c):
    return x, y, z, 1 - c


def gather_x1(x, y, z, c):
    return x ^ near(c ^ (z & 1)), y, z, c


def gather_x2(x, y, z, c):
    return x ^ (4 - near(c ^ (z & 1))), y, z, c


def flip_y(x, y, z, c):
    return x, y ^ near(c), z, c


def pair_z(x, y, z, c):
    return x, y, (z ^ 1) if c == 0 else ((z + 1) % 8 if z % 2 else (z - 1) % 8), c


def x_1(x, y, z, c):
    return x ^ near(c), y, z, c


def x_2(x, y, z, c):
    return x ^ (4 - near(c)), y, z, c


def y_1(x, y, z, c):
    return x, y ^ near(c), z, c


def y_2(x, y, z, c):
    return x, y ^ (4 - near(c)), z, c


VM = pl.BlockSpec(memory_space=pltpu.VMEM)
SM = pl.BlockSpec(memory_space=pltpu.SMEM)
ANY = pl.BlockSpec(memory_space=pl.ANY)


def dot(a, b, dims):
    return lax.dot_general(a, b, (dims, ((), ())), preferred_element_type=F32)


def norm_body(c, tokens, normed, scale_r, mine, theirs):
    full = tokens[...].astype(F32)
    r = lax.rsqrt(jnp.sum(full * full, axis=1, keepdims=True) * (1.0 / D) + 1e-05)
    scale_r[...] = r
    normed[...] = (full * r).astype(BF16)
    for b in range(8):
        for half, out in ((c[0], mine), (1 - c[0], theirs)):
            cols = pl.ds(pl.multiple_of(b * BLK + half * HALF, HALF), HALF)
            out[b * HALF : (b + 1) * HALF, :] = normed[:, cols].T


def norm(c, tokens):
    turned = jax.ShapeDtypeStruct((D // 2, TOK), BF16)
    return pl.pallas_call(
        norm_body,
        out_shape=(
            jax.ShapeDtypeStruct((TOK, D), BF16),
            jax.ShapeDtypeStruct((TOK, 1), F32),
            turned,
            turned,
        ),
        in_specs=[SM, VM],
        out_specs=(VM, VM, VM, VM),
        compiler_params=pltpu.CompilerParams(vmem_limit_bytes=12 << 20),
        cost_estimate=pl.CostEstimate(flops=10 * TOK * D, bytes_accessed=6 << 20, transcendentals=0),
        name="norm",
    )(c.reshape(1).astype(jnp.int32), tokens)


def halves(pieces):
    return [piece.at[pl.ds(k, HALF), :] for piece in pieces for k in range(0, piece.shape[0], HALF)]


def fetch(pieces, held, sems):
    copies = []
    for i, piece in enumerate(halves(pieces)):
        copies.append(pltpu.make_async_copy(piece, held.at[pl.ds(i * HALF, HALF), :], sems.at[i]))
        copies[-1].start()
    return copies


def project(total, at, normed, held, copies, chunk):
    for first in range(0, len(copies), chunk):
        lhs = []
        for i in range(first, min(first + chunk, len(copies))):
            copies[i].wait()
            lhs.append(normed[:, pl.ds(pl.multiple_of(at[i], HALF), HALF)])
        rows = slice(first * HALF, (first + len(lhs)) * HALF)
        part = dot(jnp.concatenate(lhs, axis=1), held[rows, :], ((1,), (0,)))
        total = part if total is None else total + part
    return total


def part_body(count, at, normed, *refs):
    pieces, out, held, sems = refs[:count], refs[count], refs[count + 1], refs[count + 2]
    out[...] = project(None, at, normed, held, fetch(pieces, held, sems), 4)


def part_qkv(at, normed, pieces):
    count, rows = len(pieces), at.shape[0] * HALF
    return pl.pallas_call(
        lambda *refs: part_body(count, *refs),
        out_shape=jax.ShapeDtypeStruct((TOK, QKV), F32),
        in_specs=[SM, VM] + [ANY] * count,
        out_specs=VM,
        scratch_shapes=[pltpu.VMEM((rows, QKV), BF16), pltpu.SemaphoreType.DMA((rows // HALF,))],
        compiler_params=pltpu.CompilerParams(vmem_limit_bytes=20 << 20),
        cost_estimate=pl.CostEstimate(
            flops=2 * TOK * rows * QKV, bytes_accessed=rows * QKV * 2, transcendentals=0
        ),
        name="qkv_part",
    )(at, normed, *pieces)


def visible(doc_row, doc_col):
    rows = lax.broadcasted_iota(jnp.int32, (TOK, TOK), 0)
    cols = lax.broadcasted_iota(jnp.int32, (TOK, TOK), 1)
    return (cols <= rows) & (doc_col[...] == doc_row[...])


def turn(value, cos, sin):
    return value * cos + pltpu.roll(value, HD // 2, 1) * sin


def head_grads(q_rot, g, k_rot, val, seen, cos, sin):
    scale = HD**-0.5
    scores = jnp.where(seen, dot(q_rot, k_rot, ((1,), (1,))), -1e30)
    expo = jnp.exp((scores - jnp.max(scores, axis=1, keepdims=True)) * scale)
    probs = expo * (1.0 / jnp.sum(expo, axis=1, keepdims=True))
    d_probs = dot(g, val, ((1,), (1,)))
    delta = jnp.sum(d_probs * probs, axis=1, keepdims=True)
    d_scores = (probs * (d_probs - delta)).astype(BF16)
    d_val = dot(probs.astype(BF16), g, ((0,), (0,)))
    d_key = dot(d_scores, q_rot, ((0,), (0,)))
    d_query = dot(d_scores, k_rot, ((1,), (0,))) * scale
    return turn(d_query, cos, -sin).astype(BF16), d_key, d_val


def attend_low_body(count, at, normed, old, grad, doc_row, doc_col, cosine, sine, *refs):
    pieces = refs[:count]
    out, rest, d_key, d_val, held, sems, qkv = refs[count:]
    qkv[...] = project(old[...], at, normed, held, fetch(pieces, held, sems), 2)
    cos, sin = cosine[...], sine[...]
    seen = visible(doc_row, doc_col)
    k_rot = turn(qkv[:, OUTW : OUTW + HD], cos, sin).astype(BF16)
    val = qkv[:, OUTW + HD :].astype(BF16)
    total_key, total_val = jnp.zeros((TOK, HD), F32), jnp.zeros((TOK, HD), F32)
    for h in range(QH):
        head = slice(h * HD, (h + 1) * HD)
        q_rot = turn(qkv[:, head], cos, sin).astype(BF16)
        if h < LOW:
            out[:, head], key, value = head_grads(q_rot, grad[:, head], k_rot, val, seen, cos, sin)
            total_key, total_val = total_key + key, total_val + value
        else:
            rest[:, (h - LOW) * HD : (h - LOW + 1) * HD] = q_rot
    rest[:, COLS - 2 * HD : COLS - HD] = k_rot
    rest[:, COLS - HD :] = val
    d_key[...] = total_key
    d_val[...] = total_val


def attend_high_body(rest, key_low, val_low, grad, doc_row, doc_col, cosine, sine, out):
    cos, sin = cosine[...], sine[...]
    seen = visible(doc_row, doc_col)
    k_rot, val = rest[:, COLS - 2 * HD : COLS - HD], rest[:, COLS - HD :]
    total_key, total_val = key_low[...], val_low[...]
    for h in range(LOW, QH):
        here = slice((h - LOW) * HD, (h - LOW + 1) * HD)
        g = grad[:, h * HD : (h + 1) * HD]
        out[:, here], key, value = head_grads(rest[:, here], g, k_rot, val, seen, cos, sin)
        total_key, total_val = total_key + key, total_val + value
    out[:, COLS - 2 * HD : COLS - HD] = turn(total_key * HD**-0.5, cos, -sin).astype(BF16)
    out[:, COLS - HD :] = total_val.astype(BF16)


def attend_cost(heads):
    return pl.CostEstimate(
        flops=10 * TOK * TOK * HD * heads, bytes_accessed=4 << 20, transcendentals=TOK * TOK * heads
    )


def attend_low(at, normed, pieces, old, grad, doc, cosine, sine):
    count = len(pieces)
    wide, half = jax.ShapeDtypeStruct((TOK, COLS), BF16), jax.ShapeDtypeStruct((TOK, HD), F32)
    return pl.pallas_call(
        lambda *refs: attend_low_body(count, *refs),
        out_shape=(wide, wide, half, half),
        in_specs=[SM] + [VM] * 7 + [ANY] * count,
        out_specs=(VM,) * 4,
        scratch_shapes=[
            pltpu.VMEM((count * HALF, QKV), BF16),
            pltpu.SemaphoreType.DMA((count,)),
            pltpu.VMEM((TOK, QKV), F32),
        ],
        compiler_params=pltpu.CompilerParams(vmem_limit_bytes=16 << 20),
        cost_estimate=attend_cost(LOW),
        name="attend_low",
    )(at, normed, old, grad, doc, doc.reshape(TOK, 1), cosine, sine, *pieces)


def attend_high(rest, d_key, d_val, grad, doc, cosine, sine):
    return pl.pallas_call(
        attend_high_body,
        out_shape=jax.ShapeDtypeStruct((TOK, COLS), BF16),
        in_specs=[VM] * 8,
        out_specs=VM,
        compiler_params=pltpu.CompilerParams(vmem_limit_bytes=12 << 20),
        cost_estimate=attend_cost(QH - LOW),
        name="attend_high",
    )(rest, d_key, d_val, grad, doc, doc.reshape(TOK, 1), cosine, sine)


SLOTS = 4


def tokens_body(count, at, d_low, d_high, tokens, scale_r, *refs):
    pieces = halves(refs[:count])
    out, slots, sems, held, d_qkv = refs[count:]
    count = len(pieces)

    def copy(i):
        return pltpu.make_async_copy(pieces[i], slots.at[i % SLOTS], sems.at[i % SLOTS])

    for i in range(SLOTS):
        copy(i).start()
    d_qkv[:, :COLS] = d_low[...]
    d_qkv[:, COLS:] = d_high[...]
    total = jnp.zeros((TOK, 128), F32)
    for i in range(count):
        cols = pl.ds(pl.multiple_of(at[i], HALF), HALF)
        copy(i).wait()
        part = dot(d_qkv[...], slots[i % SLOTS], ((1,), (1,)))
        if i + SLOTS < count:
            copy(i + SLOTS).start()
        held[:, cols] = part
        part = part * tokens[:, cols].astype(F32)
        for k in range(0, HALF, 128):
            total = total + part[:, k : k + 128]
    r = scale_r[...]
    back = r * r * r * (jnp.sum(total, axis=1, keepdims=True) * (1.0 / D))
    for k in range(0, D, 512):
        cols = slice(k, k + 512)
        out[:, cols] = (r * held[:, cols] - tokens[:, cols].astype(F32) * back).astype(BF16)


def tokens_grad(at, d_low, d_high, tokens, scale_r, pieces):
    count = len(pieces)
    return pl.pallas_call(
        lambda *refs: tokens_body(count, *refs),
        out_shape=jax.ShapeDtypeStruct((TOK, D), BF16),
        in_specs=[SM] + [VM] * 4 + [ANY] * count,
        out_specs=VM,
        scratch_shapes=[
            pltpu.VMEM((SLOTS, HALF, QKV), BF16),
            pltpu.SemaphoreType.DMA((SLOTS,)),
            pltpu.VMEM((TOK, D), F32),
            pltpu.VMEM((TOK, QKV), BF16),
        ],
        compiler_params=pltpu.CompilerParams(vmem_limit_bytes=20 << 20),
        cost_estimate=pl.CostEstimate(flops=2 * TOK * D * QKV, bytes_accessed=16 << 20, transcendentals=0),
        name="tokens_grad",
    )(at, d_low, d_high, tokens, scale_r, *pieces)


def term_product(count, at, feats, feats_other, d_own, d_other, left, sems):
    copies = []
    for i in range(count):
        rows = pl.ds(pl.multiple_of(at[i], QUART), QUART)
        into = pl.ds(i * QUART, QUART)
        for k, ref in enumerate((feats, feats_other)):
            cols = pl.ds(k * TOK, TOK)
            copies.append(pltpu.make_async_copy(ref.at[rows, :], left.at[into, cols], sems.at[2 * i + k]))
            copies[-1].start()
    right = jnp.concatenate([d_own[...], d_other[...]], axis=0)
    for copy in copies:
        copy.wait()
    return dot(left[...], right, ((1,), (0,)))


def term_body(count, at, feats, feats_other, d_own, d_other, out, left, sems):
    part = term_product(count, at, feats, feats_other, d_own, d_other, left, sems)
    out[...] = part.astype(BF16).reshape(count, QUART, COLS)


def term_add_body(count, at, feats, feats_other, d_own, d_other, came, kept, sent, left, sems):
    part = term_product(count, at, feats, feats_other, d_own, d_other, left, sems)
    part = (part.reshape(count, QUART, COLS) + came[...].astype(F32)).astype(BF16)
    kept[...] = part[: count // 2]
    sent[...] = part[count // 2 :]


def terms(at, made, *came):
    count = at.shape[0]
    if came:
        half = jax.ShapeDtypeStruct((count // 2, QUART, COLS), BF16)
        body, out_shape, out_specs = term_add_body, (half, half), (VM, VM)
    else:
        out_shape, out_specs = jax.ShapeDtypeStruct((count, QUART, COLS), BF16), VM
        body = term_body
    return pl.pallas_call(
        lambda *refs: body(count, *refs),
        out_shape=out_shape,
        in_specs=[SM, ANY, ANY, VM, VM] + [VM] * len(came),
        out_specs=out_specs,
        scratch_shapes=[pltpu.VMEM((count * QUART, 2 * TOK), BF16), pltpu.SemaphoreType.DMA((2 * count,))],
        compiler_params=pltpu.CompilerParams(vmem_limit_bytes=12 << 20),
        cost_estimate=pl.CostEstimate(
            flops=2 * count * QUART * COLS * 2 * TOK, bytes_accessed=4 << 20, transcendentals=0
        ),
        name="terms",
    )(at, *made, *came)


def split_body(count, old, came, kept, sent):
    part = (old[...].astype(F32) + came[...].astype(F32)).astype(BF16)
    kept[...] = part[: count // 2]
    sent[...] = part[count // 2 :]


def split(old, came):
    count = old.shape[0]
    half = jax.ShapeDtypeStruct((count // 2, QUART, COLS), BF16)
    return pl.pallas_call(
        lambda *refs: split_body(count, *refs),
        out_shape=(half, half),
        in_specs=[VM, VM],
        out_specs=(VM, VM),
        compiler_params=pltpu.CompilerParams(vmem_limit_bytes=6 << 20),
        name="split",
    )(old, came)


def join_body(old_x, came_x, old_y, came_y, out):
    out[:, :, :COLS] = (old_x[...].astype(F32) + came_x[...].astype(F32)).astype(BF16).reshape(8, PIECE, COLS)
    out[:, :, COLS:] = (old_y[...].astype(F32) + came_y[...].astype(F32)).astype(BF16).reshape(8, PIECE, COLS)


def join(*parts):
    return pl.pallas_call(
        join_body,
        out_shape=jax.ShapeDtypeStruct((8, PIECE, QKV), BF16),
        in_specs=[VM] * 4,
        out_specs=VM,
        compiler_params=pltpu.CompilerParams(vmem_limit_bytes=4 << 20),
        name="join",
    )(*parts)


def finish_body(parts, out):
    total = sum(parts[i].astype(F32) for i in range(8)).astype(BF16)
    for i in range(16):
        out[i] = total


def finish(parts):
    return pl.pallas_call(
        finish_body,
        out_shape=jax.ShapeDtypeStruct((16, PIECE, QKV), BF16),
        in_specs=[VM],
        out_specs=VM,
        compiler_params=pltpu.CompilerParams(vmem_limit_bytes=4 << 20),
        name="finish",
    )(parts)


def squares_body(got, out):
    total = jnp.zeros((PIECE, QKV), F32)
    for i in range(16):
        value = got[i].astype(F32)
        total = total + value * value
    total = jnp.sum(jnp.sum(total, axis=1, keepdims=True), axis=0, keepdims=True)
    out[...] = jnp.broadcast_to(total.reshape(1, 1, 1), (16, 8, 128))


def squares(got):
    return pl.pallas_call(
        squares_body,
        out_shape=jax.ShapeDtypeStruct((16, 8, 128), F32),
        in_specs=[VM],
        out_specs=VM,
        compiler_params=pltpu.CompilerParams(vmem_limit_bytes=4 << 20),
        name="squares",
    )(got)


def rescale_body(at, parts, mine, theirs, out):
    total = sum(parts[i] for i in range(16))
    factor = (target_rms * lax.rsqrt(total * (1.0 / (D * QKV)) + 1e-06))[:1, :1]
    for i, half in enumerate((mine, theirs)):
        rows = pl.ds(pl.multiple_of(at[i], HALF), HALF)
        out[rows, :] = (half[...].reshape(HALF, QKV).astype(F32) * factor).astype(BF16)


def rescale(at, parts, mine, theirs):
    return pl.pallas_call(
        rescale_body,
        out_shape=jax.ShapeDtypeStruct((BLK, QKV), BF16),
        in_specs=[SM, VM, VM, VM],
        out_specs=VM,
        compiler_params=pltpu.CompilerParams(vmem_limit_bytes=8 << 20),
        name="rescale",
    )(at, parts, mine, theirs)


def tables():
    position = jnp.arange(TOK, dtype=F32)
    freq = jnp.exp(-jnp.log(rope_base) * 2.0 * jnp.arange(HD // 2, dtype=F32) / HD)
    angle = position[:, None] * freq[None, :]
    cos, sin = jnp.cos(angle), jnp.sin(angle)
    return jnp.concatenate([cos, cos], axis=1), jnp.concatenate([-sin, sin], axis=1)


def on_device(tokens, grad_attended, doc_ids, w_own):
    x, y, z, c = place()

    w00 = lax.dynamic_slice_in_dim(w_own, c * HALF, HALF, 0)
    wa0 = swap(w00, gather_x1)
    w01 = swap(w00, flip_y)
    normed, scale_r, feats, theirs = norm(c, tokens)
    cosine, sine = tables()
    wa0, normed, theirs, cosine, sine = lax.optimization_barrier((wa0, normed, theirs, cosine, sine))
    wo0 = swap(wa0, gather_x2)
    wa1 = swap(wa0, flip_y)
    wb0 = swap(wa0, pair_z)
    vb0 = swap(wa0, other_core)
    v01 = swap(w01, other_core)

    turn = c ^ (z & 1)
    p1 = 1 + 2 * turn
    p2 = 4 - p1
    step = {"0": 0, "a": p1, "b": p2, "o": 2}

    def column(name, flip, half):
        return ((x ^ step[name]) * 2 + ((y & 1) ^ flip)) * BLK + half * HALF

    def spots(group):
        return jnp.stack([spot for _, *spots in group for spot in spots]).astype(jnp.int32)

    def pieces(group):
        return [piece for piece, *_ in group]

    early = [
        (w_own, column("0", 0, 0), column("0", 0, 1)),
        (w01, column("0", 1, c)),
        (wa0, column("a", 0, c)),
        (vb0, column("b", 0, 1 - c)),
        (v01, column("0", 1, 1 - c)),
    ]
    wo1 = swap(wo0, flip_y)
    wb1 = swap(wa1, pair_z)
    vo0 = swap(wo0, other_core)
    va0 = swap(wb0, other_core)
    vb1 = swap(wa1, other_core)
    feats_other = swap(theirs, other_core)
    middle = [
        (wo0, column("o", 0, c)),
        (wa1, column("a", 1, c)),
        (wb0, column("b", 0, c)),
        (vo0, column("o", 0, 1 - c)),
        (vb1, column("b", 1, 1 - c)),
        (va0, column("a", 0, 1 - c)),
    ]
    part = part_qkv(spots(early + middle), normed, pieces(early + middle))
    wo1, wb1, part = lax.optimization_barrier((wo1, wb1, part))
    vo1 = swap(wo1, other_core)
    va1 = swap(wb1, other_core)
    late = [
        (wo1, column("o", 1, c)),
        (wb1, column("b", 1, c)),
        (vo1, column("o", 1, 1 - c)),
        (va1, column("a", 1, 1 - c)),
    ]
    d_low, rest, d_key, d_val = attend_low(
        spots(late), normed, pieces(late), part, grad_attended, doc_ids, cosine, sine
    )

    low_other = swap(d_low, other_core)
    d_high = attend_high(rest, d_key, d_val, grad_attended, doc_ids, cosine, sine)
    low_other, d_high = lax.optimization_barrier((low_other, d_high))
    high_other = swap(d_high, other_core)
    q1 = 1 + 2 * c
    order = [0, 4 - q1, q1, 2]

    def row(xm, ym):
        yy = y ^ ym
        return ((x ^ xm) * 2 + (yy & 1)) * HALF + (yy >> 1) * QUART

    def along_x(first, second):
        return jnp.stack([row(order[i], order[j]) for i in (first, second) for j in range(4)]).astype(jnp.int32)

    def along_y(first, second):
        return jnp.stack([row(order[i], order[j]) for j in (first, second) for i in range(4)]).astype(jnp.int32)

    lows, highs = (feats, feats_other, d_low, low_other), (feats, feats_other, d_high, high_other)
    came_x = swap(terms(along_x(2, 3), lows), x_1)
    came_y = swap(terms(along_y(2, 3), highs), y_1)
    every = early + middle + late
    d_tokens = tokens_grad(spots(every), d_low, d_high, tokens, scale_r, pieces(every))
    came_x, came_y, d_tokens = lax.optimization_barrier((came_x, came_y, d_tokens))
    sum_x, sent_x = terms(along_x(0, 1), lows, came_x)
    came_x = swap(sent_x, x_2)
    sum_y, sent_y = terms(along_y(0, 1), highs, came_y)
    came_y = swap(sent_y, y_2)
    for step_x, step_y in ((y_1, x_1), (y_2, x_2)):
        sum_x, sent_x = split(sum_x, came_x)
        came_x = swap(sent_x, step_x)
        sum_y, sent_y = split(sum_y, came_y)
        came_y = swap(sent_y, step_y)

    total = join(sum_x, came_x, sum_y, came_y)
    got = finish(lax.all_to_all(total, "z", 0, 0))
    got = lax.all_to_all(got, ("y_hi", "z"), 0, 0)

    theirs = swap(got, other_core)
    parts = lax.all_to_all(squares(got), ("x", "y_lo", "core"), 0, 0)
    at = jnp.stack([c * HALF, (1 - c) * HALF]).astype(jnp.int32)
    return d_tokens, rescale(at, parts, got, theirs)


def solution(mesh):
    mesh = Mesh(mesh.devices.reshape(SIZES), AXES)
    spread, rows = P(AXES, None), P(AXES[:2], None)
    return jax.shard_map(
        on_device,
        mesh=mesh,
        in_specs=(spread, spread, spread, rows),
        out_specs=(spread, rows),
        check_vma=False,
    )
```

profile of v0, /device:TPU:1, one launch (start us, length us, event | category | flops | bytes accessed | tf_op | source)
XLA Modules:
  0.0 181.2 jit_solution(16306830317020042823)
XLA Ops:
  1.8 3.4 %collective-permute-start = (bf16[256,1280]{1,0:T(8,128)(2,1)S(1)}, bf16[256,1280]{1,0:T(8,128)(2,1)S(1)}, u32[]{:S(2)}, u32[]{:S(2)}) collective-permute-start(bf16[256,1280]{1,0:T(8,128)(2,1)S(1)} %constant_dynamic-slice_fusion), channel_id=1, source_target_pairs={{0,64},{1,193},{2,194},{3,67},{4,68},{5,197},{6,198},{7,71},{8,72}... | collective-permute-start | bytes 1966088 | tf_op jit(solution)/shard_map/ppermute | solution.py:46
  5.2 2.7 %collective-permute-start.6 = (bf16[256,1280]{1,0:T(8,128)(2,1)S(1)}, bf16[256,1280]{1,0:T(8,128)(2,1)S(1)}, u32[]{:S(2)}, u32[]{:S(2)}) collective-permute-start(bf16[256,1280]{1,0:T(8,128)(2,1)S(1)} %constant_dynamic-slice_fusion), channel_id=1, source_target_pairs={{0,32},{1,49},{2,34},{3,51},{4,36},{5,53},{6,38},{7,55},{8,40},{9,... | collective-permute-start | bytes 1966088 | tf_op jit(solution)/shard_map/ppermute | solution.py:46
  7.9 1.6 copy-done
  9.5 2.4 %norm.1 = (bf16[256,4096]{1,0:T(8,128)(2,1)S(1)}, f32[256,1]{1,0:T(8,128)S(1)}, bf16[2048,256]{1,0:T(8,128)(2,1)S(1)}, bf16[2048,256]{1,0:T(8,128)(2,1)}) custom-call(s32[1]{0:T(128)} %bitcast.8.c, bf16[256,4096]{1,0:T(8,128)(2,1)S(1)} %copy-done), custom_call_target="tpu_custom_call" | custom-call | flops 10485760 | bytes 6291456 | tf_op jit(solution)/shard_map/norm/pallas_call | solution.py:111
  13.3 4.7 %collective-permute-start.9 = (bf16[256,1280]{1,0:T(8,128)(2,1)S(1)}, bf16[256,1280]{1,0:T(8,128)(2,1)}, u32[]{:S(2)}, u32[]{:S(2)}) collective-permute-start(bf16[256,1280]{1,0:T(8,128)(2,1)S(1)} %collective-permute-done.refs_4_.refs_7_), channel_id=1, source_target_pairs={{0,2},{1,15},{2,0},{3,5},{4,6},{5,3},{6,4},{7,9},{8,10},{9,7},{10,... | collective-permute-start | bytes 1966088 | tf_op jit(solution)/shard_map/ppermute | solution.py:46
  18.0 2.7 %collective-permute-start.4 = (bf16[256,1280]{1,0:T(8,128)(2,1)S(1)}, bf16[256,1280]{1,0:T(8,128)(2,1)}, u32[]{:S(2)}, u32[]{:S(2)}) collective-permute-start(bf16[256,1280]{1,0:T(8,128)(2,1)S(1)} %collective-permute-done.refs_4_.refs_7_), channel_id=1, source_target_pairs={{0,32},{1,49},{2,34},{3,51},{4,36},{5,53},{6,38},{7,55},{8,40},{9,... | collective-permute-start | bytes 1966088 | tf_op jit(solution)/shard_map/ppermute | solution.py:46
  24.2 2.2 %collective-permute-done.9.refs_9_.refs_12_ = bf16[256,1280]{1,0:T(8,128)(2,1)} collective-permute-done((bf16[256,1280]{1,0:T(8,128)(2,1)S(1)}, bf16[256,1280]{1,0:T(8,128)(2,1)}, u32[]{:S(2)}, u32[]{:S(2)}) %collective-permute-start.9) | collective-permute-done | bytes 655392 | tf_op jit(solution)/shard_map/ppermute | solution.py:46
  26.4 2.7 %collective-permute-done.4.refs_8_.refs_11_ = bf16[256,1280]{1,0:T(8,128)(2,1)} collective-permute-done((bf16[256,1280]{1,0:T(8,128)(2,1)S(1)}, bf16[256,1280]{1,0:T(8,128)(2,1)}, u32[]{:S(2)}, u32[]{:S(2)}) %collective-permute-start.4) | collective-permute-done | bytes 655392 | tf_op jit(solution)/shard_map/ppermute | solution.py:46
  31.4 2.5 %collective-permute-start.5 = (bf16[256,1280]{1,0:T(8,128)(2,1)}, bf16[256,1280]{1,0:T(8,128)(2,1)}, u32[]{:S(2)}, u32[]{:S(2)}) collective-permute-start(bf16[256,1280]{1,0:T(8,128)(2,1)} %collective-permute-done.4.refs_8_.refs_11_), channel_id=1, source_target_pairs={{0,2},{1,15},{2,0},{3,5},{4,6},{5,3},{6,4},{7,9},{8,10},{9,7},{10,... | collective-permute-start | bytes 1966088 | tf_op jit(solution)/shard_map/ppermute | solution.py:46
  34.7 1.9 %collective-permute-start.3 = (bf16[256,1280]{1,0:T(8,128)(2,1)}, bf16[256,1280]{1,0:T(8,128)(2,1)}, u32[]{:S(2)}, u32[]{:S(2)}) collective-permute-start(bf16[256,1280]{1,0:T(8,128)(2,1)} %collective-permute-done.2.refs_7_.refs_10_), channel_id=1, source_target_pairs={{0,32},{1,49},{2,34},{3,51},{4,36},{5,53},{6,38},{7,55},{8,40},{9,... | collective-permute-start | bytes 1966088 | tf_op jit(solution)/shard_map/ppermute | solution.py:46
  42.4 5.7 %qkv_part.1.refs_2_ = f32[256,1280]{1,0:T(8,128)S(1)} custom-call(s32[12]{0:T(128)S(1)} %stack.184.refs_0_, bf16[256,4096]{1,0:T(8,128)(2,1)S(1)} %get-tuple-element.39.refs_1_, bf16[512,1280]{1,0:T(8,128)(2,1)S(1)} %copy-done.4, bf16[256,1280]{1,0:T(8,128)(2,1)S(1)} %copy-done.14, bf16[256,1280]{1,0:T(8,128)(2,1)S(1)} %copy-done.11, ...), custom_call_target="tpu_custom_call" | custom-call | flops 2013265920 | bytes 7864320 | tf_op jit(solution)/shard_map/qkv_part/pallas_call | solution.py:158
  51.5 2.0 %collective-permute-done.14.refs_11_.refs_19_ = bf16[256,1280]{1,0:T(8,128)(2,1)} collective-permute-done((bf16[256,1280]{1,0:T(8,128)(2,1)}, bf16[256,1280]{1,0:T(8,128)(2,1)}, u32[]{:S(2)}, u32[]{:S(2)}) %collective-permute-start.14) | collective-permute-done | bytes 655392 | tf_op jit(solution)/shard_map/ppermute | solution.py:46
  53.5 1.6 copy-done.3
  57.5 6.1 %attend_low.1 = (bf16[256,640]{1,0:T(8,128)(2,1)S(1)}, bf16[256,640]{1,0:T(8,128)(2,1)S(1)}, f32[256,128]{1,0:T(8,128)S(1)}, f32[256,128]{1,0:T(8,128)S(1)}) custom-call(s32[4]{0:T(128)S(1)} %pad_add_fusion.refs_0_, bf16[256,4096]{1,0:T(8,128)(2,1)S(1)} %copy-done.3, f32[256,1280]{1,0:T(8,128)S(1)} %copy-done.7, bf16[256,1024]{1,0:T(8,128)(2,1)S(1)} %copy-done.24, ...), custom_call_target="tpu_custom_call" | custom-call | flops 419430400 | bytes 4194304 | tf_op jit(solution)/shard_map/attend_low/pallas_call | solution.py:242
  63.8 2.6 %attend_high.1.refs_3_.refs_2_ = bf16[256,640]{1,0:T(8,128)(2,1)} custom-call(bf16[256,640]{1,0:T(8,128)(2,1)S(1)} %get-tuple-element.47.rest, f32[256,128]{1,0:T(8,128)S(1)} %get-tuple-element.48.key_low, f32[256,128]{1,0:T(8,128)S(1)} %get-tuple-element.49.val_low, bf16[256,1024]{1,0:T(8,128)(2,1)S(1)} %copy-done.24, s32[1,256]{1,0:T(1,128)S(1)} %copy-done.29, ...), custom_call_target="tpu_custom_call" | custom-call | flops 251658240 | bytes 4194304 | tf_op jit(solution)/shard_map/attend_high/pallas_call | solution.py:259
  67.0 2.9 %terms.4 = bf16[8,128,640]{2,1,0:T(8,128)(2,1)} custom-call(s32[8]{0:T(128)S(1)} %stack.166.refs_0_, bf16[2048,256]{1,0:T(8,128)(2,1)S(1)} %get-tuple-element.35.refs_1_, bf16[2048,256]{1,0:T(8,128)(2,1)S(1)} %collective-permute-done.1.refs_2_, bf16[256,640]{1,0:T(8,128)(2,1)S(1)} %get-tuple-element.46.refs_3_.refs_1_, ...), custom_call_target="tpu_custom_call" | custom-call | flops 671088640 | bytes 4194304 | tf_op jit(solution)/shard_map/terms/pallas_call | solution.py:357
  70.7 2.5 %collective-permute-start.16 = (bf16[8,128,640]{2,1,0:T(8,128)(2,1)}, bf16[8,128,640]{2,1,0:T(8,128)(2,1)}, u32[]{:S(2)}, u32[]{:S(2)}) collective-permute-start(bf16[8,128,640]{2,1,0:T(8,128)(2,1)} %terms.4), channel_id=1, source_target_pairs={{0,64},{1,193},{2,66},{3,195},{4,68},{5,197},{6,70},{7,199},{8,72}... | collective-permute-start | bytes 3932168 | tf_op jit(solution)/shard_map/ppermute | solution.py:46
  73.1 3.5 %terms.5 = bf16[8,128,640]{2,1,0:T(8,128)(2,1)} custom-call(s32[8]{0:T(128)S(1)} %stack.189.refs_0_, bf16[2048,256]{1,0:T(8,128)(2,1)S(1)} %get-tuple-element.35.refs_1_, bf16[2048,256]{1,0:T(8,128)(2,1)S(1)} %collective-permute-done.1.refs_2_, bf16[256,640]{1,0:T(8,128)(2,1)} %attend_high.1.refs_3_.refs_2_, bf16[256,640]{1,0:T(8,128)(2,1)} %collective-permute-done.17.refs_4_), custom_call_target="tpu_custom_call" | custom-call | flops 671088640 | bytes 4194304 | tf_op jit(solution)/shard_map/terms/pallas_call | solution.py:357
  86.0 13.1 %tokens_grad.1 = bf16[256,4096]{1,0:T(8,128)(2,1)} custom-call(s32[16]{0:T(128)S(1)} %stack.190.refs_0_, bf16[256,640]{1,0:T(8,128)(2,1)S(1)} %copy-done.9, bf16[256,640]{1,0:T(8,128)(2,1)} %attend_high.1.refs_3_.refs_2_, bf16[256,4096]{1,0:T(8,128)(2,1)S(1)} %copy-done.1, f32[256,1]{1,0:T(8,128)S(1)} %copy-done.28, bf16[512,1280]{1,0:T(8,128)(2,1)S(1)} %copy-done.5, ...), custom_call_target="tpu_custom_call" | custom-call | flops 2684354560 | bytes 16777216 | tf_op jit(solution)/shard_map/tokens_grad/pallas_call | solution.py:305
  99.2 2.7 %terms.6 = (bf16[4,128,640]{2,1,0:T(8,128)(2,1)S(1)}, bf16[4,128,640]{2,1,0:T(8,128)(2,1)S(1)}) custom-call(s32[8]{0:T(128)S(1)} %stack.198.refs_0_, bf16[2048,256]{1,0:T(8,128)(2,1)S(1)} %get-tuple-element.35.refs_1_, bf16[2048,256]{1,0:T(8,128)(2,1)S(1)} %collective-permute-done.1.refs_2_, bf16[256,640]{1,0:T(8,128)(2,1)S(1)} %copy-done.9, ...), custom_call_target="tpu_custom_call" | custom-call | flops 671088640 | bytes 4194304 | tf_op jit(solution)/shard_map/terms/pallas_call | solution.py:357
  101.9 2.9 %terms.7 = (bf16[4,128,640]{2,1,0:T(8,128)(2,1)S(1)}, bf16[4,128,640]{2,1,0:T(8,128)(2,1)S(1)}) custom-call(s32[8]{0:T(128)S(1)} %stack.199.refs_0_, bf16[2048,256]{1,0:T(8,128)(2,1)S(1)} %get-tuple-element.35.refs_1_, bf16[2048,256]{1,0:T(8,128)(2,1)S(1)} %collective-permute-done.1.refs_2_, bf16[256,640]{1,0:T(8,128)(2,1)} %attend_high.1.refs_3_.refs_2_, ...), custom_call_target="tpu_custom_call" | custom-call | flops 671088640 | bytes 4194304 | tf_op jit(solution)/shard_map/terms/pallas_call | solution.py:357
  104.9 6.7 %collective-permute-done.19.refs_1_ = bf16[4,128,640]{2,1,0:T(8,128)(2,1)S(1)} collective-permute-done((bf16[4,128,640]{2,1,0:T(8,128)(2,1)S(1)}, bf16[4,128,640]{2,1,0:T(8,128)(2,1)S(1)}, u32[]{:S(2)}, u32[]{:S(2)}) %collective-permute-start.19) | collective-permute-done | bytes 655392 | tf_op jit(solution)/shard_map/ppermute | solution.py:46
  111.8 2.0 %collective-permute-start.20 = (bf16[2,128,640]{2,1,0:T(8,128)(2,1)S(1)}, bf16[2,128,640]{2,1,0:T(8,128)(2,1)S(1)}, u32[]{:S(2)}, u32[]{:S(2)}) collective-permute-start(bf16[2,128,640]{2,1,0:T(8,128)(2,1)S(1)} %get-tuple-element.58), channel_id=1, source_target_pairs={{0,32},{1,49},{2,34},{3,51},{4,36},{5,53},{6,38},{7,55},{8,40},{9,... | collective-permute-start | bytes 983048 | tf_op jit(solution)/shard_map/ppermute | solution.py:46
  115.6 4.8 %collective-permute-done.20.refs_1_ = bf16[2,128,640]{2,1,0:T(8,128)(2,1)S(1)} collective-permute-done((bf16[2,128,640]{2,1,0:T(8,128)(2,1)S(1)}, bf16[2,128,640]{2,1,0:T(8,128)(2,1)S(1)}, u32[]{:S(2)}, u32[]{:S(2)}) %collective-permute-start.20) | collective-permute-done | bytes 327712 | tf_op jit(solution)/shard_map/ppermute | solution.py:46
  123.0 2.0 %collective-permute-done.21.came_x = bf16[1,128,640]{2,1,0:T(8,128)(2,1)S(1)} collective-permute-done((bf16[1,128,640]{2,1,0:T(8,128)(2,1)S(1)}, bf16[1,128,640]{2,1,0:T(8,128)(2,1)S(1)}, u32[]{:S(2)}, u32[]{:S(2)}) %collective-permute-start.21) | collective-permute-done | bytes 163872 | tf_op jit(solution)/shard_map/ppermute | solution.py:46
  125.1 2.3 %collective-permute-done.24.came_y = bf16[1,128,640]{2,1,0:T(8,128)(2,1)S(1)} collective-permute-done((bf16[1,128,640]{2,1,0:T(8,128)(2,1)S(1)}, bf16[1,128,640]{2,1,0:T(8,128)(2,1)S(1)}, u32[]{:S(2)}, u32[]{:S(2)}) %collective-permute-start.24) | collective-permute-done | bytes 163872 | tf_op jit(solution)/shard_map/ppermute | solution.py:46
  127.4 14.5 %all_to_all.15.parts = bf16[8,16,1280]{2,1,0:T(8,128)(2,1)S(1)} all-to-all(bf16[8,16,1280]{2,1,0:T(8,128)(2,1)S(1)} %join.1), channel_id=1, replica_groups=mesh['x'=4,'y_lo'=2,'y_hi'=2,'z'=8,'core'=2] {'z'}, dimensions={0} | all-to-all | bytes 655360 | tf_op jit(solution)/shard_map/all_to_all | solution.py:568
  142.0 17.1 %all_to_all.16.got.mine = bf16[16,16,1280]{2,1,0:T(8,128)(2,1)S(1)} all-to-all(bf16[16,16,1280]{2,1,0:T(8,128)(2,1)S(1)} %finish.1), channel_id=1, replica_groups=mesh['x'=4,'y_lo'=2,'y_hi'=2,'z'=8,'core'=2] {'y_hi','z'}, dimensions={0} | all-to-all | bytes 1310720 | tf_op jit(solution)/shard_map/all_to_all | solution.py:569
  159.1 10.1 %collective-permute-start.25 = (bf16[16,16,1280]{2,1,0:T(8,128)(2,1)S(1)}, bf16[16,16,1280]{2,1,0:T(8,128)(2,1)S(1)}, u32[]{:S(2)}, u32[]{:S(2)}) collective-permute-start(bf16[16,16,1280]{2,1,0:T(8,128)(2,1)S(1)} %all_to_all.16.got.mine), channel_id=1, source_target_pairs={{0,1},{1,0},{2,3},{3,2},{4,5},{5,4},{6,7},{7,6},{8,9},{9,8},{10,11... | collective-permute-start | bytes 1966088 | tf_op jit(solution)/shard_map/ppermute | solution.py:46
  169.9 3.4 %all-to-all-start.2 = ((f32[16,8,128]{2,1,0:T(8,128)}), f32[16,8,128]{2,1,0:T(8,128)S(1)}, u32[]{:S(2)}, u32[]{:S(2)}) async-start(f32[16,8,128]{2,1,0:T(8,128)} %squares.1), calls=%async_computation.2 | async-start | bytes 131072 | tf_op jit(solution)/shard_map/all_to_all | solution.py:572
  173.4 5.7 %all-to-all-done.2.parts = f32[16,8,128]{2,1,0:T(8,128)S(1)} async-done(((f32[16,8,128]{2,1,0:T(8,128)}), f32[16,8,128]{2,1,0:T(8,128)S(1)}, u32[]{:S(2)}, u32[]{:S(2)}) %all-to-all-start.2) | async-done | bytes 65568 | tf_op jit(solution)/shard_map/all_to_all | solution.py:572
  179.2 2.0 %rescale.1 = bf16[512,1280]{1,0:T(8,128)(2,1)} custom-call(s32[2]{0:T(128)S(1)} %pad_add_fusion.1.at, f32[16,8,128]{2,1,0:T(8,128)S(1)} %all-to-all-done.2.parts, bf16[16,16,1280]{2,1,0:T(8,128)(2,1)S(1)} %all_to_all.16.got.mine, bf16[16,16,1280]{2,1,0:T(8,128)(2,1)S(1)} %collective-permute-done.25.theirs), custom_call_target="tpu_custom_call" | custom-call | tf_op jit(solution)/shard_map/rescale/pallas_call | solution.py:452
  (114 shorter events, 37.1 us)
Async XLA Ops:
  1.8 11.5 %collective-permute-start = (bf16[256,1280]{1,0:T(8,128)(2,1)S(1)}, bf16[256,1280]{1,0:T(8,128)(2,1)S(1)}, u32[]{:S(2)}, u32[]{:S(2)}) collective-permute-start(bf16[256,1280]{1,0:T(8,128)(2,1)S(1)} %constant_dynamic-slice_fusion), channel_id=1, source_target_pairs={{0,64},{1,193},{2,194},{3,67},{4,68},{5,197},{6,198},{7,71},{8,72}... | collective-permute-start | bytes 1966088 | tf_op jit(solution)/shard_map/ppermute | solution.py:46
  5.2 16.8 %collective-permute-start.6 = (bf16[256,1280]{1,0:T(8,128)(2,1)S(1)}, bf16[256,1280]{1,0:T(8,128)(2,1)S(1)}, u32[]{:S(2)}, u32[]{:S(2)}) collective-permute-start(bf16[256,1280]{1,0:T(8,128)(2,1)S(1)} %constant_dynamic-slice_fusion), channel_id=1, source_target_pairs={{0,32},{1,49},{2,34},{3,51},{4,36},{5,53},{6,38},{7,55},{8,40},{9,... | collective-permute-start | bytes 1966088 | tf_op jit(solution)/shard_map/ppermute | solution.py:46
  12.6 35.5 %copy-start.2 = (bf16[256,4096]{1,0:T(8,128)(2,1)}, bf16[256,4096]{1,0:T(8,128)(2,1)S(1)}, u32[]{:S(2)}) copy-start(bf16[256,4096]{1,0:T(8,128)(2,1)S(1)} %get-tuple-element.39.refs_1_) | copy-start | bytes 6291460
  13.3 13.1 %collective-permute-start.9 = (bf16[256,1280]{1,0:T(8,128)(2,1)S(1)}, bf16[256,1280]{1,0:T(8,128)(2,1)}, u32[]{:S(2)}, u32[]{:S(2)}) collective-permute-start(bf16[256,1280]{1,0:T(8,128)(2,1)S(1)} %collective-permute-done.refs_4_.refs_7_), channel_id=1, source_target_pairs={{0,2},{1,15},{2,0},{3,5},{4,6},{5,3},{6,4},{7,9},{8,10},{9,7},{10,... | collective-permute-start | bytes 1966088 | tf_op jit(solution)/shard_map/ppermute | solution.py:46
  18.0 11.1 %collective-permute-start.4 = (bf16[256,1280]{1,0:T(8,128)(2,1)S(1)}, bf16[256,1280]{1,0:T(8,128)(2,1)}, u32[]{:S(2)}, u32[]{:S(2)}) collective-permute-start(bf16[256,1280]{1,0:T(8,128)(2,1)S(1)} %collective-permute-done.refs_4_.refs_7_), channel_id=1, source_target_pairs={{0,32},{1,49},{2,34},{3,51},{4,36},{5,53},{6,38},{7,55},{8,40},{9,... | collective-permute-start | bytes 1966088 | tf_op jit(solution)/shard_map/ppermute | solution.py:46
  20.7 9.5 %collective-permute-start.2 = (bf16[256,1280]{1,0:T(8,128)(2,1)S(1)}, bf16[256,1280]{1,0:T(8,128)(2,1)}, u32[]{:S(2)}, u32[]{:S(2)}) collective-permute-start(bf16[256,1280]{1,0:T(8,128)(2,1)S(1)} %collective-permute-done.refs_4_.refs_7_), channel_id=1, source_target_pairs={{0,192},{1,65},{2,66},{3,195},{4,196},{5,69},{6,70},{7,199},{8,200... | collective-permute-start | bytes 1966088 | tf_op jit(solution)/shard_map/ppermute | solution.py:46
  21.9 8.6 %collective-permute-start.8 = (bf16[256,1280]{1,0:T(8,128)(2,1)S(1)}, bf16[256,1280]{1,0:T(8,128)(2,1)S(1)}, u32[]{:S(2)}, u32[]{:S(2)}) collective-permute-start(bf16[256,1280]{1,0:T(8,128)(2,1)S(1)} %collective-permute-done.6.refs_3_.refs_6_), channel_id=1, source_target_pairs={{0,1},{1,0},{2,3},{3,2},{4,5},{5,4},{6,7},{7,6},{8,9},{9,8},{10,11... | collective-permute-start | bytes 1966088 | tf_op jit(solution)/shard_map/ppermute | solution.py:46
  22.8 11.0 %collective-permute-start.7 = (bf16[256,1280]{1,0:T(8,128)(2,1)S(1)}, bf16[256,1280]{1,0:T(8,128)(2,1)S(1)}, u32[]{:S(2)}, u32[]{:S(2)}) collective-permute-start(bf16[256,1280]{1,0:T(8,128)(2,1)S(1)} %collective-permute-done.refs_4_.refs_7_), channel_id=1, source_target_pairs={{0,1},{1,0},{2,3},{3,2},{4,5},{5,4},{6,7},{7,6},{8,9},{9,8},{10,11... | collective-permute-start | bytes 1966088 | tf_op jit(solution)/shard_map/ppermute | solution.py:46
  26.4 10.3 %collective-permute-start.12 = (bf16[256,1280]{1,0:T(8,128)(2,1)}, bf16[256,1280]{1,0:T(8,128)(2,1)}, u32[]{:S(2)}, u32[]{:S(2)}) collective-permute-start(bf16[256,1280]{1,0:T(8,128)(2,1)} %collective-permute-done.9.refs_9_.refs_12_), channel_id=1, source_target_pairs={{0,1},{1,0},{2,3},{3,2},{4,5},{5,4},{6,7},{7,6},{8,9},{9,8},{10,11... | collective-permute-start | bytes 1966088 | tf_op jit(solution)/shard_map/ppermute | solution.py:46
  29.1 7.6 %collective-permute-start.11 = (bf16[256,1280]{1,0:T(8,128)(2,1)}, bf16[256,1280]{1,0:T(8,128)(2,1)}, u32[]{:S(2)}, u32[]{:S(2)}) collective-permute-start(bf16[256,1280]{1,0:T(8,128)(2,1)} %collective-permute-done.4.refs_8_.refs_11_), channel_id=1, source_target_pairs={{0,1},{1,0},{2,3},{3,2},{4,5},{5,4},{6,7},{7,6},{8,9},{9,8},{10,11... | collective-permute-start | bytes 1966088 | tf_op jit(solution)/shard_map/ppermute | solution.py:46
  30.3 6.4 %collective-permute-start.10 = (bf16[256,1280]{1,0:T(8,128)(2,1)}, bf16[256,1280]{1,0:T(8,128)(2,1)}, u32[]{:S(2)}, u32[]{:S(2)}) collective-permute-start(bf16[256,1280]{1,0:T(8,128)(2,1)} %collective-permute-done.2.refs_7_.refs_10_), channel_id=1, source_target_pairs={{0,1},{1,0},{2,3},{3,2},{4,5},{5,4},{6,7},{7,6},{8,9},{9,8},{10,11... | collective-permute-start | bytes 1966088 | tf_op jit(solution)/shard_map/ppermute | solution.py:46
  31.4 17.8 %collective-permute-start.5 = (bf16[256,1280]{1,0:T(8,128)(2,1)}, bf16[256,1280]{1,0:T(8,128)(2,1)}, u32[]{:S(2)}, u32[]{:S(2)}) collective-permute-start(bf16[256,1280]{1,0:T(8,128)(2,1)} %collective-permute-done.4.refs_8_.refs_11_), channel_id=1, source_target_pairs={{0,2},{1,15},{2,0},{3,5},{4,6},{5,3},{6,4},{7,9},{8,10},{9,7},{10,... | collective-permute-start | bytes 1966088 | tf_op jit(solution)/shard_map/ppermute | solution.py:46
  34.7 14.5 %collective-permute-start.3 = (bf16[256,1280]{1,0:T(8,128)(2,1)}, bf16[256,1280]{1,0:T(8,128)(2,1)}, u32[]{:S(2)}, u32[]{:S(2)}) collective-permute-start(bf16[256,1280]{1,0:T(8,128)(2,1)} %collective-permute-done.2.refs_7_.refs_10_), channel_id=1, source_target_pairs={{0,32},{1,49},{2,34},{3,51},{4,36},{5,53},{6,38},{7,55},{8,40},{9,... | collective-permute-start | bytes 1966088 | tf_op jit(solution)/shard_map/ppermute | solution.py:46
  36.6 13.4 %copy-start.29 = (s32[1,256]{1,0:T(1,128)S(1)}, s32[1,256]{1,0:T(1,128)}, u32[]{:S(2)}) copy-start(s32[1,256]{1,0:T(1,128)} %doc_row.1) | copy-start | bytes 3076
  49.2 2.3 %collective-permute-start.13 = (bf16[256,1280]{1,0:T(8,128)(2,1)}, bf16[256,1280]{1,0:T(8,128)(2,1)S(1)}, u32[]{:S(2)}, u32[]{:S(2)}) collective-permute-start(bf16[256,1280]{1,0:T(8,128)(2,1)} %collective-permute-done.3.refs_8_.refs_16_), channel_id=1, source_target_pairs={{0,1},{1,0},{2,3},{3,2},{4,5},{5,4},{6,7},{7,6},{8,9},{9,8},{10,11... | collective-permute-start | bytes 1966088 | tf_op jit(solution)/shard_map/ppermute | solution.py:46
  49.2 4.3 %collective-permute-start.14 = (bf16[256,1280]{1,0:T(8,128)(2,1)}, bf16[256,1280]{1,0:T(8,128)(2,1)}, u32[]{:S(2)}, u32[]{:S(2)}) collective-permute-start(bf16[256,1280]{1,0:T(8,128)(2,1)} %collective-permute-done.5.refs_9_.refs_17_), channel_id=1, source_target_pairs={{0,1},{1,0},{2,3},{3,2},{4,5},{5,4},{6,7},{7,6},{8,9},{9,8},{10,11... | collective-permute-start | bytes 1966088 | tf_op jit(solution)/shard_map/ppermute | solution.py:46
  49.7 17.3 %collective-permute-start.1 = (bf16[2048,256]{1,0:T(8,128)(2,1)}, bf16[2048,256]{1,0:T(8,128)(2,1)S(1)}, u32[]{:S(2)}, u32[]{:S(2)}) collective-permute-start(bf16[2048,256]{1,0:T(8,128)(2,1)} %get-tuple-element.38), channel_id=1, source_target_pairs={{0,1},{1,0},{2,3},{3,2},{4,5},{5,4},{6,7},{7,6},{8,9},{9,8},{10,11... | collective-permute-start | bytes 3145736 | tf_op jit(solution)/shard_map/ppermute | solution.py:46
  51.5 12.1 %copy-start.22 = (bf16[256,1280]{1,0:T(8,128)(2,1)}, bf16[256,1280]{1,0:T(8,128)(2,1)S(1)}, u32[]{:S(2)}) copy-start(bf16[256,1280]{1,0:T(8,128)(2,1)S(1)} %collective-permute-done.13.refs_10_.refs_18_) | copy-start | bytes 1966084
  63.6 2.8 %collective-permute-start.15 = (bf16[256,640]{1,0:T(8,128)(2,1)S(1)}, bf16[256,640]{1,0:T(8,128)(2,1)S(1)}, u32[]{:S(2)}, u32[]{:S(2)}) collective-permute-start(bf16[256,640]{1,0:T(8,128)(2,1)S(1)} %get-tuple-element.46.refs_3_.refs_1_), channel_id=1, source_target_pairs={{0,1},{1,0},{2,3},{3,2},{4,5},{5,4},{6,7},{7,6},{8,9},{9,8},{10,11... | collective-permute-start | bytes 983048 | tf_op jit(solution)/shard_map/ppermute | solution.py:46
  66.4 6.7 %collective-permute-start.17 = (bf16[256,640]{1,0:T(8,128)(2,1)}, bf16[256,640]{1,0:T(8,128)(2,1)}, u32[]{:S(2)}, u32[]{:S(2)}) collective-permute-start(bf16[256,640]{1,0:T(8,128)(2,1)} %attend_high.1.refs_3_.refs_2_), channel_id=1, source_target_pairs={{0,1},{1,0},{2,3},{3,2},{4,5},{5,4},{6,7},{7,6},{8,9},{9,8},{10,11... | collective-permute-start | bytes 983048 | tf_op jit(solution)/shard_map/ppermute | solution.py:46
  70.7 7.3 %copy-start.28 = (f32[256,1]{1,0:T(8,128)S(1)}, f32[256,1]{1,0:T(8,128)}, u32[]{:S(2)}) copy-start(f32[256,1]{1,0:T(8,128)} %copy-done.27) | copy-start | bytes 3076
  70.7 28.5 %collective-permute-start.16 = (bf16[8,128,640]{2,1,0:T(8,128)(2,1)}, bf16[8,128,640]{2,1,0:T(8,128)(2,1)}, u32[]{:S(2)}, u32[]{:S(2)}) collective-permute-start(bf16[8,128,640]{2,1,0:T(8,128)(2,1)} %terms.4), channel_id=1, source_target_pairs={{0,64},{1,193},{2,66},{3,195},{4,68},{5,197},{6,70},{7,199},{8,72}... | collective-permute-start | bytes 3932168 | tf_op jit(solution)/shard_map/ppermute | solution.py:46
  76.6 22.5 %collective-permute-start.18 = (bf16[8,128,640]{2,1,0:T(8,128)(2,1)}, bf16[8,128,640]{2,1,0:T(8,128)(2,1)}, u32[]{:S(2)}, u32[]{:S(2)}) collective-permute-start(bf16[8,128,640]{2,1,0:T(8,128)(2,1)} %terms.5), channel_id=1, source_target_pairs={{0,32},{1,49},{2,34},{3,51},{4,36},{5,53},{6,38},{7,55},{8,40},{9,... | collective-permute-start | bytes 3932168 | tf_op jit(solution)/shard_map/ppermute | solution.py:46
  86.0 13.1 %copy-start.26 = (bf16[256,640]{1,0:T(8,128)(2,1)S(1)}, bf16[256,640]{1,0:T(8,128)(2,1)}, u32[]{:S(2)}) copy-start(bf16[256,640]{1,0:T(8,128)(2,1)} %copy-done.25) | copy-start | bytes 983044
  101.8 9.8 %collective-permute-start.19 = (bf16[4,128,640]{2,1,0:T(8,128)(2,1)S(1)}, bf16[4,128,640]{2,1,0:T(8,128)(2,1)S(1)}, u32[]{:S(2)}, u32[]{:S(2)}) collective-permute-start(bf16[4,128,640]{2,1,0:T(8,128)(2,1)S(1)} %get-tuple-element.56), channel_id=1, source_target_pairs={{0,192},{1,65},{2,194},{3,67},{4,196},{5,69},{6,198},{7,71},{8,200... | collective-permute-start | bytes 1966088 | tf_op jit(solution)/shard_map/ppermute | solution.py:46
  104.8 9.8 %collective-permute-start.22 = (bf16[4,128,640]{2,1,0:T(8,128)(2,1)S(1)}, bf16[4,128,640]{2,1,0:T(8,128)(2,1)S(1)}, u32[]{:S(2)}, u32[]{:S(2)}) collective-permute-start(bf16[4,128,640]{2,1,0:T(8,128)(2,1)S(1)} %get-tuple-element.63), channel_id=1, source_target_pairs={{0,48},{1,33},{2,50},{3,35},{4,52},{5,37},{6,54},{7,39},{8,56},{9,... | collective-permute-start | bytes 1966088 | tf_op jit(solution)/shard_map/ppermute | solution.py:46
  111.8 8.6 %collective-permute-start.20 = (bf16[2,128,640]{2,1,0:T(8,128)(2,1)S(1)}, bf16[2,128,640]{2,1,0:T(8,128)(2,1)S(1)}, u32[]{:S(2)}, u32[]{:S(2)}) collective-permute-start(bf16[2,128,640]{2,1,0:T(8,128)(2,1)S(1)} %get-tuple-element.58), channel_id=1, source_target_pairs={{0,32},{1,49},{2,34},{3,51},{4,36},{5,53},{6,38},{7,55},{8,40},{9,... | collective-permute-start | bytes 983048 | tf_op jit(solution)/shard_map/ppermute | solution.py:46
  114.8 7.2 %collective-permute-start.23 = (bf16[2,128,640]{2,1,0:T(8,128)(2,1)S(1)}, bf16[2,128,640]{2,1,0:T(8,128)(2,1)S(1)}, u32[]{:S(2)}, u32[]{:S(2)}) collective-permute-start(bf16[2,128,640]{2,1,0:T(8,128)(2,1)S(1)} %get-tuple-element.65), channel_id=1, source_target_pairs={{0,64},{1,193},{2,66},{3,195},{4,68},{5,197},{6,70},{7,199},{8,72}... | collective-permute-start | bytes 983048 | tf_op jit(solution)/shard_map/ppermute | solution.py:46
  120.5 4.6 %collective-permute-start.21 = (bf16[1,128,640]{2,1,0:T(8,128)(2,1)S(1)}, bf16[1,128,640]{2,1,0:T(8,128)(2,1)S(1)}, u32[]{:S(2)}, u32[]{:S(2)}) collective-permute-start(bf16[1,128,640]{2,1,0:T(8,128)(2,1)S(1)} %get-tuple-element.60), channel_id=1, source_target_pairs={{0,48},{1,33},{2,50},{3,35},{4,52},{5,37},{6,54},{7,39},{8,56},{9,... | collective-permute-start | bytes 491528 | tf_op jit(solution)/shard_map/ppermute | solution.py:46
  122.1 5.2 %collective-permute-start.24 = (bf16[1,128,640]{2,1,0:T(8,128)(2,1)S(1)}, bf16[1,128,640]{2,1,0:T(8,128)(2,1)S(1)}, u32[]{:S(2)}, u32[]{:S(2)}) collective-permute-start(bf16[1,128,640]{2,1,0:T(8,128)(2,1)S(1)} %get-tuple-element.67), channel_id=1, source_target_pairs={{0,192},{1,65},{2,194},{3,67},{4,196},{5,69},{6,198},{7,71},{8,200... | collective-permute-start | bytes 491528 | tf_op jit(solution)/shard_map/ppermute | solution.py:46
  159.1 20.1 %collective-permute-start.25 = (bf16[16,16,1280]{2,1,0:T(8,128)(2,1)S(1)}, bf16[16,16,1280]{2,1,0:T(8,128)(2,1)S(1)}, u32[]{:S(2)}, u32[]{:S(2)}) collective-permute-start(bf16[16,16,1280]{2,1,0:T(8,128)(2,1)S(1)} %all_to_all.16.got.mine), channel_id=1, source_target_pairs={{0,1},{1,0},{2,3},{3,2},{4,5},{5,4},{6,7},{7,6},{8,9},{9,8},{10,11... | collective-permute-start | bytes 1966088 | tf_op jit(solution)/shard_map/ppermute | solution.py:46
  169.9 9.2 %all-to-all-start.2 = ((f32[16,8,128]{2,1,0:T(8,128)}), f32[16,8,128]{2,1,0:T(8,128)S(1)}, u32[]{:S(2)}, u32[]{:S(2)}) async-start(f32[16,8,128]{2,1,0:T(8,128)} %squares.1), calls=%async_computation.2 | async-start | bytes 131072 | tf_op jit(solution)/shard_map/all_to_all | solution.py:572
  (25 other events, 35.8 us)
where the time goes:
time: 182 us; the launch traced here: 181 us
  Pallas kernels  45.3 us (25%)
  starting transfers between devices  42.5 us (23%)
  waiting for transfers between devices  33.1 us (18%)
  blocking collectives  31.6 us (17%)
  local copies, waits for them, and re-layouts  26.8 us (15%)
    ppermute x26, starting transfers between devices, swap(): return lax.ppermute(value, AXES, pairs)  39.1 us
    ppermute x26, waiting for transfers between devices, swap(): return lax.ppermute(value, AXES, pairs)  27.4 us
    unnamed x60, local copies, waits for them, and re-layouts  25 us
    all_to_all x1, blocking collectives, on_device(): got = lax.all_to_all(got, ('y_hi', 'z'), 0, 0)  17.1 us
    all_to_all x1, blocking collectives, on_device(): got = finish(lax.all_to_all(total, 'z', 0, 0))  14.5 us
    pallas_call x1, Pallas kernels, tokens_grad(): pl.pallas_call(lambda *refs: tokens_body(count, *refs), out_shape=jax.Sha...  13.1 us
    pallas_call x4, Pallas kernels, terms(): pl.pallas_call(lambda *refs: body(count, *refs), out_shape=out_shape, in_...  11.9 us
    pallas_call x1, Pallas kernels, attend_low(): pl.pallas_call(lambda *refs: attend_low_body(count, *refs), out_shape=(wi...  6.08 us
  transfers between devices with their start and end apart: 27, of which 12 were waited for; matrix products, arithmetic and copies ran while one was open for 1% of the time, Pallas kernels for 22%

commit v1 on v0

v1 whole, which is shorter than its diff:
```python
import jax
import jax.numpy as jnp
import numpy as np
from jax import lax
from jax.experimental import pallas as pl
from jax.experimental.pallas import tpu as pltpu
from jax.sharding import Mesh
from jax.sharding import PartitionSpec as P

D = 4096
HD = 128
QH = 8
QKV = 1280
TOK = 256
BLK = D // 8
HALF = BLK // 2
QUART = HALF // 2
PIECE = QUART // 8
COLS = QKV // 2
OUTW = QH * HD
LOW = COLS // HD

AXES = ("x", "y_lo", "y_hi", "z", "core")
SIZES = (4, 2, 2, 8, 2)
target_rms = 0.5
rope_base = 500000.0
F32 = jnp.float32
BF16 = jnp.bfloat16


def flat(x, y, z, c):
    return (x * 2 + y % 2) * 32 + (y // 2) * 16 + z * 2 + c


def swap(value, partner):
    pairs = []
    for x in range(4):
        for y in range(4):
            for z in range(8):
                for c in range(2):
                    pairs.append((flat(x, y, z, c), flat(*partner(x, y, z, c))))
    return lax.ppermute(value, AXES, pairs)


def near(c):
    return 1 if c == 0 else 3


def other_core(x, y, z, c):
    return x, y, z, 1 - c


def gather_x1(x, y, z, c):
    return x ^ near(c ^ (z & 1)), y, z, c


def gather_x2(x, y, z, c):
    return x ^ (4 - near(c ^ (z & 1))), y, z, c


def flip_y(x, y, z, c):
    return x, y ^ near(c), z, c


def pair_z(x, y, z, c):
    return x, y, (z ^ 1) if c == 0 else ((z + 1) % 8 if z % 2 else (z - 1) % 8), c


def x_1(x, y, z, c):
    return x ^ near(c), y, z, c


def x_2(x, y, z, c):
    return x ^ (4 - near(c)), y, z, c


def y_1(x, y, z, c):
    return x, y ^ near(c), z, c


def y_2(x, y, z, c):
    return x, y ^ (4 - near(c)), z, c


VM = pl.BlockSpec(memory_space=pltpu.VMEM)
SM = pl.BlockSpec(memory_space=pltpu.SMEM)
ANY = pl.BlockSpec(memory_space=pl.ANY)


def dot(a, b, dims):
    return lax.dot_general(a, b, (dims, ((), ())), preferred_element_type=F32)


def norm_body(at, tokens, normed, scale_r, mine, theirs):
    full = tokens[...].astype(F32)
    r = lax.rsqrt(jnp.sum(full * full, axis=1, keepdims=True) * (1.0 / D) + 1e-05)
    scale_r[...] = r
    normed[...] = (full * r).astype(BF16)
    for b in range(8):
        for k, out in enumerate((mine, theirs)):
            cols = pl.ds(pl.multiple_of(b * BLK + at[SIDE + k], HALF), HALF)
            out[b * HALF : (b + 1) * HALF, :] = normed[:, cols].T


def norm(at, tokens):
    turned = jax.ShapeDtypeStruct((D // 2, TOK), BF16)
    return pl.pallas_call(
        norm_body,
        out_shape=(
            jax.ShapeDtypeStruct((TOK, D), BF16),
            jax.ShapeDtypeStruct((TOK, 1), F32),
            turned,
            turned,
        ),
        in_specs=[SM, VM],
        out_specs=(VM, VM, VM, VM),
        compiler_params=pltpu.CompilerParams(vmem_limit_bytes=12 << 20),
        cost_estimate=pl.CostEstimate(flops=10 * TOK * D, bytes_accessed=6 << 20, transcendentals=0),
        name="norm",
    )(at, tokens)


def halves(pieces):
    return [piece[k : k + HALF, :] for piece in pieces for k in range(0, piece.shape[0], HALF)]


def project(at, first, normed, pieces):
    rows = halves(pieces)
    lhs = [normed[:, pl.ds(pl.multiple_of(at[first + i], HALF), HALF)] for i in range(len(rows))]
    return dot(jnp.concatenate(lhs, axis=1), jnp.concatenate(rows, axis=0), ((1,), (0,)))


def part_body(count, first, at, normed, *refs):
    part = project(at, first, normed, refs[:count])
    out = refs[-1]
    out[...] = part if len(refs) == count + 1 else part + refs[count][...]


def part_qkv(at, first, normed, pieces, *old):
    count, rows = len(pieces), sum(piece.shape[0] for piece in pieces)
    return pl.pallas_call(
        lambda *refs: part_body(count, first, *refs),
        out_shape=jax.ShapeDtypeStruct((TOK, QKV), F32),
        in_specs=[SM, VM] + [VM] * (count + len(old)),
        out_specs=VM,
        compiler_params=pltpu.CompilerParams(vmem_limit_bytes=16 << 20),
        cost_estimate=pl.CostEstimate(
            flops=2 * TOK * rows * QKV, bytes_accessed=rows * QKV * 2, transcendentals=0
        ),
        name="qkv_part",
    )(at, normed, *pieces, *old)


def visible(doc):
    rows = lax.broadcasted_iota(jnp.int32, (TOK, TOK), 0)
    cols = lax.broadcasted_iota(jnp.int32, (TOK, TOK), 1)
    along = jnp.broadcast_to(doc[...], (TOK, TOK))
    return (cols <= rows) & (along == along.T)


def turn(value, cos, sin):
    return value * cos + pltpu.roll(value, HD // 2, 1) * sin


def head_grads(q_rot, g, k_rot, val, seen, cos, sin):
    scale = HD**-0.5
    scores = jnp.where(seen, dot(q_rot, k_rot, ((1,), (1,))), -1e30)
    expo = jnp.exp((scores - jnp.max(scores, axis=1, keepdims=True)) * scale)
    probs = expo * (1.0 / jnp.sum(expo, axis=1, keepdims=True))
    d_probs = dot(g, val, ((1,), (1,)))
    delta = jnp.sum(d_probs * probs, axis=1, keepdims=True)
    d_scores = (probs * (d_probs - delta)).astype(BF16)
    d_val = dot(probs.astype(BF16), g, ((0,), (0,)))
    d_key = dot(d_scores, q_rot, ((0,), (0,)))
    d_query = dot(d_scores, k_rot, ((1,), (0,))) * scale
    return turn(d_query, cos, -sin).astype(BF16), d_key, d_val


def attend_low_body(count, first, at, normed, old, grad, doc, cosine, sine, *refs):
    pieces = refs[:count]
    out, rest, d_key, d_val, qkv = refs[count:]
    qkv[...] = old[...] + project(at, first, normed, pieces)
    cos, sin = cosine[...], sine[...]
    seen = visible(doc)
    k_rot = turn(qkv[:, OUTW : OUTW + HD], cos, sin).astype(BF16)
    val = qkv[:, OUTW + HD :].astype(BF16)
    total_key, total_val = jnp.zeros((TOK, HD), F32), jnp.zeros((TOK, HD), F32)
    for h in range(QH):
        head = slice(h * HD, (h + 1) * HD)
        q_rot = turn(qkv[:, head], cos, sin).astype(BF16)
        if h < LOW:
            out[:, head], key, value = head_grads(q_rot, grad[:, head], k_rot, val, seen, cos, sin)
            total_key, total_val = total_key + key, total_val + value
        else:
            rest[:, (h - LOW) * HD : (h - LOW + 1) * HD] = q_rot
    rest[:, COLS - 2 * HD : COLS - HD] = k_rot
    rest[:, COLS - HD :] = val
    d_key[...] = total_key
    d_val[...] = total_val


def attend_high_body(rest, key_low, val_low, grad, doc, cosine, sine, out):
    cos, sin = cosine[...], sine[...]
    seen = visible(doc)
    k_rot, val = rest[:, COLS - 2 * HD : COLS - HD], rest[:, COLS - HD :]
    total_key, total_val = key_low[...], val_low[...]
    for h in range(LOW, QH):
        here = slice((h - LOW) * HD, (h - LOW + 1) * HD)
        g = grad[:, h * HD : (h + 1) * HD]
        out[:, here], key, value = head_grads(rest[:, here], g, k_rot, val, seen, cos, sin)
        total_key, total_val = total_key + key, total_val + value
    out[:, COLS - 2 * HD : COLS - HD] = turn(total_key * HD**-0.5, cos, -sin).astype(BF16)
    out[:, COLS - HD :] = total_val.astype(BF16)


def attend_cost(heads):
    return pl.CostEstimate(
        flops=10 * TOK * TOK * HD * heads, bytes_accessed=4 << 20, transcendentals=TOK * TOK * heads
    )


def attend_low(at, first, normed, pieces, old, grad, doc):
    count = len(pieces)
    wide, half = jax.ShapeDtypeStruct((TOK, COLS), BF16), jax.ShapeDtypeStruct((TOK, HD), F32)
    return pl.pallas_call(
        lambda *refs: attend_low_body(count, first, *refs),
        out_shape=(wide, wide, half, half),
        in_specs=[SM] + [VM] * (6 + count),
        out_specs=(VM,) * 4,
        scratch_shapes=[pltpu.VMEM((TOK, QKV), F32)],
        compiler_params=pltpu.CompilerParams(vmem_limit_bytes=12 << 20),
        cost_estimate=attend_cost(LOW),
        name="attend_low",
    )(at, normed, old, grad, doc, *TABLES, *pieces)


def attend_high(rest, d_key, d_val, grad, doc):
    return pl.pallas_call(
        attend_high_body,
        out_shape=jax.ShapeDtypeStruct((TOK, COLS), BF16),
        in_specs=[VM] * 7,
        out_specs=VM,
        compiler_params=pltpu.CompilerParams(vmem_limit_bytes=12 << 20),
        cost_estimate=attend_cost(QH - LOW),
        name="attend_high",
    )(rest, d_key, d_val, grad, doc, *TABLES)


def tokens_body(count, first, at, d_low, d_high, tokens, scale_r, *refs):
    out, held = refs[count:]
    d_qkv = jnp.concatenate([d_low[...], d_high[...]], axis=1)
    total = jnp.zeros((TOK, 128), F32)
    for i, piece in enumerate(halves(refs[:count])):
        cols = pl.ds(pl.multiple_of(at[first + i], HALF), HALF)
        part = dot(d_qkv, piece, ((1,), (1,)))
        held[:, cols] = part
        part = part * tokens[:, cols].astype(F32)
        for k in range(0, HALF, 128):
            total = total + part[:, k : k + 128]
    r = scale_r[...]
    back = r * r * r * (jnp.sum(total, axis=1, keepdims=True) * (1.0 / D))
    for k in range(0, D, 512):
        cols = slice(k, k + 512)
        out[:, cols] = (r * held[:, cols] - tokens[:, cols].astype(F32) * back).astype(BF16)


def tokens_grad(at, first, d_low, d_high, tokens, scale_r, pieces):
    count = len(pieces)
    return pl.pallas_call(
        lambda *refs: tokens_body(count, first, *refs),
        out_shape=jax.ShapeDtypeStruct((TOK, D), BF16),
        in_specs=[SM] + [VM] * (4 + count),
        out_specs=VM,
        scratch_shapes=[pltpu.VMEM((TOK, D), F32)],
        compiler_params=pltpu.CompilerParams(vmem_limit_bytes=28 << 20),
        cost_estimate=pl.CostEstimate(flops=2 * TOK * D * QKV, bytes_accessed=16 << 20, transcendentals=0),
        name="tokens_grad",
    )(at, d_low, d_high, tokens, scale_r, *pieces)


def term_product(first, at, feats, feats_other, d_own, d_other):
    left = []
    for ref in (feats, feats_other):
        rows = [ref[pl.ds(pl.multiple_of(at[first + i], QUART), QUART), :] for i in range(8)]
        left.append(jnp.concatenate(rows, axis=0))
    right = jnp.concatenate([d_own[...], d_other[...]], axis=0)
    part = dot(jnp.concatenate(left, axis=1), right, ((1,), (0,)))
    return part.reshape(8, QUART, COLS)


def term_body(first, at, feats, feats_other, d_own, d_other, out):
    out[...] = term_product(first, at, feats, feats_other, d_own, d_other).astype(BF16)


def term_add_body(first, at, feats, feats_other, d_own, d_other, came, kept, sent):
    part = term_product(first, at, feats, feats_other, d_own, d_other)
    part = (part + came[...].astype(F32)).astype(BF16)
    kept[...] = part[:4]
    sent[...] = part[4:]


def terms(at, first, made, *came):
    if came:
        half = jax.ShapeDtypeStruct((4, QUART, COLS), BF16)
        body, out_shape, out_specs = term_add_body, (half, half), (VM, VM)
    else:
        out_shape, out_specs = jax.ShapeDtypeStruct((8, QUART, COLS), BF16), VM
        body = term_body
    return pl.pallas_call(
        lambda *refs: body(first, *refs),
        out_shape=out_shape,
        in_specs=[SM] + [VM] * (4 + len(came)),
        out_specs=out_specs,
        compiler_params=pltpu.CompilerParams(vmem_limit_bytes=12 << 20),
        cost_estimate=pl.CostEstimate(
            flops=2 * 8 * QUART * COLS * 2 * TOK, bytes_accessed=4 << 20, transcendentals=0
        ),
        name="terms",
    )(at, *made, *came)


def split_body(count, old, came, kept, sent):
    part = (old[...].astype(F32) + came[...].astype(F32)).astype(BF16)
    kept[...] = part[: count // 2]
    sent[...] = part[count // 2 :]


def split(old, came):
    count = old.shape[0]
    half = jax.ShapeDtypeStruct((count // 2, QUART, COLS), BF16)
    return pl.pallas_call(
        lambda *refs: split_body(count, *refs),
        out_shape=(half, half),
        in_specs=[VM, VM],
        out_specs=(VM, VM),
        compiler_params=pltpu.CompilerParams(vmem_limit_bytes=6 << 20),
        name="split",
    )(old, came)


def join_body(old_x, came_x, old_y, came_y, out):
    out[:, :, :COLS] = (old_x[...].astype(F32) + came_x[...].astype(F32)).astype(BF16).reshape(8, PIECE, COLS)
    out[:, :, COLS:] = (old_y[...].astype(F32) + came_y[...].astype(F32)).astype(BF16).reshape(8, PIECE, COLS)


def join(*parts):
    return pl.pallas_call(
        join_body,
        out_shape=jax.ShapeDtypeStruct((8, PIECE, QKV), BF16),
        in_specs=[VM] * 4,
        out_specs=VM,
        compiler_params=pltpu.CompilerParams(vmem_limit_bytes=4 << 20),
        name="join",
    )(*parts)


def finish_body(parts, out):
    total = sum(parts[i].astype(F32) for i in range(8)).astype(BF16)
    for i in range(16):
        out[i] = total


def finish(parts):
    return pl.pallas_call(
        finish_body,
        out_shape=jax.ShapeDtypeStruct((16, PIECE, QKV), BF16),
        in_specs=[VM],
        out_specs=VM,
        compiler_params=pltpu.CompilerParams(vmem_limit_bytes=4 << 20),
        name="finish",
    )(parts)


def squares_body(got, out):
    total = jnp.zeros((PIECE, QKV), F32)
    for i in range(16):
        value = got[i].astype(F32)
        total = total + value * value
    total = jnp.sum(jnp.sum(total, axis=1, keepdims=True), axis=0, keepdims=True)
    out[...] = jnp.broadcast_to(total.reshape(1, 1, 1), (16, 8, 128))


def squares(got):
    return pl.pallas_call(
        squares_body,
        out_shape=jax.ShapeDtypeStruct((16, 8, 128), F32),
        in_specs=[VM],
        out_specs=VM,
        compiler_params=pltpu.CompilerParams(vmem_limit_bytes=4 << 20),
        name="squares",
    )(got)


def rescale_body(at, parts, mine, theirs, out):
    total = sum(parts[i] for i in range(16))
    factor = (target_rms * lax.rsqrt(total * (1.0 / (D * QKV)) + 1e-06))[:1, :1]
    for i, half in enumerate((mine, theirs)):
        rows = pl.ds(pl.multiple_of(at[SIDE + i], HALF), HALF)
        out[rows, :] = (half[...].reshape(HALF, QKV).astype(F32) * factor).astype(BF16)


def rescale(at, parts, mine, theirs):
    return pl.pallas_call(
        rescale_body,
        out_shape=jax.ShapeDtypeStruct((BLK, QKV), BF16),
        in_specs=[SM, VM, VM, VM],
        out_specs=VM,
        compiler_params=pltpu.CompilerParams(vmem_limit_bytes=8 << 20),
        name="rescale",
    )(at, parts, mine, theirs)


def tables():
    freq = np.exp(-np.log(rope_base) * 2.0 * np.arange(HD // 2) / HD)
    angle = np.arange(TOK)[:, None] * freq[None, :]
    cos, sin = np.cos(angle), np.sin(angle)
    return np.concatenate([cos, cos], 1).astype(np.float32), np.concatenate([-sin, sin], 1).astype(np.float32)


TABLES = tables()

LATE, SIDE, SEND_X, SEND_Y, KEEP_X, KEEP_Y = 12, 16, 18, 26, 34, 42


def indices(x, y, z, c):
    turned = c ^ (z & 1)
    step = {"0": 0, "a": 1 + 2 * turned, "b": 3 - 2 * turned, "o": 2}

    def column(name, flip, half):
        return ((x ^ step[name]) * 2 + ((y & 1) ^ flip)) * BLK + half * HALF

    own, other = c, 1 - c
    first = [("0", 0, 0), ("0", 0, 1), ("0", 1, own), ("a", 0, own), ("b", 0, other), ("0", 1, other)]
    middle = [("o", 0, own), ("a", 1, own), ("b", 0, own), ("o", 0, other), ("b", 1, other), ("a", 0, other)]
    late = [("o", 1, own), ("b", 1, own), ("o", 1, other), ("a", 1, other)]
    out = [column(*spot) for spot in first + middle + late] + [own * HALF, other * HALF]
    order = [0, 3 - 2 * c, 1 + 2 * c, 2]

    def row(i, j):
        yy = y ^ order[j]
        return ((x ^ order[i]) * 2 + (yy & 1)) * HALF + (yy >> 1) * QUART

    for pair in ((2, 3), (0, 1)):
        out += [row(i, j) for i in pair for j in range(4)]
        out += [row(i, j) for j in pair for i in range(4)]
    return out


def index_table():
    rows = [None] * 256
    for x in range(4):
        for y in range(4):
            for z in range(8):
                for c in range(2):
                    rows[flat(x, y, z, c)] = indices(x, y, z, c)
    return np.array(rows, np.int32)


def on_device(tokens, grad_attended, doc_ids, w_own):
    c = lax.axis_index("core")
    at = lax.dynamic_index_in_dim(jnp.asarray(index_table()), lax.axis_index(AXES), 0, False)

    w00 = lax.dynamic_slice_in_dim(w_own, c * HALF, HALF, 0)
    at, w00 = lax.optimization_barrier((at, w00))
    wa0 = swap(w00, gather_x1)
    w01 = swap(w00, flip_y)
    normed, scale_r, feats, theirs = norm(at, tokens)
    wa0, normed, theirs = lax.optimization_barrier((wa0, normed, theirs))
    wo0 = swap(wa0, gather_x2)
    wa1 = swap(wa0, flip_y)
    wb0 = swap(wa0, pair_z)
    vb0 = swap(wa0, other_core)
    v01 = swap(w01, other_core)
    early = [w_own, w01, wa0, vb0, v01]
    part = part_qkv(at, 0, normed, early)
    wo0, wa1, part = lax.optimization_barrier((wo0, wa1, part))
    wo1 = swap(wo0, flip_y)
    wb1 = swap(wa1, pair_z)
    vo0 = swap(wo0, other_core)
    va0 = swap(wb0, other_core)
    vb1 = swap(wa1, other_core)
    feats_other = swap(theirs, other_core)
    middle = [wo0, wa1, wb0, vo0, vb1, va0]
    part = part_qkv(at, 6, normed, middle, part)
    wo1, wb1, part = lax.optimization_barrier((wo1, wb1, part))
    vo1 = swap(wo1, other_core)
    va1 = swap(wb1, other_core)
    late = [wo1, wb1, vo1, va1]
    d_low, rest, d_key, d_val = attend_low(at, LATE, normed, late, part, grad_attended, doc_ids)

    low_other = swap(d_low, other_core)
    d_high = attend_high(rest, d_key, d_val, grad_attended, doc_ids)
    low_other, d_high = lax.optimization_barrier((low_other, d_high))
    high_other = swap(d_high, other_core)
    lows, highs = (feats, feats_other, d_low, low_other), (feats, feats_other, d_high, high_other)
    came_x = swap(terms(at, SEND_X, lows), x_1)
    came_y = swap(terms(at, SEND_Y, highs), y_1)
    d_tokens = tokens_grad(at, 0, d_low, d_high, tokens, scale_r, early + middle + late)
    came_x, came_y, d_tokens = lax.optimization_barrier((came_x, came_y, d_tokens))
    sum_x, sent_x = terms(at, KEEP_X, lows, came_x)
    came_x = swap(sent_x, x_2)
    sum_y, sent_y = terms(at, KEEP_Y, highs, came_y)
    came_y = swap(sent_y, y_2)
    for step_x, step_y in ((y_1, x_1), (y_2, x_2)):
        sum_x, sent_x = split(sum_x, came_x)
        came_x = swap(sent_x, step_x)
        sum_y, sent_y = split(sum_y, came_y)
        came_y = swap(sent_y, step_y)

    total = join(sum_x, came_x, sum_y, came_y)
    got = finish(lax.all_to_all(total, "z", 0, 0))
    got = lax.all_to_all(got, ("y_hi", "z"), 0, 0)

    theirs = swap(got, other_core)
    parts = lax.all_to_all(squares(got), ("x", "y_lo", "core"), 0, 0)
    return d_tokens, rescale(at, parts, got, theirs)


def solution(mesh):
    mesh = Mesh(mesh.devices.reshape(SIZES), AXES)
    spread, rows = P(AXES, None), P(AXES[:2], None)
    return jax.shard_map(
        on_device,
        mesh=mesh,
        in_specs=(spread, spread, spread, rows),
        out_specs=(spread, rows),
        check_vma=False,
    )
```

time: 182 us -> 159 us (0.87)
  local copies, waits for them, and re-layouts: 26.8 us -> 3.56 us
  Pallas kernels: 45.3 us -> 26.8 us
  waiting for transfers between devices: 33.1 us -> 46.5 us
  blocking collectives: 31.6 us -> 41.5 us
  starting transfers between devices: 42.5 us -> 39.8 us
    unnamed x60 -> x14, local copies, waits for them, and re-layouts: 25 us -> 1.63 us
    ppermute x26, waiting for transfers between devices: 27.4 us -> 46.5 us  [swap(): return lax.ppermute(value, AXES, pairs)]
    pallas_call x7 -> x8, Pallas kernels: 36.8 us -> 20.1 us  [the longest x4 6.06 us: terms(): pl.pallas_call(lambda *refs: body(first, *refs), out_shape=out_shape, in_...]
    all_to_all x0 -> x1, blocking collectives: none -> 9.81 us  [on_device(): parts = lax.all_to_all(squares(got), ('x', 'y_lo', 'core'), 0, 0)]
    all_to_all x1 -> x0, waiting for transfers between devices: 5.73 us -> none  [on_device(): parts = lax.all_to_all(squares(got), ('x', 'y_lo', 'core'), 0, 0)]
    all_to_all x1 -> x0, starting transfers between devices: 3.4 us -> none  [on_device(): parts = lax.all_to_all(squares(got), ('x', 'y_lo', 'core'), 0, 0)]
  transfers between devices with their start and end apart: 27 -> 26, of which waited for: 12 -> 15; matrix products, arithmetic and copies ran while one was open for 1% -> 0% of each run, Pallas kernels for 22% -> 15%
where the time goes in v1:
time: 159 us
  waiting for transfers between devices  46.5 us (29%)
  blocking collectives  41.5 us (26%)
  starting transfers between devices  39.8 us (25%)
  Pallas kernels  26.8 us (17%)
  local copies, waits for them, and re-layouts  3.56 us (2%)
    ppermute x26, waiting for transfers between devices, swap(): return lax.ppermute(value, AXES, pairs)  46.5 us
    ppermute x26, starting transfers between devices, swap(): return lax.ppermute(value, AXES, pairs)  39.8 us
    all_to_all x1, blocking collectives, on_device(): got = lax.all_to_all(got, ('y_hi', 'z'), 0, 0)  17.6 us
    all_to_all x1, blocking collectives, on_device(): got = finish(lax.all_to_all(total, 'z', 0, 0))  14.1 us
    all_to_all x1, blocking collectives, on_device(): parts = lax.all_to_all(squares(got), ('x', 'y_lo', 'core'), 0, 0)  9.81 us
    pallas_call x4, Pallas kernels, terms(): pl.pallas_call(lambda *refs: body(first, *refs), out_shape=out_shape, in_...  6.06 us
    pallas_call x1, Pallas kernels, tokens_grad(): pl.pallas_call(lambda *refs: tokens_body(count, first, *refs), out_shape=...  5.82 us
    pallas_call x1, Pallas kernels, attend_low(): pl.pallas_call(lambda *refs: attend_low_body(count, first, *refs), out_sh...  4.79 us
  transfers between devices with their start and end apart: 26, of which 15 were waited for; matrix products, arithmetic and copies ran while one was open for 0% of the time, Pallas kernels for 15%

profile of v1, /device:TPU:1, one launch (start us, length us, event | category | flops | bytes accessed | tf_op | source)
XLA Modules:
  0.0 159.0 jit_solution(17831990488708383227)
XLA Ops:
  2.6 3.4 %collective-permute-start = (bf16[256,1280]{1,0:T(8,128)(2,1)S(1)}, bf16[256,1280]{1,0:T(8,128)(2,1)S(1)}, u32[]{:S(2)}, u32[]{:S(2)}) collective-permute-start(bf16[256,1280]{1,0:T(8,128)(2,1)S(1)} %constant_dynamic-slice_fusion), channel_id=1, source_target_pairs={{0,64},{1,193},{2,194},{3,67},{4,68},{5,197},{6,198},{7,71},{8,72}... | collective-permute-start | bytes 1966088 | tf_op jit(solution)/shard_map/ppermute | solution.py:42
  6.0 2.7 %collective-permute-start.4 = (bf16[256,1280]{1,0:T(8,128)(2,1)S(1)}, bf16[256,1280]{1,0:T(8,128)(2,1)S(1)}, u32[]{:S(2)}, u32[]{:S(2)}) collective-permute-start(bf16[256,1280]{1,0:T(8,128)(2,1)S(1)} %constant_dynamic-slice_fusion), channel_id=1, source_target_pairs={{0,32},{1,49},{2,34},{3,51},{4,36},{5,53},{6,38},{7,55},{8,40},{9,... | collective-permute-start | bytes 1966088 | tf_op jit(solution)/shard_map/ppermute | solution.py:42
  8.7 1.6 copy-done
  10.3 2.0 %norm.1 = (bf16[256,4096]{1,0:T(8,128)(2,1)S(1)}, f32[256,1]{1,0:T(8,128)S(1)}, bf16[2048,256]{1,0:T(8,128)(2,1)S(1)}, bf16[2048,256]{1,0:T(8,128)(2,1)S(1)}) custom-call(s32[50]{0:T(128)S(1)} %dynamic-slice_bitcast_fusion.at.refs_0_, bf16[256,4096]{1,0:T(8,128)(2,1)S(1)} %copy-done), custom_call_target="tpu_custom_call" | custom-call | flops 10485760 | bytes 6291456 | tf_op jit(solution)/shard_map/norm/pallas_call | solution.py:107
  12.3 1.7 %collective-permute-done.refs_4_.refs_7_ = bf16[256,1280]{1,0:T(8,128)(2,1)S(1)} collective-permute-done((bf16[256,1280]{1,0:T(8,128)(2,1)S(1)}, bf16[256,1280]{1,0:T(8,128)(2,1)S(1)}, u32[]{:S(2)}, u32[]{:S(2)}) %collective-permute-start) | collective-permute-done | bytes 655392 | tf_op jit(solution)/shard_map/ppermute | solution.py:42
  14.0 2.7 %collective-permute-done.4.refs_3_.refs_6_ = bf16[256,1280]{1,0:T(8,128)(2,1)S(1)} collective-permute-done((bf16[256,1280]{1,0:T(8,128)(2,1)S(1)}, bf16[256,1280]{1,0:T(8,128)(2,1)S(1)}, u32[]{:S(2)}, u32[]{:S(2)}) %collective-permute-start.4) | collective-permute-done | bytes 655392 | tf_op jit(solution)/shard_map/ppermute | solution.py:42
  17.2 2.7 %collective-permute-start.3 = (bf16[256,1280]{1,0:T(8,128)(2,1)S(1)}, bf16[256,1280]{1,0:T(8,128)(2,1)S(1)}, u32[]{:S(2)}, u32[]{:S(2)}) collective-permute-start(bf16[256,1280]{1,0:T(8,128)(2,1)S(1)} %collective-permute-done.refs_4_.refs_7_), channel_id=1, source_target_pairs={{0,32},{1,49},{2,34},{3,51},{4,36},{5,53},{6,38},{7,55},{8,40},{9,... | collective-permute-start | bytes 1966088 | tf_op jit(solution)/shard_map/ppermute | solution.py:42
  19.9 6.9 %collective-permute-start.9 = (bf16[256,1280]{1,0:T(8,128)(2,1)S(1)}, bf16[256,1280]{1,0:T(8,128)(2,1)S(1)}, u32[]{:S(2)}, u32[]{:S(2)}) collective-permute-start(bf16[256,1280]{1,0:T(8,128)(2,1)S(1)} %collective-permute-done.refs_4_.refs_7_), channel_id=1, source_target_pairs={{0,2},{1,15},{2,0},{3,5},{4,6},{5,3},{6,4},{7,9},{8,10},{9,7},{10,... | collective-permute-start | bytes 1966088 | tf_op jit(solution)/shard_map/ppermute | solution.py:42
  26.8 1.7 %qkv_part.2.refs_8_ = f32[256,1280]{1,0:T(8,128)S(1)} custom-call(s32[50]{0:T(128)S(1)} %dynamic-slice_bitcast_fusion.at.refs_0_, bf16[256,4096]{1,0:T(8,128)(2,1)S(1)} %get-tuple-element.44.refs_1_, bf16[512,1280]{1,0:T(8,128)(2,1)S(1)} %copy-done.2, bf16[256,1280]{1,0:T(8,128)(2,1)S(1)} %collective-permute-done.4.refs_3_.refs_6_, ...), custom_call_target="tpu_custom_call" | custom-call | flops 1006632960 | bytes 3932160 | tf_op jit(solution)/shard_map/qkv_part/pallas_call | solution.py:141
  30.1 4.6 %collective-permute-done.9.refs_4_.refs_12_ = bf16[256,1280]{1,0:T(8,128)(2,1)S(1)} collective-permute-done((bf16[256,1280]{1,0:T(8,128)(2,1)S(1)}, bf16[256,1280]{1,0:T(8,128)(2,1)S(1)}, u32[]{:S(2)}, u32[]{:S(2)}) %collective-permute-start.9) | collective-permute-done | bytes 655392 | tf_op jit(solution)/shard_map/ppermute | solution.py:42
  35.3 2.9 %collective-permute-start.8 = (bf16[256,1280]{1,0:T(8,128)(2,1)S(1)}, bf16[256,1280]{1,0:T(8,128)(2,1)S(1)}, u32[]{:S(2)}, u32[]{:S(2)}) collective-permute-start(bf16[256,1280]{1,0:T(8,128)(2,1)S(1)} %collective-permute-done.3.refs_3_.refs_11_), channel_id=1, source_target_pairs={{0,2},{1,15},{2,0},{3,5},{4,6},{5,3},{6,4},{7,9},{8,10},{9,7},{10,... | collective-permute-start | bytes 1966088 | tf_op jit(solution)/shard_map/ppermute | solution.py:42
  38.2 1.7 %qkv_part.3.refs_2_ = f32[256,1280]{1,0:T(8,128)S(1)} custom-call(s32[50]{0:T(128)S(1)} %dynamic-slice_bitcast_fusion.at.refs_0_, bf16[256,4096]{1,0:T(8,128)(2,1)S(1)} %get-tuple-element.44.refs_1_, bf16[256,1280]{1,0:T(8,128)(2,1)S(1)} %collective-permute-done.2.refs_2_.refs_10_, bf16[256,1280]{1,0:T(8,128)(2,1)S(1)} %collective-permute-done.3.refs_3_.refs_11_, ...), custom_call_target="tpu_custom_call" | custom-call | flops 1006632960 | bytes 3932160 | tf_op jit(solution)/shard_map/qkv_part/pallas_call | solution.py:141
  39.9 6.0 %collective-permute-done.7.refs_7_.refs_16_ = bf16[256,1280]{1,0:T(8,128)(2,1)S(1)} collective-permute-done((bf16[256,1280]{1,0:T(8,128)(2,1)S(1)}, bf16[256,1280]{1,0:T(8,128)(2,1)S(1)}, u32[]{:S(2)}, u32[]{:S(2)}) %collective-permute-start.7) | collective-permute-done | bytes 655392 | tf_op jit(solution)/shard_map/ppermute | solution.py:42
  46.7 1.6 collective-permute-done.13.refs_9_.refs_18_
  49.2 4.8 %attend_low.1 = (bf16[256,640]{1,0:T(8,128)(2,1)S(1)}, bf16[256,640]{1,0:T(8,128)(2,1)S(1)}, f32[256,128]{1,0:T(8,128)S(1)}, f32[256,128]{1,0:T(8,128)S(1)}) custom-call(s32[50]{0:T(128)S(1)} %dynamic-slice_bitcast_fusion.at.refs_0_, bf16[256,4096]{1,0:T(8,128)(2,1)S(1)} %get-tuple-element.44.refs_1_, f32[256,1280]{1,0:T(8,128)S(1)} %qkv_part.3.refs_2_, ...), custom_call_target="tpu_custom_call" | custom-call | flops 419430400 | bytes 4194304 | tf_op jit(solution)/shard_map/attend_low/pallas_call | solution.py:225
  54.2 1.9 %attend_high.1.refs_3_.refs_2_ = bf16[256,640]{1,0:T(8,128)(2,1)S(1)} custom-call(bf16[256,640]{1,0:T(8,128)(2,1)S(1)} %get-tuple-element.53.rest, f32[256,128]{1,0:T(8,128)S(1)} %get-tuple-element.54.key_low, f32[256,128]{1,0:T(8,128)S(1)} %get-tuple-element.55.val_low, bf16[256,1024]{1,0:T(8,128)(2,1)S(1)} %copy-done.3, s32[1,256]{1,0:T(1,128)S(1)} %copy-done.6, ...), custom_call_target="tpu_custom_call" | custom-call | flops 251658240 | bytes 4194304 | tf_op jit(solution)/shard_map/attend_high/pallas_call | solution.py:238
  58.1 1.6 collective-permute-start.16
  61.3 3.0 %collective-permute-start.18 = (bf16[8,128,640]{2,1,0:T(8,128)(2,1)S(1)}, bf16[8,128,640]{2,1,0:T(8,128)(2,1)S(1)}, u32[]{:S(2)}, u32[]{:S(2)}) collective-permute-start(bf16[8,128,640]{2,1,0:T(8,128)(2,1)S(1)} %terms.5), channel_id=1, source_target_pairs={{0,32},{1,49},{2,34},{3,51},{4,36},{5,53},{6,38},{7,55},{8,40},{9,... | collective-permute-start | bytes 3932168 | tf_op jit(solution)/shard_map/ppermute | solution.py:42
  64.2 5.8 %tokens_grad.1 = bf16[256,4096]{1,0:T(8,128)(2,1)} custom-call(s32[50]{0:T(128)S(1)} %dynamic-slice_bitcast_fusion.at.refs_0_, bf16[256,640]{1,0:T(8,128)(2,1)S(1)} %get-tuple-element.52.refs_3_.refs_1_, bf16[256,640]{1,0:T(8,128)(2,1)S(1)} %attend_high.1.refs_3_.refs_2_, bf16[256,4096]{1,0:T(8,128)(2,1)S(1)} %copy-done.1, ...), custom_call_target="tpu_custom_call" | custom-call | flops 2684354560 | bytes 16777216 | tf_op jit(solution)/shard_map/tokens_grad/pallas_call | solution.py:269
  70.0 5.9 %collective-permute-done.16.refs_5_ = bf16[8,128,640]{2,1,0:T(8,128)(2,1)S(1)} collective-permute-done((bf16[8,128,640]{2,1,0:T(8,128)(2,1)S(1)}, bf16[8,128,640]{2,1,0:T(8,128)(2,1)S(1)}, u32[]{:S(2)}, u32[]{:S(2)}) %collective-permute-start.16) | collective-permute-done | bytes 1310752 | tf_op jit(solution)/shard_map/ppermute | solution.py:42
  75.9 3.3 %collective-permute-done.18.refs_5_ = bf16[8,128,640]{2,1,0:T(8,128)(2,1)S(1)} collective-permute-done((bf16[8,128,640]{2,1,0:T(8,128)(2,1)S(1)}, bf16[8,128,640]{2,1,0:T(8,128)(2,1)S(1)}, u32[]{:S(2)}, u32[]{:S(2)}) %collective-permute-start.18) | collective-permute-done | bytes 1310752 | tf_op jit(solution)/shard_map/ppermute | solution.py:42
  82.5 8.0 %collective-permute-done.19.refs_1_ = bf16[4,128,640]{2,1,0:T(8,128)(2,1)S(1)} collective-permute-done((bf16[4,128,640]{2,1,0:T(8,128)(2,1)S(1)}, bf16[4,128,640]{2,1,0:T(8,128)(2,1)S(1)}, u32[]{:S(2)}, u32[]{:S(2)}) %collective-permute-start.19) | collective-permute-done | bytes 655392 | tf_op jit(solution)/shard_map/ppermute | solution.py:42
  90.7 2.7 %collective-permute-start.20 = (bf16[2,128,640]{2,1,0:T(8,128)(2,1)S(1)}, bf16[2,128,640]{2,1,0:T(8,128)(2,1)S(1)}, u32[]{:S(2)}, u32[]{:S(2)}) collective-permute-start(bf16[2,128,640]{2,1,0:T(8,128)(2,1)S(1)} %get-tuple-element.64), channel_id=1, source_target_pairs={{0,32},{1,49},{2,34},{3,51},{4,36},{5,53},{6,38},{7,55},{8,40},{9,... | collective-permute-start | bytes 983048 | tf_op jit(solution)/shard_map/ppermute | solution.py:42
  94.7 3.7 %collective-permute-done.20.refs_1_ = bf16[2,128,640]{2,1,0:T(8,128)(2,1)S(1)} collective-permute-done((bf16[2,128,640]{2,1,0:T(8,128)(2,1)S(1)}, bf16[2,128,640]{2,1,0:T(8,128)(2,1)S(1)}, u32[]{:S(2)}, u32[]{:S(2)}) %collective-permute-start.20) | collective-permute-done | bytes 327712 | tf_op jit(solution)/shard_map/ppermute | solution.py:42
  98.6 2.3 %collective-permute-done.23.refs_1_ = bf16[2,128,640]{2,1,0:T(8,128)(2,1)S(1)} collective-permute-done((bf16[2,128,640]{2,1,0:T(8,128)(2,1)S(1)}, bf16[2,128,640]{2,1,0:T(8,128)(2,1)S(1)}, u32[]{:S(2)}, u32[]{:S(2)}) %collective-permute-start.23) | collective-permute-done | bytes 327712 | tf_op jit(solution)/shard_map/ppermute | solution.py:42
  101.0 1.8 %collective-permute-done.21.came_x = bf16[1,128,640]{2,1,0:T(8,128)(2,1)S(1)} collective-permute-done((bf16[1,128,640]{2,1,0:T(8,128)(2,1)S(1)}, bf16[1,128,640]{2,1,0:T(8,128)(2,1)S(1)}, u32[]{:S(2)}, u32[]{:S(2)}) %collective-permute-start.21) | collective-permute-done | bytes 163872 | tf_op jit(solution)/shard_map/ppermute | solution.py:42
  102.8 2.7 %collective-permute-done.24.came_y = bf16[1,128,640]{2,1,0:T(8,128)(2,1)S(1)} collective-permute-done((bf16[1,128,640]{2,1,0:T(8,128)(2,1)S(1)}, bf16[1,128,640]{2,1,0:T(8,128)(2,1)S(1)}, u32[]{:S(2)}, u32[]{:S(2)}) %collective-permute-start.24) | collective-permute-done | bytes 163872 | tf_op jit(solution)/shard_map/ppermute | solution.py:42
  105.6 14.1 %all_to_all.15.parts = bf16[8,16,1280]{2,1,0:T(8,128)(2,1)S(1)} all-to-all(bf16[8,16,1280]{2,1,0:T(8,128)(2,1)S(1)} %join.1), channel_id=1, replica_groups=mesh['x'=4,'y_lo'=2,'y_hi'=2,'z'=8,'core'=2] {'z'}, dimensions={0} | all-to-all | bytes 655360 | tf_op jit(solution)/shard_map/all_to_all | solution.py:511
  119.7 17.6 %all_to_all.16.got.mine = bf16[16,16,1280]{2,1,0:T(8,128)(2,1)S(1)} all-to-all(bf16[16,16,1280]{2,1,0:T(8,128)(2,1)S(1)} %finish.1), channel_id=1, replica_groups=mesh['x'=4,'y_lo'=2,'y_hi'=2,'z'=8,'core'=2] {'y_hi','z'}, dimensions={0} | all-to-all | bytes 1310720 | tf_op jit(solution)/shard_map/all_to_all | solution.py:512
  137.3 9.7 %collective-permute-start.25 = (bf16[16,16,1280]{2,1,0:T(8,128)(2,1)S(1)}, bf16[16,16,1280]{2,1,0:T(8,128)(2,1)S(1)}, u32[]{:S(2)}, u32[]{:S(2)}) collective-permute-start(bf16[16,16,1280]{2,1,0:T(8,128)(2,1)S(1)} %all_to_all.16.got.mine), channel_id=1, source_target_pairs={{0,1},{1,0},{2,3},{3,2},{4,5},{5,4},{6,7},{7,6},{8,9},{9,8},{10,11... | collective-permute-start | bytes 1966088 | tf_op jit(solution)/shard_map/ppermute | solution.py:42
  147.2 9.8 %all_to_all.17.parts = f32[16,8,128]{2,1,0:T(8,128)S(1)} all-to-all(f32[16,8,128]{2,1,0:T(8,128)S(1)} %squares.1), channel_id=1, replica_groups=mesh['x'=4,'y_lo'=2,'y_hi'=2,'z'=8,'core'=2] {'x','y_lo','core'}, dimensions={0} | all-to-all | bytes 131072 | tf_op jit(solution)/shard_map/all_to_all | solution.py:515
  157.0 2.0 %rescale.1 = bf16[512,1280]{1,0:T(8,128)(2,1)} custom-call(s32[50]{0:T(128)S(1)} %dynamic-slice_bitcast_fusion.at.refs_0_, f32[16,8,128]{2,1,0:T(8,128)S(1)} %all_to_all.17.parts, bf16[16,16,1280]{2,1,0:T(8,128)(2,1)S(1)} %all_to_all.16.got.mine, bf16[16,16,1280]{2,1,0:T(8,128)(2,1)S(1)} %collective-permute-done.25.theirs), custom_call_target="tpu_custom_call" | custom-call | tf_op jit(solution)/shard_map/rescale/pallas_call | solution.py:403
  (57 shorter events, 15.3 us)
Async XLA Ops:
  1.3 25.4 %copy-start.2 = (bf16[512,1280]{1,0:T(8,128)(2,1)S(1)}, bf16[512,1280]{1,0:T(8,128)(2,1)}, u32[]{:S(2)}) copy-start(bf16[512,1280]{1,0:T(8,128)(2,1)} %refs_5_.2) | copy-start | bytes 3932164
  2.6 11.4 %collective-permute-start = (bf16[256,1280]{1,0:T(8,128)(2,1)S(1)}, bf16[256,1280]{1,0:T(8,128)(2,1)S(1)}, u32[]{:S(2)}, u32[]{:S(2)}) collective-permute-start(bf16[256,1280]{1,0:T(8,128)(2,1)S(1)} %constant_dynamic-slice_fusion), channel_id=1, source_target_pairs={{0,64},{1,193},{2,194},{3,67},{4,68},{5,197},{6,198},{7,71},{8,72}... | collective-permute-start | bytes 1966088 | tf_op jit(solution)/shard_map/ppermute | solution.py:42
  6.0 10.7 %collective-permute-start.4 = (bf16[256,1280]{1,0:T(8,128)(2,1)S(1)}, bf16[256,1280]{1,0:T(8,128)(2,1)S(1)}, u32[]{:S(2)}, u32[]{:S(2)}) collective-permute-start(bf16[256,1280]{1,0:T(8,128)(2,1)S(1)} %constant_dynamic-slice_fusion), channel_id=1, source_target_pairs={{0,32},{1,49},{2,34},{3,51},{4,36},{5,53},{6,38},{7,55},{8,40},{9,... | collective-permute-start | bytes 1966088 | tf_op jit(solution)/shard_map/ppermute | solution.py:42
  16.7 10.1 %collective-permute-start.6 = (bf16[256,1280]{1,0:T(8,128)(2,1)S(1)}, bf16[256,1280]{1,0:T(8,128)(2,1)S(1)}, u32[]{:S(2)}, u32[]{:S(2)}) collective-permute-start(bf16[256,1280]{1,0:T(8,128)(2,1)S(1)} %collective-permute-done.4.refs_3_.refs_6_), channel_id=1, source_target_pairs={{0,1},{1,0},{2,3},{3,2},{4,5},{5,4},{6,7},{7,6},{8,9},{9,8},{10,11... | collective-permute-start | bytes 1966088 | tf_op jit(solution)/shard_map/ppermute | solution.py:42
  16.7 10.1 %collective-permute-start.5 = (bf16[256,1280]{1,0:T(8,128)(2,1)S(1)}, bf16[256,1280]{1,0:T(8,128)(2,1)S(1)}, u32[]{:S(2)}, u32[]{:S(2)}) collective-permute-start(bf16[256,1280]{1,0:T(8,128)(2,1)S(1)} %collective-permute-done.refs_4_.refs_7_), channel_id=1, source_target_pairs={{0,1},{1,0},{2,3},{3,2},{4,5},{5,4},{6,7},{7,6},{8,9},{9,8},{10,11... | collective-permute-start | bytes 1966088 | tf_op jit(solution)/shard_map/ppermute | solution.py:42
  17.2 11.4 %collective-permute-start.3 = (bf16[256,1280]{1,0:T(8,128)(2,1)S(1)}, bf16[256,1280]{1,0:T(8,128)(2,1)S(1)}, u32[]{:S(2)}, u32[]{:S(2)}) collective-permute-start(bf16[256,1280]{1,0:T(8,128)(2,1)S(1)} %collective-permute-done.refs_4_.refs_7_), channel_id=1, source_target_pairs={{0,32},{1,49},{2,34},{3,51},{4,36},{5,53},{6,38},{7,55},{8,40},{9,... | collective-permute-start | bytes 1966088 | tf_op jit(solution)/shard_map/ppermute | solution.py:42
  19.9 9.7 %collective-permute-start.2 = (bf16[256,1280]{1,0:T(8,128)(2,1)S(1)}, bf16[256,1280]{1,0:T(8,128)(2,1)S(1)}, u32[]{:S(2)}, u32[]{:S(2)}) collective-permute-start(bf16[256,1280]{1,0:T(8,128)(2,1)S(1)} %collective-permute-done.refs_4_.refs_7_), channel_id=1, source_target_pairs={{0,192},{1,65},{2,66},{3,195},{4,196},{5,69},{6,70},{7,199},{8,200... | collective-permute-start | bytes 1966088 | tf_op jit(solution)/shard_map/ppermute | solution.py:42
  19.9 14.9 %collective-permute-start.9 = (bf16[256,1280]{1,0:T(8,128)(2,1)S(1)}, bf16[256,1280]{1,0:T(8,128)(2,1)S(1)}, u32[]{:S(2)}, u32[]{:S(2)}) collective-permute-start(bf16[256,1280]{1,0:T(8,128)(2,1)S(1)} %collective-permute-done.refs_4_.refs_7_), channel_id=1, source_target_pairs={{0,2},{1,15},{2,0},{3,5},{4,6},{5,3},{6,4},{7,9},{8,10},{9,7},{10,... | collective-permute-start | bytes 1966088 | tf_op jit(solution)/shard_map/ppermute | solution.py:42
  28.5 20.7 %copy-start.3 = (bf16[256,1024]{1,0:T(8,128)(2,1)S(1)}, bf16[256,1024]{1,0:T(8,128)(2,1)}, u32[]{:S(2)}) copy-start(bf16[256,1024]{1,0:T(8,128)(2,1)} %grad.1) | copy-start | bytes 1572868
  28.5 20.7 %copy-start.4 = (f32[256,128]{1,0:T(8,128)S(1)}, f32[256,128]{1,0:T(8,128)}, u32[]{:S(2)}) copy-start(f32[256,128]{1,0:T(8,128)} %constant.48.clone.refs_6_.sine) | copy-start | bytes 393220
  28.5 20.7 %copy-start.5 = (f32[256,128]{1,0:T(8,128)S(1)}, f32[256,128]{1,0:T(8,128)}, u32[]{:S(2)}) copy-start(f32[256,128]{1,0:T(8,128)} %constant.47.clone.refs_5_.cosine) | copy-start | bytes 393220
  28.6 20.6 %copy-start.6 = (s32[1,256]{1,0:T(1,128)S(1)}, s32[1,256]{1,0:T(1,128)}, u32[]{:S(2)}) copy-start(s32[1,256]{1,0:T(1,128)} %doc.1) | copy-start | bytes 3076
  29.6 8.6 %collective-permute-start.10 = (bf16[256,1280]{1,0:T(8,128)(2,1)S(1)}, bf16[256,1280]{1,0:T(8,128)(2,1)S(1)}, u32[]{:S(2)}, u32[]{:S(2)}) collective-permute-start(bf16[256,1280]{1,0:T(8,128)(2,1)S(1)} %collective-permute-done.2.refs_2_.refs_10_), channel_id=1, source_target_pairs={{0,1},{1,0},{2,3},{3,2},{4,5},{5,4},{6,7},{7,6},{8,9},{9,8},{10,11... | collective-permute-start | bytes 1966088 | tf_op jit(solution)/shard_map/ppermute | solution.py:42
  34.7 3.4 %collective-permute-start.12 = (bf16[256,1280]{1,0:T(8,128)(2,1)S(1)}, bf16[256,1280]{1,0:T(8,128)(2,1)S(1)}, u32[]{:S(2)}, u32[]{:S(2)}) collective-permute-start(bf16[256,1280]{1,0:T(8,128)(2,1)S(1)} %collective-permute-done.9.refs_4_.refs_12_), channel_id=1, source_target_pairs={{0,1},{1,0},{2,3},{3,2},{4,5},{5,4},{6,7},{7,6},{8,9},{9,8},{10,11... | collective-permute-start | bytes 1966088 | tf_op jit(solution)/shard_map/ppermute | solution.py:42
  34.7 3.5 %collective-permute-start.11 = (bf16[256,1280]{1,0:T(8,128)(2,1)S(1)}, bf16[256,1280]{1,0:T(8,128)(2,1)S(1)}, u32[]{:S(2)}, u32[]{:S(2)}) collective-permute-start(bf16[256,1280]{1,0:T(8,128)(2,1)S(1)} %collective-permute-done.3.refs_3_.refs_11_), channel_id=1, source_target_pairs={{0,1},{1,0},{2,3},{3,2},{4,5},{5,4},{6,7},{7,6},{8,9},{9,8},{10,11... | collective-permute-start | bytes 1966088 | tf_op jit(solution)/shard_map/ppermute | solution.py:42
  35.3 10.6 %collective-permute-start.7 = (bf16[256,1280]{1,0:T(8,128)(2,1)S(1)}, bf16[256,1280]{1,0:T(8,128)(2,1)S(1)}, u32[]{:S(2)}, u32[]{:S(2)}) collective-permute-start(bf16[256,1280]{1,0:T(8,128)(2,1)S(1)} %collective-permute-done.2.refs_2_.refs_10_), channel_id=1, source_target_pairs={{0,32},{1,49},{2,34},{3,51},{4,36},{5,53},{6,38},{7,55},{8,40},{9,... | collective-permute-start | bytes 1966088 | tf_op jit(solution)/shard_map/ppermute | solution.py:42
  35.3 10.9 %collective-permute-start.8 = (bf16[256,1280]{1,0:T(8,128)(2,1)S(1)}, bf16[256,1280]{1,0:T(8,128)(2,1)S(1)}, u32[]{:S(2)}, u32[]{:S(2)}) collective-permute-start(bf16[256,1280]{1,0:T(8,128)(2,1)S(1)} %collective-permute-done.3.refs_3_.refs_11_), channel_id=1, source_target_pairs={{0,2},{1,15},{2,0},{3,5},{4,6},{5,3},{6,4},{7,9},{8,10},{9,7},{10,... | collective-permute-start | bytes 1966088 | tf_op jit(solution)/shard_map/ppermute | solution.py:42
  46.2 2.1 %collective-permute-start.13 = (bf16[256,1280]{1,0:T(8,128)(2,1)S(1)}, bf16[256,1280]{1,0:T(8,128)(2,1)S(1)}, u32[]{:S(2)}, u32[]{:S(2)}) collective-permute-start(bf16[256,1280]{1,0:T(8,128)(2,1)S(1)} %collective-permute-done.7.refs_7_.refs_16_), channel_id=1, source_target_pairs={{0,1},{1,0},{2,3},{3,2},{4,5},{5,4},{6,7},{7,6},{8,9},{9,8},{10,11... | collective-permute-start | bytes 1966088 | tf_op jit(solution)/shard_map/ppermute | solution.py:42
  46.2 3.0 %collective-permute-start.14 = (bf16[256,1280]{1,0:T(8,128)(2,1)S(1)}, bf16[256,1280]{1,0:T(8,128)(2,1)S(1)}, u32[]{:S(2)}, u32[]{:S(2)}) collective-permute-start(bf16[256,1280]{1,0:T(8,128)(2,1)S(1)} %collective-permute-done.8.refs_8_.refs_17_), channel_id=1, source_target_pairs={{0,1},{1,0},{2,3},{3,2},{4,5},{5,4},{6,7},{7,6},{8,9},{9,8},{10,11... | collective-permute-start | bytes 1966088 | tf_op jit(solution)/shard_map/ppermute | solution.py:42
  46.7 9.9 %collective-permute-start.1 = (bf16[2048,256]{1,0:T(8,128)(2,1)S(1)}, bf16[2048,256]{1,0:T(8,128)(2,1)S(1)}, u32[]{:S(2)}, u32[]{:S(2)}) collective-permute-start(bf16[2048,256]{1,0:T(8,128)(2,1)S(1)} %get-tuple-element.43), channel_id=1, source_target_pairs={{0,1},{1,0},{2,3},{3,2},{4,5},{5,4},{6,7},{7,6},{8,9},{9,8},{10,11... | collective-permute-start | bytes 3145736 | tf_op jit(solution)/shard_map/ppermute | solution.py:42
  54.0 2.1 %collective-permute-start.15 = (bf16[256,640]{1,0:T(8,128)(2,1)S(1)}, bf16[256,640]{1,0:T(8,128)(2,1)S(1)}, u32[]{:S(2)}, u32[]{:S(2)}) collective-permute-start(bf16[256,640]{1,0:T(8,128)(2,1)S(1)} %get-tuple-element.52.refs_3_.refs_1_), channel_id=1, source_target_pairs={{0,1},{1,0},{2,3},{3,2},{4,5},{5,4},{6,7},{7,6},{8,9},{9,8},{10,11... | collective-permute-start | bytes 983048 | tf_op jit(solution)/shard_map/ppermute | solution.py:42
  56.1 3.6 %collective-permute-start.17 = (bf16[256,640]{1,0:T(8,128)(2,1)S(1)}, bf16[256,640]{1,0:T(8,128)(2,1)S(1)}, u32[]{:S(2)}, u32[]{:S(2)}) collective-permute-start(bf16[256,640]{1,0:T(8,128)(2,1)S(1)} %attend_high.1.refs_3_.refs_2_), channel_id=1, source_target_pairs={{0,1},{1,0},{2,3},{3,2},{4,5},{5,4},{6,7},{7,6},{8,9},{9,8},{10,11... | collective-permute-start | bytes 983048 | tf_op jit(solution)/shard_map/ppermute | solution.py:42
  58.1 6.1 %copy-start.1 = (bf16[256,4096]{1,0:T(8,128)(2,1)S(1)}, bf16[256,4096]{1,0:T(8,128)(2,1)}, u32[]{:S(2)}) copy-start(bf16[256,4096]{1,0:T(8,128)(2,1)} %refs_3_.3) | copy-start | bytes 6291460
  58.1 17.8 %collective-permute-start.16 = (bf16[8,128,640]{2,1,0:T(8,128)(2,1)S(1)}, bf16[8,128,640]{2,1,0:T(8,128)(2,1)S(1)}, u32[]{:S(2)}, u32[]{:S(2)}) collective-permute-start(bf16[8,128,640]{2,1,0:T(8,128)(2,1)S(1)} %terms.4), channel_id=1, source_target_pairs={{0,64},{1,193},{2,66},{3,195},{4,68},{5,197},{6,70},{7,199},{8,72}... | collective-permute-start | bytes 3932168 | tf_op jit(solution)/shard_map/ppermute | solution.py:42
  61.3 18.0 %collective-permute-start.18 = (bf16[8,128,640]{2,1,0:T(8,128)(2,1)S(1)}, bf16[8,128,640]{2,1,0:T(8,128)(2,1)S(1)}, u32[]{:S(2)}, u32[]{:S(2)}) collective-permute-start(bf16[8,128,640]{2,1,0:T(8,128)(2,1)S(1)} %terms.5), channel_id=1, source_target_pairs={{0,32},{1,49},{2,34},{3,51},{4,36},{5,53},{6,38},{7,55},{8,40},{9,... | collective-permute-start | bytes 3932168 | tf_op jit(solution)/shard_map/ppermute | solution.py:42
  80.8 9.8 %collective-permute-start.19 = (bf16[4,128,640]{2,1,0:T(8,128)(2,1)S(1)}, bf16[4,128,640]{2,1,0:T(8,128)(2,1)S(1)}, u32[]{:S(2)}, u32[]{:S(2)}) collective-permute-start(bf16[4,128,640]{2,1,0:T(8,128)(2,1)S(1)} %get-tuple-element.62), channel_id=1, source_target_pairs={{0,192},{1,65},{2,194},{3,67},{4,196},{5,69},{6,198},{7,71},{8,200... | collective-permute-start | bytes 1966088 | tf_op jit(solution)/shard_map/ppermute | solution.py:42
  82.4 11.1 %collective-permute-start.22 = (bf16[4,128,640]{2,1,0:T(8,128)(2,1)S(1)}, bf16[4,128,640]{2,1,0:T(8,128)(2,1)S(1)}, u32[]{:S(2)}, u32[]{:S(2)}) collective-permute-start(bf16[4,128,640]{2,1,0:T(8,128)(2,1)S(1)} %get-tuple-element.69), channel_id=1, source_target_pairs={{0,48},{1,33},{2,50},{3,35},{4,52},{5,37},{6,54},{7,39},{8,56},{9,... | collective-permute-start | bytes 1966088 | tf_op jit(solution)/shard_map/ppermute | solution.py:42
  90.7 7.6 %collective-permute-start.20 = (bf16[2,128,640]{2,1,0:T(8,128)(2,1)S(1)}, bf16[2,128,640]{2,1,0:T(8,128)(2,1)S(1)}, u32[]{:S(2)}, u32[]{:S(2)}) collective-permute-start(bf16[2,128,640]{2,1,0:T(8,128)(2,1)S(1)} %get-tuple-element.64), channel_id=1, source_target_pairs={{0,32},{1,49},{2,34},{3,51},{4,36},{5,53},{6,38},{7,55},{8,40},{9,... | collective-permute-start | bytes 983048 | tf_op jit(solution)/shard_map/ppermute | solution.py:42
  93.6 7.2 %collective-permute-start.23 = (bf16[2,128,640]{2,1,0:T(8,128)(2,1)S(1)}, bf16[2,128,640]{2,1,0:T(8,128)(2,1)S(1)}, u32[]{:S(2)}, u32[]{:S(2)}) collective-permute-start(bf16[2,128,640]{2,1,0:T(8,128)(2,1)S(1)} %get-tuple-element.71), channel_id=1, source_target_pairs={{0,64},{1,193},{2,66},{3,195},{4,68},{5,197},{6,70},{7,199},{8,72}... | collective-permute-start | bytes 983048 | tf_op jit(solution)/shard_map/ppermute | solution.py:42
  98.5 4.4 %collective-permute-start.21 = (bf16[1,128,640]{2,1,0:T(8,128)(2,1)S(1)}, bf16[1,128,640]{2,1,0:T(8,128)(2,1)S(1)}, u32[]{:S(2)}, u32[]{:S(2)}) collective-permute-start(bf16[1,128,640]{2,1,0:T(8,128)(2,1)S(1)} %get-tuple-element.66), channel_id=1, source_target_pairs={{0,48},{1,33},{2,50},{3,35},{4,52},{5,37},{6,54},{7,39},{8,56},{9,... | collective-permute-start | bytes 491528 | tf_op jit(solution)/shard_map/ppermute | solution.py:42
  100.9 4.6 %collective-permute-start.24 = (bf16[1,128,640]{2,1,0:T(8,128)(2,1)S(1)}, bf16[1,128,640]{2,1,0:T(8,128)(2,1)S(1)}, u32[]{:S(2)}, u32[]{:S(2)}) collective-permute-start(bf16[1,128,640]{2,1,0:T(8,128)(2,1)S(1)} %get-tuple-element.73), channel_id=1, source_target_pairs={{0,192},{1,65},{2,194},{3,67},{4,196},{5,69},{6,198},{7,71},{8,200... | collective-permute-start | bytes 491528 | tf_op jit(solution)/shard_map/ppermute | solution.py:42
  137.3 19.7 %collective-permute-start.25 = (bf16[16,16,1280]{2,1,0:T(8,128)(2,1)S(1)}, bf16[16,16,1280]{2,1,0:T(8,128)(2,1)S(1)}, u32[]{:S(2)}, u32[]{:S(2)}) collective-permute-start(bf16[16,16,1280]{2,1,0:T(8,128)(2,1)S(1)} %all_to_all.16.got.mine), channel_id=1, source_target_pairs={{0,1},{1,0},{2,3},{3,2},{4,5},{5,4},{6,7},{7,6},{8,9},{9,8},{10,11... | collective-permute-start | bytes 1966088 | tf_op jit(solution)/shard_map/ppermute | solution.py:42
  (1 other events, 1.6 us)

commit v2 on v1

v2 whole, which is shorter than its diff:
```python
import jax
import jax.numpy as jnp
import numpy as np
from jax import lax
from jax.experimental import pallas as pl
from jax.experimental.pallas import tpu as pltpu
from jax.sharding import Mesh
from jax.sharding import PartitionSpec as P

D = 4096
HD = 128
QH = 8
QKV = 1280
TOK = 256
BLK = D // 8
HALF = BLK // 2
QUART = HALF // 2
PIECE = QUART // 8
COLS = QKV // 2
OUTW = QH * HD
LOW = COLS // HD

AXES = ("x", "y_lo", "y_hi", "z", "core")
SIZES = (4, 2, 2, 8, 2)
target_rms = 0.5
rope_base = 500000.0
F32 = jnp.float32
BF16 = jnp.bfloat16


def flat(x, y, z, c):
    return (x * 2 + y % 2) * 32 + (y // 2) * 16 + z * 2 + c


def swap(value, partner):
    pairs = []
    for x in range(4):
        for y in range(4):
            for z in range(8):
                for c in range(2):
                    pairs.append((flat(x, y, z, c), flat(*partner(x, y, z, c))))
    return lax.ppermute(value, AXES, pairs)


def near(c):
    return 1 if c == 0 else 3


def other_core(x, y, z, c):
    return x, y, z, 1 - c


def gather_x1(x, y, z, c):
    return x ^ near(c ^ (z & 1)), y, z, c


def gather_x2(x, y, z, c):
    return x ^ (4 - near(c ^ (z & 1))), y, z, c


def flip_y(x, y, z, c):
    return x, y ^ near(c), z, c


def pair_z(x, y, z, c):
    return x, y, (z ^ 1) if c == 0 else ((z + 1) % 8 if z % 2 else (z - 1) % 8), c


def x_1(x, y, z, c):
    return x ^ near(c), y, z, c


def x_2(x, y, z, c):
    return x ^ (4 - near(c)), y, z, c


def y_1(x, y, z, c):
    return x, y ^ near(c), z, c


def y_2(x, y, z, c):
    return x, y ^ (4 - near(c)), z, c


VM = pl.BlockSpec(memory_space=pltpu.VMEM)
SM = pl.BlockSpec(memory_space=pltpu.SMEM)


def dot(a, b, dims):
    return lax.dot_general(a, b, (dims, ((), ())), preferred_element_type=F32)


def where():
    x, y_lo, y_hi, z, c = (lax.axis_index(axis) for axis in AXES)
    return x, y_hi * 2 + y_lo, z, c


def aligned(start, size):
    return pl.ds(pl.multiple_of(start, size), size)


def norm_body(tokens, scale_r, own, send_low, send_high):
    full = tokens[...].astype(F32)
    r = lax.rsqrt(jnp.sum(full * full, axis=1, keepdims=True) * (1.0 / D) + 1e-05)
    scale_r[...] = r
    c = lax.axis_index("core")
    for b in range(8):
        here = slice(b * HALF, (b + 1) * HALF)
        for side in (c, 1 - c):
            part = (tokens[:, aligned(b * BLK + side * HALF, HALF)].astype(F32) * r).astype(BF16)
            if side is c:
                own[:, here] = part
            else:
                send_low[:, here] = part[: TOK // 2]
                send_high[:, here] = part[TOK // 2 :]


def norm(tokens):
    half = jax.ShapeDtypeStruct((TOK, D // 2), BF16)
    quarter = jax.ShapeDtypeStruct((TOK // 2, D // 2), BF16)
    return pl.pallas_call(
        norm_body,
        out_shape=(jax.ShapeDtypeStruct((TOK, 1), F32), half, quarter, quarter),
        in_specs=[VM],
        out_specs=(VM,) * 4,
        compiler_params=pltpu.CompilerParams(vmem_limit_bytes=12 << 20),
        cost_estimate=pl.CostEstimate(flops=10 * TOK * D, bytes_accessed=4 << 20, transcendentals=0),
        name="norm",
    )(tokens)


def transpose_body(own, low, high, out):
    for b in range(8):
        cols = slice(b * HALF, (b + 1) * HALF)
        out[cols, :TOK] = own[:, cols].T
        out[cols, TOK:] = jnp.concatenate([low[:, cols], high[:, cols]], axis=0).T


def transpose(own, low, high):
    return pl.pallas_call(
        transpose_body,
        out_shape=jax.ShapeDtypeStruct((D // 2, 2 * TOK), BF16),
        in_specs=[VM] * 3,
        out_specs=VM,
        compiler_params=pltpu.CompilerParams(vmem_limit_bytes=6 << 20),
        cost_estimate=pl.CostEstimate(flops=4 * TOK * D, bytes_accessed=4 << 20, transcendentals=0),
        name="transpose",
    )(own, low, high)


def block(name, flip):
    x, y, z, c = where()
    turned = c ^ (z & 1)
    step = {"0": 0, "a": 1 + 2 * turned, "b": 3 - 2 * turned, "o": 2}[name]
    return (x ^ step) * 2 + ((y & 1) ^ flip)


def product(spots, feats, pieces):
    cols = [aligned(block(*spot) * HALF, HALF) for spot in spots]
    lhs = jnp.concatenate([jnp.concatenate([ref[:, k] for k in cols], axis=1) for ref in feats], axis=0)
    return dot(lhs, jnp.concatenate([p[...] for p in pieces], axis=0), ((1,), (0,)))


def part_body(spots, own, low, high, *refs):
    count = len(spots)
    pieces, old, outs = refs[:count], refs[count:-2], refs[-2:]
    part = product(spots, (own, low, high), pieces)
    for k, half in enumerate((part[:TOK], part[TOK:])):
        outs[k][...] = half + old[k][...] if old else half


def project(spots, feats, pieces, *old):
    count, out = len(pieces), jax.ShapeDtypeStruct((TOK, QKV), F32)
    return pl.pallas_call(
        lambda *refs: part_body(spots, *refs),
        out_shape=(out, out),
        in_specs=[VM] * (3 + count + len(old)),
        out_specs=(VM, VM),
        compiler_params=pltpu.CompilerParams(vmem_limit_bytes=12 << 20),
        cost_estimate=pl.CostEstimate(
            flops=4 * TOK * HALF * count * QKV, bytes_accessed=6 << 20, transcendentals=0
        ),
        name="project",
    )(*feats, *pieces, *old)


def late_body(spots, count, *refs):
    feats, pieces, old, out = refs[:count], refs[count:-2], refs[-2], refs[-1]
    out[...] = (old[...] + product(spots, feats, pieces)).astype(out.dtype)


def project_late(spots, feats, pieces, old, dtype):
    count = len(feats)
    return pl.pallas_call(
        lambda *refs: late_body(spots, count, *refs),
        out_shape=jax.ShapeDtypeStruct((TOK, QKV), dtype),
        in_specs=[VM] * (1 + count + len(pieces)),
        out_specs=VM,
        compiler_params=pltpu.CompilerParams(vmem_limit_bytes=8 << 20),
        cost_estimate=pl.CostEstimate(
            flops=2 * TOK * HALF * len(pieces) * QKV, bytes_accessed=4 << 20, transcendentals=0
        ),
        name="project_late",
    )(*feats, *pieces, old)


def visible(doc):
    rows = lax.broadcasted_iota(jnp.int32, (TOK, TOK), 0)
    cols = lax.broadcasted_iota(jnp.int32, (TOK, TOK), 1)
    along = jnp.broadcast_to(doc[...], (TOK, TOK))
    return (cols <= rows) & (along == along.T)


def turn(value, cos, sin):
    return value * cos + pltpu.roll(value, HD // 2, 1) * sin


def head_grads(q_rot, g, k_rot, val, seen, cos, sin):
    scale = HD**-0.5
    scores = jnp.where(seen, dot(q_rot, k_rot, ((1,), (1,))), -1e30)
    expo = jnp.exp((scores - jnp.max(scores, axis=1, keepdims=True)) * scale)
    probs = expo * (1.0 / jnp.sum(expo, axis=1, keepdims=True))
    d_probs = dot(g, val, ((1,), (1,)))
    delta = jnp.sum(d_probs * probs, axis=1, keepdims=True)
    d_scores = (probs * (d_probs - delta)).astype(BF16)
    d_val = dot(probs.astype(BF16), g, ((0,), (0,)))
    d_key = dot(d_scores, q_rot, ((0,), (0,)))
    d_query = dot(d_scores, k_rot, ((1,), (0,))) * scale
    return turn(d_query, cos, -sin).astype(BF16), d_key, d_val


def attend_low_body(own, came, grad, doc, cosine, sine, out, rest, d_key, d_val, qkv):
    qkv[...] = own[...] + came[...].astype(F32)
    cos, sin = cosine[...], sine[...]
    seen = visible(doc)
    k_rot = turn(qkv[:, OUTW : OUTW + HD], cos, sin).astype(BF16)
    val = qkv[:, OUTW + HD :].astype(BF16)
    total_key, total_val = jnp.zeros((TOK, HD), F32), jnp.zeros((TOK, HD), F32)
    for h in range(QH):
        head = slice(h * HD, (h + 1) * HD)
        q_rot = turn(qkv[:, head], cos, sin).astype(BF16)
        if h < LOW:
            out[:, head], key, value = head_grads(q_rot, grad[:, head], k_rot, val, seen, cos, sin)
            total_key, total_val = total_key + key, total_val + value
        else:
            rest[:, (h - LOW) * HD : (h - LOW + 1) * HD] = q_rot
    rest[:, COLS - 2 * HD : COLS - HD] = k_rot
    rest[:, COLS - HD :] = val
    d_key[...] = total_key
    d_val[...] = total_val


def attend_high_body(rest, key_low, val_low, grad, doc, cosine, sine, out):
    cos, sin = cosine[...], sine[...]
    seen = visible(doc)
    k_rot, val = rest[:, COLS - 2 * HD : COLS - HD], rest[:, COLS - HD :]
    total_key, total_val = key_low[...], val_low[...]
    for h in range(LOW, QH):
        here = slice((h - LOW) * HD, (h - LOW + 1) * HD)
        g = grad[:, h * HD : (h + 1) * HD]
        out[:, here], key, value = head_grads(rest[:, here], g, k_rot, val, seen, cos, sin)
        total_key, total_val = total_key + key, total_val + value
    out[:, COLS - 2 * HD : COLS - HD] = turn(total_key * HD**-0.5, cos, -sin).astype(BF16)
    out[:, COLS - HD :] = total_val.astype(BF16)


def attend_cost(heads):
    return pl.CostEstimate(
        flops=10 * TOK * TOK * HD * heads, bytes_accessed=4 << 20, transcendentals=TOK * TOK * heads
    )


def attend_low(own, came, grad, doc):
    wide, half = jax.ShapeDtypeStruct((TOK, COLS), BF16), jax.ShapeDtypeStruct((TOK, HD), F32)
    return pl.pallas_call(
        attend_low_body,
        out_shape=(wide, wide, half, half),
        in_specs=[VM] * 6,
        out_specs=(VM,) * 4,
        scratch_shapes=[pltpu.VMEM((TOK, QKV), F32)],
        compiler_params=pltpu.CompilerParams(vmem_limit_bytes=12 << 20),
        cost_estimate=attend_cost(LOW),
        name="attend_low",
    )(own, came, grad, doc, *TABLES)


def attend_high(rest, d_key, d_val, grad, doc):
    return pl.pallas_call(
        attend_high_body,
        out_shape=jax.ShapeDtypeStruct((TOK, COLS), BF16),
        in_specs=[VM] * 7,
        out_specs=VM,
        compiler_params=pltpu.CompilerParams(vmem_limit_bytes=12 << 20),
        cost_estimate=attend_cost(QH - LOW),
        name="attend_high",
    )(rest, d_key, d_val, grad, doc, *TABLES)


def normed_body(spots, low, low_other, high, high_other, *refs):
    pieces, own, send = refs[: len(spots)], refs[-2], refs[-1]
    for lower, higher, out in ((low_other, high_other, send), (low, high, own)):
        d_qkv = jnp.concatenate([lower[...], higher[...]], axis=1)
        for spot, piece in zip(spots, pieces):
            part = dot(d_qkv, piece[...], ((1,), (1,)))
            out[:, aligned(block(*spot) * HALF, HALF)] = part.astype(out.dtype)


def normed_grad(spots, grads, pieces):
    count = len(pieces)
    return pl.pallas_call(
        lambda *refs: normed_body(spots, *refs),
        out_shape=(
            jax.ShapeDtypeStruct((TOK, D // 2), F32),
            jax.ShapeDtypeStruct((TOK, D // 2), BF16),
        ),
        in_specs=[VM] * (4 + count),
        out_specs=(VM, VM),
        compiler_params=pltpu.CompilerParams(vmem_limit_bytes=12 << 20),
        cost_estimate=pl.CostEstimate(flops=2 * TOK * D * QKV, bytes_accessed=8 << 20, transcendentals=0),
        name="normed_grad",
    )(*grads, *pieces)


def tokens_body(own, came, tokens, scale_r, out):
    c = lax.axis_index("core")
    places = [
        (aligned(b * BLK + side * HALF, HALF), ref, slice(b * HALF, (b + 1) * HALF))
        for b in range(8)
        for side, ref in ((c, own), (1 - c, came))
    ]
    total = jnp.zeros((TOK, HALF), F32)
    for cols, ref, here in places:
        total = total + ref[:, here].astype(F32) * tokens[:, cols].astype(F32)
    r = scale_r[...]
    back = r * r * r * (jnp.sum(total, axis=1, keepdims=True) * (1.0 / D))
    for cols, ref, here in places:
        out[:, cols] = (r * ref[:, here].astype(F32) - tokens[:, cols].astype(F32) * back).astype(BF16)


def tokens_grad(own, came, tokens, scale_r):
    return pl.pallas_call(
        tokens_body,
        out_shape=jax.ShapeDtypeStruct((TOK, D), BF16),
        in_specs=[VM] * 4,
        out_specs=VM,
        compiler_params=pltpu.CompilerParams(vmem_limit_bytes=8 << 20),
        cost_estimate=pl.CostEstimate(flops=10 * TOK * D, bytes_accessed=8 << 20, transcendentals=0),
        name="tokens_grad",
    )(own, came, tokens, scale_r)


def term_product(along_x, level, feats, d_own, d_other):
    x, y, z, c = where()
    order = (0, 3 - 2 * c, 1 + 2 * c, 2)
    rows = []
    for first in (2 * level, 2 * level + 1):
        for second in range(4):
            i, j = (first, second) if along_x else (second, first)
            yy = y ^ order[j]
            start = ((x ^ order[i]) * 2 + (yy & 1)) * HALF + (yy >> 1) * QUART
            rows.append(feats[aligned(start, QUART), :])
    right = jnp.concatenate([d_own[...], d_other[...]], axis=0)
    return dot(jnp.concatenate(rows, axis=0), right, ((1,), (0,))).reshape(8, QUART, COLS)


def term_body(along_x, feats, d_own, d_other, out):
    out[...] = term_product(along_x, 1, feats, d_own, d_other).astype(BF16)


def term_add_body(along_x, feats, d_own, d_other, came, kept, sent):
    part = term_product(along_x, 0, feats, d_own, d_other)
    part = (part + came[...].astype(F32)).astype(BF16)
    kept[...] = part[:4]
    sent[...] = part[4:]


def terms(along_x, made, *came):
    if came:
        half = jax.ShapeDtypeStruct((4, QUART, COLS), BF16)
        body, out_shape, out_specs = term_add_body, (half, half), (VM, VM)
    else:
        out_shape, out_specs = jax.ShapeDtypeStruct((8, QUART, COLS), BF16), VM
        body = term_body
    return pl.pallas_call(
        lambda *refs: body(along_x, *refs),
        out_shape=out_shape,
        in_specs=[VM] * (3 + len(came)),
        out_specs=out_specs,
        compiler_params=pltpu.CompilerParams(vmem_limit_bytes=12 << 20),
        cost_estimate=pl.CostEstimate(
            flops=2 * 8 * QUART * COLS * 2 * TOK, bytes_accessed=4 << 20, transcendentals=0
        ),
        name="terms",
    )(*made, *came)


def split_body(count, old, came, kept, sent):
    part = (old[...].astype(F32) + came[...].astype(F32)).astype(BF16)
    kept[...] = part[: count // 2]
    sent[...] = part[count // 2 :]


def split(old, came):
    count = old.shape[0]
    half = jax.ShapeDtypeStruct((count // 2, QUART, COLS), BF16)
    return pl.pallas_call(
        lambda *refs: split_body(count, *refs),
        out_shape=(half, half),
        in_specs=[VM, VM],
        out_specs=(VM, VM),
        compiler_params=pltpu.CompilerParams(vmem_limit_bytes=6 << 20),
        name="split",
    )(old, came)


def join_body(old_x, came_x, old_y, came_y, out):
    out[:, :, :COLS] = (old_x[...].astype(F32) + came_x[...].astype(F32)).astype(BF16).reshape(8, PIECE, COLS)
    out[:, :, COLS:] = (old_y[...].astype(F32) + came_y[...].astype(F32)).astype(BF16).reshape(8, PIECE, COLS)


def join(*parts):
    return pl.pallas_call(
        join_body,
        out_shape=jax.ShapeDtypeStruct((8, PIECE, QKV), BF16),
        in_specs=[VM] * 4,
        out_specs=VM,
        compiler_params=pltpu.CompilerParams(vmem_limit_bytes=4 << 20),
        name="join",
    )(*parts)


def finish_body(parts, out):
    total = sum(parts[i].astype(F32) for i in range(8)).astype(BF16)
    for i in range(16):
        out[i] = total


def finish(parts):
    return pl.pallas_call(
        finish_body,
        out_shape=jax.ShapeDtypeStruct((16, PIECE, QKV), BF16),
        in_specs=[VM],
        out_specs=VM,
        compiler_params=pltpu.CompilerParams(vmem_limit_bytes=4 << 20),
        name="finish",
    )(parts)


def squares_body(got, out):
    total = jnp.zeros((PIECE, QKV), F32)
    for i in range(16):
        value = got[i].astype(F32)
        total = total + value * value
    total = jnp.sum(jnp.sum(total, axis=1, keepdims=True), axis=0, keepdims=True)
    out[...] = jnp.broadcast_to(total.reshape(1, 1, 1), (16, 8, 128))


def squares(got):
    return pl.pallas_call(
        squares_body,
        out_shape=jax.ShapeDtypeStruct((16, 8, 128), F32),
        in_specs=[VM],
        out_specs=VM,
        compiler_params=pltpu.CompilerParams(vmem_limit_bytes=4 << 20),
        name="squares",
    )(got)


def rescale_body(parts, mine, theirs, out):
    total = sum(parts[i] for i in range(16))
    factor = (target_rms * lax.rsqrt(total * (1.0 / (D * QKV)) + 1e-06))[:1, :1]
    c = lax.axis_index("core")
    for side, half in ((c, mine), (1 - c, theirs)):
        out[aligned(side * HALF, HALF), :] = (half[...].reshape(HALF, QKV).astype(F32) * factor).astype(BF16)


def rescale(parts, mine, theirs):
    return pl.pallas_call(
        rescale_body,
        out_shape=jax.ShapeDtypeStruct((BLK, QKV), BF16),
        in_specs=[VM] * 3,
        out_specs=VM,
        compiler_params=pltpu.CompilerParams(vmem_limit_bytes=8 << 20),
        name="rescale",
    )(parts, mine, theirs)


def tables():
    freq = np.exp(-np.log(rope_base) * 2.0 * np.arange(HD // 2) / HD)
    angle = np.arange(TOK)[:, None] * freq[None, :]
    cos, sin = np.cos(angle), np.sin(angle)
    return np.concatenate([cos, cos], 1).astype(np.float32), np.concatenate([-sin, sin], 1).astype(np.float32)


TABLES = tables()

def on_device(tokens, grad_attended, doc_ids, w_own):
    w00 = lax.dynamic_slice_in_dim(w_own, lax.axis_index("core") * HALF, HALF, 0)
    w00, tokens = lax.optimization_barrier((w00, tokens))
    wa0 = swap(w00, gather_x1)
    w01 = swap(w00, flip_y)
    scale_r, own, send_low, send_high = norm(tokens)
    other = [swap(send, other_core) for send in (send_low, send_high)]
    wa0, w01, own, other = lax.optimization_barrier((wa0, w01, own, other))
    both = (own, *other)
    wo0 = swap(wa0, gather_x2)
    wa1 = swap(wa0, flip_y)
    wb0 = swap(wa0, pair_z)
    early, early_spots = [w00, w01, wa0], [("0", 0), ("0", 1), ("a", 0)]
    part_own, part_other = project(early_spots, both, early)
    feats = transpose(*both)
    wo0, wa1, part_own, part_other, feats = lax.optimization_barrier((wo0, wa1, part_own, part_other, feats))
    wo1 = swap(wo0, flip_y)
    wb1 = swap(wa1, pair_z)
    middle, middle_spots = [wo0, wa1, wb0], [("o", 0), ("a", 1), ("b", 0)]
    part_own, part_other = project(middle_spots, both, middle, part_own, part_other)
    wo1, wb1, part_own, part_other = lax.optimization_barrier((wo1, wb1, part_own, part_other))
    late, late_spots = [wo1, wb1], [("o", 1), ("b", 1)]
    late_other = project_late(late_spots, other, late, part_other, BF16)
    came = swap(late_other, other_core)
    late_other, part_own = lax.optimization_barrier((late_other, part_own))
    qkv = project_late(late_spots, [own], late, part_own, F32)
    d_low, rest, d_key, d_val = attend_low(qkv, came, grad_attended, doc_ids)

    low_other = swap(d_low, other_core)
    d_high = attend_high(rest, d_key, d_val, grad_attended, doc_ids)
    low_other, d_high = lax.optimization_barrier((low_other, d_high))
    high_other = swap(d_high, other_core)
    lows, highs = (feats, d_low, low_other), (feats, d_high, high_other)
    came_x = swap(terms(True, lows), x_1)
    sent_y = terms(False, highs)
    came_y = swap(sent_y, y_1)
    spots, pieces = early_spots + middle_spots + late_spots, early + middle + late
    sent_y, d_low, low_other, d_high, high_other = lax.optimization_barrier(
        (sent_y, d_low, low_other, d_high, high_other)
    )
    normed_own, normed_send = normed_grad(spots, (d_low, low_other, d_high, high_other), pieces)
    normed_came = swap(normed_send, other_core)
    came_x, normed_own = lax.optimization_barrier((came_x, normed_own))
    sum_x, sent_x = terms(True, lows, came_x)
    came_x = swap(sent_x, x_2)
    sum_y, sent_y = terms(False, highs, came_y)
    came_y = swap(sent_y, y_2)
    sent_y, normed_came = lax.optimization_barrier((sent_y, normed_came))
    d_tokens = tokens_grad(normed_own, normed_came, tokens, scale_r)
    came_x, d_tokens = lax.optimization_barrier((came_x, d_tokens))
    for step_x, step_y in ((y_1, x_1), (y_2, x_2)):
        sum_x, sent_x = split(sum_x, came_x)
        came_x = swap(sent_x, step_x)
        sum_y, sent_y = split(sum_y, came_y)
        came_y = swap(sent_y, step_y)

    total = join(sum_x, came_x, sum_y, came_y)
    got = finish(lax.all_to_all(total, "z", 0, 0))
    got = lax.all_to_all(got, ("y_hi", "z"), 0, 0)

    theirs = swap(got, other_core)
    parts = lax.all_to_all(squares(got), ("x", "y_lo", "core"), 0, 0)
    return d_tokens, rescale(parts, got, theirs)


def solution(mesh):
    mesh = Mesh(mesh.devices.reshape(SIZES), AXES)
    spread, rows = P(AXES, None), P(AXES[:2], None)
    return jax.shard_map(
        on_device,
        mesh=mesh,
        in_specs=(spread, spread, spread, rows),
        out_specs=(spread, rows),
        check_vma=False,
    )
```

time: 159 us -> 150 us (0.943)
  Pallas kernels: 26.8 us -> 22.3 us
  waiting for transfers between devices: 46.5 us -> 42.8 us
    pallas_call x9 -> x13, Pallas kernels: 22.1 us -> 18.1 us  [the longest x4 3.91 us: terms(): pl.pallas_call(lambda *refs: body(along_x, *refs), out_shape=out_shape, i...]
    ppermute x26 -> x22, waiting for transfers between devices: 46.5 us -> 42.8 us  [swap(): return lax.ppermute(value, AXES, pairs)]
    all_to_all x1, blocking collectives: 14.1 us -> 16 us  [on_device(): got = finish(lax.all_to_all(total, 'z', 0, 0))]
    ppermute x26 -> x22, starting transfers between devices: 39.8 us -> 39 us  [swap(): return lax.ppermute(value, AXES, pairs)]
  transfers between devices with their start and end apart: 26 -> 22, of which waited for: 15 -> 16; matrix products, arithmetic and copies ran while one was open for 0% -> 0% of each run, Pallas kernels for 15% -> 11%
where the time goes in v2:
time: 150 us
  waiting for transfers between devices  42.8 us (29%)
  blocking collectives  41.6 us (28%)
  starting transfers between devices  39 us (26%)
  Pallas kernels  22.3 us (15%)
  local copies, waits for them, and re-layouts  2.98 us (2%)
    ppermute x22, waiting for transfers between devices, swap(): return lax.ppermute(value, AXES, pairs)  42.8 us
    ppermute x22, starting transfers between devices, swap(): return lax.ppermute(value, AXES, pairs)  39 us
    all_to_all x1, blocking collectives, on_device(): got = lax.all_to_all(got, ('y_hi', 'z'), 0, 0)  17 us
    all_to_all x1, blocking collectives, on_device(): got = finish(lax.all_to_all(total, 'z', 0, 0))  16 us
    all_to_all x1, blocking collectives, on_device(): parts = lax.all_to_all(squares(got), ('x', 'y_lo', 'core'), 0, 0)  8.71 us
    pallas_call x4, Pallas kernels, terms(): pl.pallas_call(lambda *refs: body(along_x, *refs), out_shape=out_shape, i...  3.91 us
    pallas_call x1, Pallas kernels, attend_low(): pl.pallas_call(attend_low_body, out_shape=(wide, wide, half, half), in_sp...  3.38 us
  transfers between devices with their start and end apart: 22, of which 16 were waited for; matrix products, arithmetic and copies ran while one was open for 0% of the time, Pallas kernels for 11%

profile of v2, /device:TPU:1, one launch (start us, length us, event | category | flops | bytes accessed | tf_op | source)
XLA Modules:
  0.0 149.6 jit_solution(9487330773920342469)
XLA Ops:
  0.6 1.3 copy-done
  2.0 3.7 %collective-permute-start.1 = (bf16[256,1280]{1,0:T(8,128)(2,1)S(1)}, bf16[256,1280]{1,0:T(8,128)(2,1)S(1)}, u32[]{:S(2)}, u32[]{:S(2)}) collective-permute-start(bf16[256,1280]{1,0:T(8,128)(2,1)S(1)} %constant_dynamic-slice_fusion.refs_3_.refs_4_), channel_id=1, source_target_pairs={{0,32},{1,49},{2,34},{3,51},{4,36},{5,53},{6,38},{7,55},{8,40},{9,... | collective-permute-start | bytes 1966088 | tf_op jit(solution)/shard_map/ppermute | solution.py:42
  5.6 2.5 %collective-permute-start = (bf16[256,1280]{1,0:T(8,128)(2,1)S(1)}, bf16[256,1280]{1,0:T(8,128)(2,1)S(1)}, u32[]{:S(2)}, u32[]{:S(2)}) collective-permute-start(bf16[256,1280]{1,0:T(8,128)(2,1)S(1)} %constant_dynamic-slice_fusion.refs_3_.refs_4_), channel_id=1, source_target_pairs={{0,64},{1,193},{2,194},{3,67},{4,68},{5,197},{6,198},{7,71},{8,72}... | collective-permute-start | bytes 1966088 | tf_op jit(solution)/shard_map/ppermute | solution.py:42
  8.1 1.6 %copy-done.1 = bf16[256,4096]{1,0:T(8,128)(2,1)S(1)} copy-done((bf16[256,4096]{1,0:T(8,128)(2,1)S(1)}, bf16[256,4096]{1,0:T(8,128)(2,1)}, u32[]{:S(2)}) %copy-start.1) | copy-done | bytes 2097176
  11.4 1.4 collective-permute-done.2.refs_1_.low.refs_0_
  13.6 2.7 %collective-permute-done.refs_5_.refs_6_ = bf16[256,1280]{1,0:T(8,128)(2,1)S(1)} collective-permute-done((bf16[256,1280]{1,0:T(8,128)(2,1)S(1)}, bf16[256,1280]{1,0:T(8,128)(2,1)S(1)}, u32[]{:S(2)}, u32[]{:S(2)}) %collective-permute-start) | collective-permute-done | bytes 655392 | tf_op jit(solution)/shard_map/ppermute | solution.py:42
  17.5 7.1 %collective-permute-start.8 = (bf16[256,1280]{1,0:T(8,128)(2,1)S(1)}, bf16[256,1280]{1,0:T(8,128)(2,1)S(1)}, u32[]{:S(2)}, u32[]{:S(2)}) collective-permute-start(bf16[256,1280]{1,0:T(8,128)(2,1)S(1)} %collective-permute-done.refs_5_.refs_6_), channel_id=1, source_target_pairs={{0,2},{1,15},{2,0},{3,5},{4,6},{5,3},{6,4},{7,9},{8,10},{9,7},{10,... | collective-permute-start | bytes 1966088 | tf_op jit(solution)/shard_map/ppermute | solution.py:42
  27.2 1.5 collective-permute-start.6
  28.7 5.6 %collective-permute-start.7 = (bf16[256,1280]{1,0:T(8,128)(2,1)S(1)}, bf16[256,1280]{1,0:T(8,128)(2,1)S(1)}, u32[]{:S(2)}, u32[]{:S(2)}) collective-permute-start(bf16[256,1280]{1,0:T(8,128)(2,1)S(1)} %collective-permute-done.5.refs_4_.refs_8_), channel_id=1, source_target_pairs={{0,2},{1,15},{2,0},{3,5},{4,6},{5,3},{6,4},{7,9},{8,10},{9,7},{10,... | collective-permute-start | bytes 1966088 | tf_op jit(solution)/shard_map/ppermute | solution.py:42
  35.5 2.4 %collective-permute-done.6.refs_2_.refs_1_.refs_10_ = bf16[256,1280]{1,0:T(8,128)(2,1)S(1)} collective-permute-done((bf16[256,1280]{1,0:T(8,128)(2,1)S(1)}, bf16[256,1280]{1,0:T(8,128)(2,1)S(1)}, u32[]{:S(2)}, u32[]{:S(2)}) %collective-permute-start.6) | collective-permute-done | bytes 655392 | tf_op jit(solution)/shard_map/ppermute | solution.py:42
  37.9 4.4 %collective-permute-done.7.refs_3_.refs_2_.refs_11_ = bf16[256,1280]{1,0:T(8,128)(2,1)S(1)} collective-permute-done((bf16[256,1280]{1,0:T(8,128)(2,1)S(1)}, bf16[256,1280]{1,0:T(8,128)(2,1)S(1)}, u32[]{:S(2)}, u32[]{:S(2)}) %collective-permute-start.7) | collective-permute-done | bytes 655392 | tf_op jit(solution)/shard_map/ppermute | solution.py:42
  43.6 1.6 %collective-permute-done.9.came = bf16[256,1280]{1,0:T(8,128)(2,1)S(1)} collective-permute-done((bf16[256,1280]{1,0:T(8,128)(2,1)S(1)}, bf16[256,1280]{1,0:T(8,128)(2,1)S(1)}, u32[]{:S(2)}, u32[]{:S(2)}) %collective-permute-start.9) | collective-permute-done | bytes 655392 | tf_op jit(solution)/shard_map/ppermute | solution.py:42
  45.2 3.4 %attend_low.1 = (bf16[256,640]{1,0:T(8,128)(2,1)S(1)}, bf16[256,640]{1,0:T(8,128)(2,1)S(1)}, f32[256,128]{1,0:T(8,128)S(1)}, f32[256,128]{1,0:T(8,128)S(1)}) custom-call(f32[256,1280]{1,0:T(8,128)S(1)} %project_late.3.own, bf16[256,1280]{1,0:T(8,128)(2,1)S(1)} %collective-permute-done.9.came, bf16[256,1024]{1,0:T(8,128)(2,1)S(1)} %copy-done.3, ...), custom_call_target="tpu_custom_call" | custom-call | flops 419430400 | bytes 4194304 | tf_op jit(solution)/shard_map/attend_low/pallas_call | solution.py:275
  48.8 1.9 %attend_high.1.refs_1_.refs_2_ = bf16[256,640]{1,0:T(8,128)(2,1)S(1)} custom-call(bf16[256,640]{1,0:T(8,128)(2,1)S(1)} %get-tuple-element.81.rest, f32[256,128]{1,0:T(8,128)S(1)} %get-tuple-element.82.key_low, f32[256,128]{1,0:T(8,128)S(1)} %get-tuple-element.83.val_low, bf16[256,1024]{1,0:T(8,128)(2,1)S(1)} %copy-done.3, s32[1,256]{1,0:T(1,128)S(1)} %copy-done.6, ...), custom_call_target="tpu_custom_call" | custom-call | flops 251658240 | bytes 4194304 | tf_op jit(solution)/shard_map/attend_high/pallas_call | solution.py:288
  52.2 2.6 %collective-permute-start.11 = (bf16[8,128,640]{2,1,0:T(8,128)(2,1)S(1)}, bf16[8,128,640]{2,1,0:T(8,128)(2,1)S(1)}, u32[]{:S(2)}, u32[]{:S(2)}) collective-permute-start(bf16[8,128,640]{2,1,0:T(8,128)(2,1)S(1)} %terms.4), channel_id=1, source_target_pairs={{0,64},{1,193},{2,66},{3,195},{4,68},{5,197},{6,70},{7,199},{8,72}... | collective-permute-start | bytes 3932168 | tf_op jit(solution)/shard_map/ppermute | solution.py:42
  55.7 1.3 collective-permute-start.14
  57.0 3.0 %normed_grad.1 = (f32[256,2048]{1,0:T(8,128)S(1)}, bf16[256,2048]{1,0:T(8,128)(2,1)S(1)}) custom-call(bf16[256,640]{1,0:T(8,128)(2,1)S(1)} %get-tuple-element.86.refs_1_.refs_0_, bf16[256,640]{1,0:T(8,128)(2,1)S(1)} %collective-permute-done.10.refs_2_.refs_1_, bf16[256,640]{1,0:T(8,128)(2,1)S(1)} %attend_high.1.refs_1_.refs_2_, ...), custom_call_target="tpu_custom_call" | custom-call | flops 2684354560 | bytes 8388608 | tf_op jit(solution)/shard_map/normed_grad/pallas_call | solution.py:310
  60.1 9.8 %collective-permute-done.11.refs_3_ = bf16[8,128,640]{2,1,0:T(8,128)(2,1)S(1)} collective-permute-done((bf16[8,128,640]{2,1,0:T(8,128)(2,1)S(1)}, bf16[8,128,640]{2,1,0:T(8,128)(2,1)S(1)}, u32[]{:S(2)}, u32[]{:S(2)}) %collective-permute-start.11) | collective-permute-done | bytes 1310752 | tf_op jit(solution)/shard_map/ppermute | solution.py:42
  71.2 2.2 %collective-permute-done.14.refs_3_ = bf16[8,128,640]{2,1,0:T(8,128)(2,1)S(1)} collective-permute-done((bf16[8,128,640]{2,1,0:T(8,128)(2,1)S(1)}, bf16[8,128,640]{2,1,0:T(8,128)(2,1)S(1)}, u32[]{:S(2)}, u32[]{:S(2)}) %collective-permute-start.14) | collective-permute-done | bytes 1310752 | tf_op jit(solution)/shard_map/ppermute | solution.py:42
  74.6 2.7 %tokens_grad.1 = bf16[256,4096]{1,0:T(8,128)(2,1)} custom-call(f32[256,2048]{1,0:T(8,128)S(1)} %get-tuple-element.93.own, bf16[256,2048]{1,0:T(8,128)(2,1)S(1)} %collective-permute-done.15.came, bf16[256,4096]{1,0:T(8,128)(2,1)S(1)} %copy-done.2, f32[256,1]{1,0:T(8,128)S(1)} %get-tuple-element.97.scale_r), custom_call_target="tpu_custom_call" | custom-call | flops 10485760 | bytes 8388608 | tf_op jit(solution)/shard_map/tokens_grad/pallas_call | solution.py:341
  77.3 3.6 %collective-permute-done.13.refs_1_ = bf16[4,128,640]{2,1,0:T(8,128)(2,1)S(1)} collective-permute-done((bf16[4,128,640]{2,1,0:T(8,128)(2,1)S(1)}, bf16[4,128,640]{2,1,0:T(8,128)(2,1)S(1)}, u32[]{:S(2)}, u32[]{:S(2)}) %collective-permute-start.13) | collective-permute-done | bytes 655392 | tf_op jit(solution)/shard_map/ppermute | solution.py:42
  81.1 1.3 collective-permute-start.16
  82.4 1.9 %collective-permute-done.18.refs_1_ = bf16[4,128,640]{2,1,0:T(8,128)(2,1)S(1)} collective-permute-done((bf16[4,128,640]{2,1,0:T(8,128)(2,1)S(1)}, bf16[4,128,640]{2,1,0:T(8,128)(2,1)S(1)}, u32[]{:S(2)}, u32[]{:S(2)}) %collective-permute-start.18) | collective-permute-done | bytes 655392 | tf_op jit(solution)/shard_map/ppermute | solution.py:42
  85.1 4.6 %collective-permute-done.16.refs_1_ = bf16[2,128,640]{2,1,0:T(8,128)(2,1)S(1)} collective-permute-done((bf16[2,128,640]{2,1,0:T(8,128)(2,1)S(1)}, bf16[2,128,640]{2,1,0:T(8,128)(2,1)S(1)}, u32[]{:S(2)}, u32[]{:S(2)}) %collective-permute-start.16) | collective-permute-done | bytes 327712 | tf_op jit(solution)/shard_map/ppermute | solution.py:42
  89.9 1.7 %collective-permute-done.19.refs_1_ = bf16[2,128,640]{2,1,0:T(8,128)(2,1)S(1)} collective-permute-done((bf16[2,128,640]{2,1,0:T(8,128)(2,1)S(1)}, bf16[2,128,640]{2,1,0:T(8,128)(2,1)S(1)}, u32[]{:S(2)}, u32[]{:S(2)}) %collective-permute-start.19) | collective-permute-done | bytes 327712 | tf_op jit(solution)/shard_map/ppermute | solution.py:42
  91.8 2.5 %collective-permute-done.17.came_x = bf16[1,128,640]{2,1,0:T(8,128)(2,1)S(1)} collective-permute-done((bf16[1,128,640]{2,1,0:T(8,128)(2,1)S(1)}, bf16[1,128,640]{2,1,0:T(8,128)(2,1)S(1)}, u32[]{:S(2)}, u32[]{:S(2)}) %collective-permute-start.17) | collective-permute-done | bytes 163872 | tf_op jit(solution)/shard_map/ppermute | solution.py:42
  94.4 2.3 %collective-permute-done.20.came_y = bf16[1,128,640]{2,1,0:T(8,128)(2,1)S(1)} collective-permute-done((bf16[1,128,640]{2,1,0:T(8,128)(2,1)S(1)}, bf16[1,128,640]{2,1,0:T(8,128)(2,1)S(1)}, u32[]{:S(2)}, u32[]{:S(2)}) %collective-permute-start.20) | collective-permute-done | bytes 163872 | tf_op jit(solution)/shard_map/ppermute | solution.py:42
  96.8 16.0 %all_to_all.15.parts = bf16[8,16,1280]{2,1,0:T(8,128)(2,1)S(1)} all-to-all(bf16[8,16,1280]{2,1,0:T(8,128)(2,1)S(1)} %join.1), channel_id=1, replica_groups=mesh['x'=4,'y_lo'=2,'y_hi'=2,'z'=8,'core'=2] {'z'}, dimensions={0} | all-to-all | bytes 655360 | tf_op jit(solution)/shard_map/all_to_all | solution.py:554
  112.8 17.0 %all_to_all.16.got.mine = bf16[16,16,1280]{2,1,0:T(8,128)(2,1)S(1)} all-to-all(bf16[16,16,1280]{2,1,0:T(8,128)(2,1)S(1)} %finish.1), channel_id=1, replica_groups=mesh['x'=4,'y_lo'=2,'y_hi'=2,'z'=8,'core'=2] {'y_hi','z'}, dimensions={0} | all-to-all | bytes 1310720 | tf_op jit(solution)/shard_map/all_to_all | solution.py:555
  129.8 9.4 %collective-permute-start.21 = (bf16[16,16,1280]{2,1,0:T(8,128)(2,1)S(1)}, bf16[16,16,1280]{2,1,0:T(8,128)(2,1)S(1)}, u32[]{:S(2)}, u32[]{:S(2)}) collective-permute-start(bf16[16,16,1280]{2,1,0:T(8,128)(2,1)S(1)} %all_to_all.16.got.mine), channel_id=1, source_target_pairs={{0,1},{1,0},{2,3},{3,2},{4,5},{5,4},{6,7},{7,6},{8,9},{9,8},{10,11... | collective-permute-start | bytes 1966088 | tf_op jit(solution)/shard_map/ppermute | solution.py:42
  139.3 8.7 %all_to_all.17.parts = f32[16,8,128]{2,1,0:T(8,128)S(1)} all-to-all(f32[16,8,128]{2,1,0:T(8,128)S(1)} %squares.1), channel_id=1, replica_groups=mesh['x'=4,'y_lo'=2,'y_hi'=2,'z'=8,'core'=2] {'x','y_lo','core'}, dimensions={0} | all-to-all | bytes 131072 | tf_op jit(solution)/shard_map/all_to_all | solution.py:558
  148.1 1.5 %rescale.1 = bf16[512,1280]{1,0:T(8,128)(2,1)} custom-call(f32[16,8,128]{2,1,0:T(8,128)S(1)} %all_to_all.17.parts, bf16[16,16,1280]{2,1,0:T(8,128)(2,1)S(1)} %all_to_all.16.got.mine, bf16[16,16,1280]{2,1,0:T(8,128)(2,1)S(1)} %collective-permute-done.21.theirs), custom_call_target="tpu_custom_call" | custom-call | tf_op jit(solution)/shard_map/rescale/pallas_call | solution.py:478
  (52 shorter events, 15.6 us)
Async XLA Ops:
  0.6 1.3 copy-start
  2.0 11.6 %collective-permute-start.1 = (bf16[256,1280]{1,0:T(8,128)(2,1)S(1)}, bf16[256,1280]{1,0:T(8,128)(2,1)S(1)}, u32[]{:S(2)}, u32[]{:S(2)}) collective-permute-start(bf16[256,1280]{1,0:T(8,128)(2,1)S(1)} %constant_dynamic-slice_fusion.refs_3_.refs_4_), channel_id=1, source_target_pairs={{0,32},{1,49},{2,34},{3,51},{4,36},{5,53},{6,38},{7,55},{8,40},{9,... | collective-permute-start | bytes 1966088 | tf_op jit(solution)/shard_map/ppermute | solution.py:42
  5.6 10.6 %collective-permute-start = (bf16[256,1280]{1,0:T(8,128)(2,1)S(1)}, bf16[256,1280]{1,0:T(8,128)(2,1)S(1)}, u32[]{:S(2)}, u32[]{:S(2)}) collective-permute-start(bf16[256,1280]{1,0:T(8,128)(2,1)S(1)} %constant_dynamic-slice_fusion.refs_3_.refs_4_), channel_id=1, source_target_pairs={{0,64},{1,193},{2,194},{3,67},{4,68},{5,197},{6,198},{7,71},{8,72}... | collective-permute-start | bytes 1966088 | tf_op jit(solution)/shard_map/ppermute | solution.py:42
  8.1 1.6 %copy-start.1 = (bf16[256,4096]{1,0:T(8,128)(2,1)S(1)}, bf16[256,4096]{1,0:T(8,128)(2,1)}, u32[]{:S(2)}) copy-start(bf16[256,4096]{1,0:T(8,128)(2,1)} %tokens.1) | copy-start | bytes 6291460
  10.8 2.0 %collective-permute-start.2 = (bf16[128,2048]{1,0:T(8,128)(2,1)S(1)}, bf16[128,2048]{1,0:T(8,128)(2,1)S(1)}, u32[]{:S(2)}, u32[]{:S(2)}) collective-permute-start(bf16[128,2048]{1,0:T(8,128)(2,1)S(1)} %get-tuple-element.59), channel_id=1, source_target_pairs={{0,1},{1,0},{2,3},{3,2},{4,5},{5,4},{6,7},{7,6},{8,9},{9,8},{10,11... | collective-permute-start | bytes 1572872 | tf_op jit(solution)/shard_map/ppermute | solution.py:42
  10.9 2.6 %collective-permute-start.3 = (bf16[128,2048]{1,0:T(8,128)(2,1)S(1)}, bf16[128,2048]{1,0:T(8,128)(2,1)S(1)}, u32[]{:S(2)}, u32[]{:S(2)}) collective-permute-start(bf16[128,2048]{1,0:T(8,128)(2,1)S(1)} %get-tuple-element.60), channel_id=1, source_target_pairs={{0,1},{1,0},{2,3},{3,2},{4,5},{5,4},{6,7},{7,6},{8,9},{9,8},{10,11... | collective-permute-start | bytes 1572872 | tf_op jit(solution)/shard_map/ppermute | solution.py:42
  16.3 10.9 %collective-permute-start.5 = (bf16[256,1280]{1,0:T(8,128)(2,1)S(1)}, bf16[256,1280]{1,0:T(8,128)(2,1)S(1)}, u32[]{:S(2)}, u32[]{:S(2)}) collective-permute-start(bf16[256,1280]{1,0:T(8,128)(2,1)S(1)} %collective-permute-done.refs_5_.refs_6_), channel_id=1, source_target_pairs={{0,32},{1,49},{2,34},{3,51},{4,36},{5,53},{6,38},{7,55},{8,40},{9,... | collective-permute-start | bytes 1966088 | tf_op jit(solution)/shard_map/ppermute | solution.py:42
  16.4 10.8 %collective-permute-start.4 = (bf16[256,1280]{1,0:T(8,128)(2,1)S(1)}, bf16[256,1280]{1,0:T(8,128)(2,1)S(1)}, u32[]{:S(2)}, u32[]{:S(2)}) collective-permute-start(bf16[256,1280]{1,0:T(8,128)(2,1)S(1)} %collective-permute-done.refs_5_.refs_6_), channel_id=1, source_target_pairs={{0,192},{1,65},{2,66},{3,195},{4,196},{5,69},{6,70},{7,199},{8,200... | collective-permute-start | bytes 1966088 | tf_op jit(solution)/shard_map/ppermute | solution.py:42
  17.5 16.8 %collective-permute-start.8 = (bf16[256,1280]{1,0:T(8,128)(2,1)S(1)}, bf16[256,1280]{1,0:T(8,128)(2,1)S(1)}, u32[]{:S(2)}, u32[]{:S(2)}) collective-permute-start(bf16[256,1280]{1,0:T(8,128)(2,1)S(1)} %collective-permute-done.refs_5_.refs_6_), channel_id=1, source_target_pairs={{0,2},{1,15},{2,0},{3,5},{4,6},{5,3},{6,4},{7,9},{8,10},{9,7},{10,... | collective-permute-start | bytes 1966088 | tf_op jit(solution)/shard_map/ppermute | solution.py:42
  27.2 10.6 %collective-permute-start.6 = (bf16[256,1280]{1,0:T(8,128)(2,1)S(1)}, bf16[256,1280]{1,0:T(8,128)(2,1)S(1)}, u32[]{:S(2)}, u32[]{:S(2)}) collective-permute-start(bf16[256,1280]{1,0:T(8,128)(2,1)S(1)} %collective-permute-done.4.refs_3_.refs_7_), channel_id=1, source_target_pairs={{0,32},{1,49},{2,34},{3,51},{4,36},{5,53},{6,38},{7,55},{8,40},{9,... | collective-permute-start | bytes 1966088 | tf_op jit(solution)/shard_map/ppermute | solution.py:42
  28.7 13.5 %collective-permute-start.7 = (bf16[256,1280]{1,0:T(8,128)(2,1)S(1)}, bf16[256,1280]{1,0:T(8,128)(2,1)S(1)}, u32[]{:S(2)}, u32[]{:S(2)}) collective-permute-start(bf16[256,1280]{1,0:T(8,128)(2,1)S(1)} %collective-permute-done.5.refs_4_.refs_8_), channel_id=1, source_target_pairs={{0,2},{1,15},{2,0},{3,5},{4,6},{5,3},{6,4},{7,9},{8,10},{9,7},{10,... | collective-permute-start | bytes 1966088 | tf_op jit(solution)/shard_map/ppermute | solution.py:42
  42.8 2.4 %copy-start.3 = (bf16[256,1024]{1,0:T(8,128)(2,1)S(1)}, bf16[256,1024]{1,0:T(8,128)(2,1)}, u32[]{:S(2)}) copy-start(bf16[256,1024]{1,0:T(8,128)(2,1)} %grad.3) | copy-start | bytes 1572868
  42.8 2.4 %copy-start.4 = (f32[256,128]{1,0:T(8,128)S(1)}, f32[256,128]{1,0:T(8,128)}, u32[]{:S(2)}) copy-start(f32[256,128]{1,0:T(8,128)} %constant.15.clone.sine) | copy-start | bytes 393220
  42.8 2.4 %copy-start.5 = (f32[256,128]{1,0:T(8,128)S(1)}, f32[256,128]{1,0:T(8,128)}, u32[]{:S(2)}) copy-start(f32[256,128]{1,0:T(8,128)} %constant.14.clone.cosine) | copy-start | bytes 393220
  42.8 2.4 %copy-start.6 = (s32[1,256]{1,0:T(1,128)S(1)}, s32[1,256]{1,0:T(1,128)}, u32[]{:S(2)}) copy-start(s32[1,256]{1,0:T(1,128)} %doc.3) | copy-start | bytes 3076
  42.8 2.4 %collective-permute-start.9 = (bf16[256,1280]{1,0:T(8,128)(2,1)S(1)}, bf16[256,1280]{1,0:T(8,128)(2,1)S(1)}, u32[]{:S(2)}, u32[]{:S(2)}) collective-permute-start(bf16[256,1280]{1,0:T(8,128)(2,1)S(1)} %project_late.2), channel_id=1, source_target_pairs={{0,1},{1,0},{2,3},{3,2},{4,5},{5,4},{6,7},{7,6},{8,9},{9,8},{10,11... | collective-permute-start | bytes 1966088 | tf_op jit(solution)/shard_map/ppermute | solution.py:42
  48.6 2.1 %collective-permute-start.10 = (bf16[256,640]{1,0:T(8,128)(2,1)S(1)}, bf16[256,640]{1,0:T(8,128)(2,1)S(1)}, u32[]{:S(2)}, u32[]{:S(2)}) collective-permute-start(bf16[256,640]{1,0:T(8,128)(2,1)S(1)} %get-tuple-element.86.refs_1_.refs_0_), channel_id=1, source_target_pairs={{0,1},{1,0},{2,3},{3,2},{4,5},{5,4},{6,7},{7,6},{8,9},{9,8},{10,11... | collective-permute-start | bytes 983048 | tf_op jit(solution)/shard_map/ppermute | solution.py:42
  50.7 4.0 %collective-permute-start.12 = (bf16[256,640]{1,0:T(8,128)(2,1)S(1)}, bf16[256,640]{1,0:T(8,128)(2,1)S(1)}, u32[]{:S(2)}, u32[]{:S(2)}) collective-permute-start(bf16[256,640]{1,0:T(8,128)(2,1)S(1)} %attend_high.1.refs_1_.refs_2_), channel_id=1, source_target_pairs={{0,1},{1,0},{2,3},{3,2},{4,5},{5,4},{6,7},{7,6},{8,9},{9,8},{10,11... | collective-permute-start | bytes 983048 | tf_op jit(solution)/shard_map/ppermute | solution.py:42
  52.2 17.8 %collective-permute-start.11 = (bf16[8,128,640]{2,1,0:T(8,128)(2,1)S(1)}, bf16[8,128,640]{2,1,0:T(8,128)(2,1)S(1)}, u32[]{:S(2)}, u32[]{:S(2)}) collective-permute-start(bf16[8,128,640]{2,1,0:T(8,128)(2,1)S(1)} %terms.4), channel_id=1, source_target_pairs={{0,64},{1,193},{2,66},{3,195},{4,68},{5,197},{6,70},{7,199},{8,72}... | collective-permute-start | bytes 3932168 | tf_op jit(solution)/shard_map/ppermute | solution.py:42
  55.7 17.8 %collective-permute-start.14 = (bf16[8,128,640]{2,1,0:T(8,128)(2,1)S(1)}, bf16[8,128,640]{2,1,0:T(8,128)(2,1)S(1)}, u32[]{:S(2)}, u32[]{:S(2)}) collective-permute-start(bf16[8,128,640]{2,1,0:T(8,128)(2,1)S(1)} %terms.5), channel_id=1, source_target_pairs={{0,32},{1,49},{2,34},{3,51},{4,36},{5,53},{6,38},{7,55},{8,40},{9,... | collective-permute-start | bytes 3932168 | tf_op jit(solution)/shard_map/ppermute | solution.py:42
  60.0 14.5 %collective-permute-start.15 = (bf16[256,2048]{1,0:T(8,128)(2,1)S(1)}, bf16[256,2048]{1,0:T(8,128)(2,1)S(1)}, u32[]{:S(2)}, u32[]{:S(2)}) collective-permute-start(bf16[256,2048]{1,0:T(8,128)(2,1)S(1)} %get-tuple-element.95), channel_id=1, source_target_pairs={{0,1},{1,0},{2,3},{3,2},{4,5},{5,4},{6,7},{7,6},{8,9},{9,8},{10,11... | collective-permute-start | bytes 3145736 | tf_op jit(solution)/shard_map/ppermute | solution.py:42
  70.9 3.7 %copy-start.2 = (bf16[256,4096]{1,0:T(8,128)(2,1)S(1)}, bf16[256,4096]{1,0:T(8,128)(2,1)}, u32[]{:S(2)}) copy-start(bf16[256,4096]{1,0:T(8,128)(2,1)} %tokens.1) | copy-start | bytes 6291460
  70.9 10.0 %collective-permute-start.13 = (bf16[4,128,640]{2,1,0:T(8,128)(2,1)S(1)}, bf16[4,128,640]{2,1,0:T(8,128)(2,1)S(1)}, u32[]{:S(2)}, u32[]{:S(2)}) collective-permute-start(bf16[4,128,640]{2,1,0:T(8,128)(2,1)S(1)} %get-tuple-element.92), channel_id=1, source_target_pairs={{0,192},{1,65},{2,194},{3,67},{4,196},{5,69},{6,198},{7,71},{8,200... | collective-permute-start | bytes 1966088 | tf_op jit(solution)/shard_map/ppermute | solution.py:42
  74.5 9.8 %collective-permute-start.18 = (bf16[4,128,640]{2,1,0:T(8,128)(2,1)S(1)}, bf16[4,128,640]{2,1,0:T(8,128)(2,1)S(1)}, u32[]{:S(2)}, u32[]{:S(2)}) collective-permute-start(bf16[4,128,640]{2,1,0:T(8,128)(2,1)S(1)} %get-tuple-element.94), channel_id=1, source_target_pairs={{0,48},{1,33},{2,50},{3,35},{4,52},{5,37},{6,54},{7,39},{8,56},{9,... | collective-permute-start | bytes 1966088 | tf_op jit(solution)/shard_map/ppermute | solution.py:42
  81.1 8.6 %collective-permute-start.16 = (bf16[2,128,640]{2,1,0:T(8,128)(2,1)S(1)}, bf16[2,128,640]{2,1,0:T(8,128)(2,1)S(1)}, u32[]{:S(2)}, u32[]{:S(2)}) collective-permute-start(bf16[2,128,640]{2,1,0:T(8,128)(2,1)S(1)} %get-tuple-element.102), channel_id=1, source_target_pairs={{0,32},{1,49},{2,34},{3,51},{4,36},{5,53},{6,38},{7,55},{8,40},{9,... | collective-permute-start | bytes 983048 | tf_op jit(solution)/shard_map/ppermute | solution.py:42
  84.4 7.2 %collective-permute-start.19 = (bf16[2,128,640]{2,1,0:T(8,128)(2,1)S(1)}, bf16[2,128,640]{2,1,0:T(8,128)(2,1)S(1)}, u32[]{:S(2)}, u32[]{:S(2)}) collective-permute-start(bf16[2,128,640]{2,1,0:T(8,128)(2,1)S(1)} %get-tuple-element.107), channel_id=1, source_target_pairs={{0,64},{1,193},{2,66},{3,195},{4,68},{5,197},{6,70},{7,199},{8,72}... | collective-permute-start | bytes 983048 | tf_op jit(solution)/shard_map/ppermute | solution.py:42
  89.8 4.6 %collective-permute-start.17 = (bf16[1,128,640]{2,1,0:T(8,128)(2,1)S(1)}, bf16[1,128,640]{2,1,0:T(8,128)(2,1)S(1)}, u32[]{:S(2)}, u32[]{:S(2)}) collective-permute-start(bf16[1,128,640]{2,1,0:T(8,128)(2,1)S(1)} %get-tuple-element.104), channel_id=1, source_target_pairs={{0,48},{1,33},{2,50},{3,35},{4,52},{5,37},{6,54},{7,39},{8,56},{9,... | collective-permute-start | bytes 491528 | tf_op jit(solution)/shard_map/ppermute | solution.py:42
  91.7 5.0 %collective-permute-start.20 = (bf16[1,128,640]{2,1,0:T(8,128)(2,1)S(1)}, bf16[1,128,640]{2,1,0:T(8,128)(2,1)S(1)}, u32[]{:S(2)}, u32[]{:S(2)}) collective-permute-start(bf16[1,128,640]{2,1,0:T(8,128)(2,1)S(1)} %get-tuple-element.109), channel_id=1, source_target_pairs={{0,192},{1,65},{2,194},{3,67},{4,196},{5,69},{6,198},{7,71},{8,200... | collective-permute-start | bytes 491528 | tf_op jit(solution)/shard_map/ppermute | solution.py:42
  129.8 18.3 %collective-permute-start.21 = (bf16[16,16,1280]{2,1,0:T(8,128)(2,1)S(1)}, bf16[16,16,1280]{2,1,0:T(8,128)(2,1)S(1)}, u32[]{:S(2)}, u32[]{:S(2)}) collective-permute-start(bf16[16,16,1280]{2,1,0:T(8,128)(2,1)S(1)} %all_to_all.16.got.mine), channel_id=1, source_target_pairs={{0,1},{1,0},{2,3},{3,2},{4,5},{5,4},{6,7},{7,6},{8,9},{9,8},{10,11... | collective-permute-start | bytes 1966088 | tf_op jit(solution)/shard_map/ppermute | solution.py:42

commit v3 on v2

--- a/solution.py
+++ b/solution.py
@@ -215,18 +215,19 @@
     return value * cos + pltpu.roll(value, HD // 2, 1) * sin
 
 
-def head_grads(q_rot, g, k_rot, val, seen, cos, sin):
+def head_grads(q_rot, g, k_rot, val, seen, count):
     scale = HD**-0.5
-    scores = jnp.where(seen, dot(q_rot, k_rot, ((1,), (1,))), -1e30)
-    expo = jnp.exp((scores - jnp.max(scores, axis=1, keepdims=True)) * scale)
-    probs = expo * (1.0 / jnp.sum(expo, axis=1, keepdims=True))
-    d_probs = dot(g, val, ((1,), (1,)))
-    delta = jnp.sum(d_probs * probs, axis=1, keepdims=True)
-    d_scores = (probs * (d_probs - delta)).astype(BF16)
-    d_val = dot(probs.astype(BF16), g, ((0,), (0,)))
+    scores = dot(q_rot, k_rot, ((1,), (1,))).reshape(count, TOK, TOK)
+    scores = jnp.where(seen[None], scores, -1e30)
+    expo = jnp.exp((scores - jnp.max(scores, axis=2, keepdims=True)) * scale)
+    probs = expo * (1.0 / jnp.sum(expo, axis=2, keepdims=True))
+    d_probs = dot(g, val, ((1,), (1,))).reshape(count, TOK, TOK)
+    delta = jnp.sum(d_probs * probs, axis=2, keepdims=True)
+    d_scores = (probs * (d_probs - delta)).astype(BF16).reshape(count * TOK, TOK)
+    probs = probs.astype(BF16).reshape(count * TOK, TOK)
+    d_val = dot(probs, g, ((0,), (0,)))
     d_key = dot(d_scores, q_rot, ((0,), (0,)))
-    d_query = dot(d_scores, k_rot, ((1,), (0,))) * scale
-    return turn(d_query, cos, -sin).astype(BF16), d_key, d_val
+    return dot(d_scores, k_rot, ((1,), (0,))) * scale, d_key, d_val
 
 
 def attend_low_body(own, came, grad, doc, cosine, sine, out, rest, d_key, d_val, qkv):
@@ -235,33 +236,30 @@
     seen = visible(doc)
     k_rot = turn(qkv[:, OUTW : OUTW + HD], cos, sin).astype(BF16)
     val = qkv[:, OUTW + HD :].astype(BF16)
-    total_key, total_val = jnp.zeros((TOK, HD), F32), jnp.zeros((TOK, HD), F32)
-    for h in range(QH):
-        head = slice(h * HD, (h + 1) * HD)
-        q_rot = turn(qkv[:, head], cos, sin).astype(BF16)
-        if h < LOW:
-            out[:, head], key, value = head_grads(q_rot, grad[:, head], k_rot, val, seen, cos, sin)
-            total_key, total_val = total_key + key, total_val + value
-        else:
-            rest[:, (h - LOW) * HD : (h - LOW + 1) * HD] = q_rot
+    q_rot = [turn(qkv[:, h * HD : (h + 1) * HD], cos, sin).astype(BF16) for h in range(QH)]
+    g = jnp.concatenate([grad[:, h * HD : (h + 1) * HD] for h in range(LOW)], axis=0)
+    stacked = jnp.concatenate(q_rot[:LOW], axis=0)
+    d_query, d_key[...], d_val[...] = head_grads(stacked, g, k_rot, val, seen, LOW)
+    for h in range(LOW):
+        out[:, h * HD : (h + 1) * HD] = turn(d_query[h * TOK : (h + 1) * TOK], cos, -sin).astype(BF16)
+    for h in range(LOW, QH):
+        rest[:, (h - LOW) * HD : (h - LOW + 1) * HD] = q_rot[h]
     rest[:, COLS - 2 * HD : COLS - HD] = k_rot
     rest[:, COLS - HD :] = val
-    d_key[...] = total_key
-    d_val[...] = total_val
 
 
 def attend_high_body(rest, key_low, val_low, grad, doc, cosine, sine, out):
     cos, sin = cosine[...], sine[...]
-    seen = visible(doc)
     k_rot, val = rest[:, COLS - 2 * HD : COLS - HD], rest[:, COLS - HD :]
-    total_key, total_val = key_low[...], val_low[...]
-    for h in range(LOW, QH):
-        here = slice((h - LOW) * HD, (h - LOW + 1) * HD)
-        g = grad[:, h * HD : (h + 1) * HD]
-        out[:, here], key, value = head_grads(rest[:, here], g, k_rot, val, seen, cos, sin)
-        total_key, total_val = total_key + key, total_val + value
-    out[:, COLS - 2 * HD : COLS - HD] = turn(total_key * HD**-0.5, cos, -sin).astype(BF16)
-    out[:, COLS - HD :] = total_val.astype(BF16)
+    count = QH - LOW
+    g = jnp.concatenate([grad[:, h * HD : (h + 1) * HD] for h in range(LOW, QH)], axis=0)
+    stacked = jnp.concatenate([rest[:, k * HD : (k + 1) * HD] for k in range(count)], axis=0)
+    d_query, key, value = head_grads(stacked, g, k_rot, val, visible(doc), count)
+    for k in range(count):
+        out[:, k * HD : (k + 1) * HD] = turn(d_query[k * TOK : (k + 1) * TOK], cos, -sin).astype(BF16)
+    total_key = (key_low[...] + key) * HD**-0.5
+    out[:, COLS - 2 * HD : COLS - HD] = turn(total_key, cos, -sin).astype(BF16)
+    out[:, COLS - HD :] = (val_low[...] + value).astype(BF16)
 
 
 def attend_cost(heads):
@@ -363,35 +361,22 @@
     return dot(jnp.concatenate(rows, axis=0), right, ((1,), (0,))).reshape(8, QUART, COLS)
 
 
-def term_body(along_x, feats, d_own, d_other, out):
-    out[...] = term_product(along_x, 1, feats, d_own, d_other).astype(BF16)
-
-
-def term_add_body(along_x, feats, d_own, d_other, came, kept, sent):
-    part = term_product(along_x, 0, feats, d_own, d_other)
-    part = (part + came[...].astype(F32)).astype(BF16)
-    kept[...] = part[:4]
-    sent[...] = part[4:]
-
-
-def terms(along_x, made, *came):
-    if came:
-        half = jax.ShapeDtypeStruct((4, QUART, COLS), BF16)
-        body, out_shape, out_specs = term_add_body, (half, half), (VM, VM)
-    else:
-        out_shape, out_specs = jax.ShapeDtypeStruct((8, QUART, COLS), BF16), VM
-        body = term_body
-    return pl.pallas_call(
-        lambda *refs: body(along_x, *refs),
-        out_shape=out_shape,
-        in_specs=[VM] * (3 + len(came)),
-        out_specs=out_specs,
+def term_body(along_x, level, feats, d_own, d_other, out):
+    out[...] = term_product(along_x, level, feats, d_own, d_other).astype(BF16)
+
+
+def terms(along_x, level, made):
+    return pl.pallas_call(
+        lambda *refs: term_body(along_x, level, *refs),
+        out_shape=jax.ShapeDtypeStruct((8, QUART, COLS), BF16),
+        in_specs=[VM] * 3,
+        out_specs=VM,
         compiler_params=pltpu.CompilerParams(vmem_limit_bytes=12 << 20),
         cost_estimate=pl.CostEstimate(
             flops=2 * 8 * QUART * COLS * 2 * TOK, bytes_accessed=4 << 20, transcendentals=0
         ),
         name="terms",
-    )(*made, *came)
+    )(*made)
 
 
 def split_body(count, old, came, kept, sent):
@@ -527,19 +512,18 @@
     low_other, d_high = lax.optimization_barrier((low_other, d_high))
     high_other = swap(d_high, other_core)
     lows, highs = (feats, d_low, low_other), (feats, d_high, high_other)
-    came_x = swap(terms(True, lows), x_1)
-    sent_y = terms(False, highs)
+    came_x = swap(terms(True, 1, lows), x_1)
+    sent_y = terms(False, 1, highs)
     came_y = swap(sent_y, y_1)
     spots, pieces = early_spots + middle_spots + late_spots, early + middle + late
-    sent_y, d_low, low_other, d_high, high_other = lax.optimization_barrier(
-        (sent_y, d_low, low_other, d_high, high_other)
-    )
-    normed_own, normed_send = normed_grad(spots, (d_low, low_other, d_high, high_other), pieces)
+    sent_y, lows, highs = lax.optimization_barrier((sent_y, lows, highs))
+    sum_x, sum_y = terms(True, 0, lows), terms(False, 0, highs)
+    normed_own, normed_send = normed_grad(spots, (*lows[1:], *highs[1:]), pieces)
     normed_came = swap(normed_send, other_core)
-    came_x, normed_own = lax.optimization_barrier((came_x, normed_own))
-    sum_x, sent_x = terms(True, lows, came_x)
+    came_x, sum_x, sum_y, normed_own = lax.optimization_barrier((came_x, sum_x, sum_y, normed_own))
+    sum_x, sent_x = split(sum_x, came_x)
     came_x = swap(sent_x, x_2)
-    sum_y, sent_y = terms(False, highs, came_y)
+    sum_y, sent_y = split(sum_y, came_y)
     came_y = swap(sent_y, y_2)
     sent_y, normed_came = lax.optimization_barrier((sent_y, normed_came))
     d_tokens = tokens_grad(normed_own, normed_came, tokens, scale_r)

time: 150 us -> 145 us (0.967)
  starting transfers between devices: 39 us -> 36.9 us
  waiting for transfers between devices: 42.8 us -> 41.3 us
    ppermute x22, starting transfers between devices: 39 us -> 36.9 us  [swap(): return lax.ppermute(value, AXES, pairs)]
  transfers between devices with their start and end apart: 22 -> 22, of which waited for: 16 -> 17; matrix products, arithmetic and copies ran while one was open for 0% -> 0% of each run, Pallas kernels for 11% -> 12%
where the time goes in v3:
time: 145 us
  blocking collectives  41.6 us (29%)
  waiting for transfers between devices  41.3 us (28%)
  starting transfers between devices  36.9 us (25%)
  Pallas kernels  21 us (14%)
  local copies, waits for them, and re-layouts  2.98 us (2%)
    ppermute x22, waiting for transfers between devices, swap(): return lax.ppermute(value, AXES, pairs)  41.3 us
    ppermute x22, starting transfers between devices, swap(): return lax.ppermute(value, AXES, pairs)  36.9 us
    all_to_all x1, blocking collectives, on_device(): got = lax.all_to_all(got, ('y_hi', 'z'), 0, 0)  17.2 us
    all_to_all x1, blocking collectives, on_device(): got = finish(lax.all_to_all(total, 'z', 0, 0))  15.9 us
    all_to_all x1, blocking collectives, on_device(): parts = lax.all_to_all(squares(got), ('x', 'y_lo', 'core'), 0, 0)  8.57 us
    pallas_call x4, Pallas kernels, terms(): pl.pallas_call(lambda *refs: term_body(along_x, level, *refs), out_shape=...  3.91 us
    pallas_call x1, Pallas kernels, normed_grad(): pl.pallas_call(lambda *refs: normed_body(spots, *refs), out_shape=(jax.Sh...  2.98 us
    unnamed x14, local copies, waits for them, and re-layouts  2.93 us
  transfers between devices with their start and end apart: 22, of which 17 were waited for; matrix products, arithmetic and copies ran while one was open for 0% of the time, Pallas kernels for 12%

profile of v3, /device:TPU:1, one launch (start us, length us, event | category | flops | bytes accessed | tf_op | source)
XLA Modules:
  0.0 144.7 jit_solution(10579036485235061588)
XLA Ops:
  0.6 1.3 copy-done
  2.0 3.7 %collective-permute-start.1 = (bf16[256,1280]{1,0:T(8,128)(2,1)S(1)}, bf16[256,1280]{1,0:T(8,128)(2,1)S(1)}, u32[]{:S(2)}, u32[]{:S(2)}) collective-permute-start(bf16[256,1280]{1,0:T(8,128)(2,1)S(1)} %constant_dynamic-slice_fusion.refs_3_.refs_4_), channel_id=1, source_target_pairs={{0,32},{1,49},{2,34},{3,51},{4,36},{5,53},{6,38},{7,55},{8,40},{9,... | collective-permute-start | bytes 1966088 | tf_op jit(solution)/shard_map/ppermute | solution.py:42
  5.6 2.5 %collective-permute-start = (bf16[256,1280]{1,0:T(8,128)(2,1)S(1)}, bf16[256,1280]{1,0:T(8,128)(2,1)S(1)}, u32[]{:S(2)}, u32[]{:S(2)}) collective-permute-start(bf16[256,1280]{1,0:T(8,128)(2,1)S(1)} %constant_dynamic-slice_fusion.refs_3_.refs_4_), channel_id=1, source_target_pairs={{0,64},{1,193},{2,194},{3,67},{4,68},{5,197},{6,198},{7,71},{8,72}... | collective-permute-start | bytes 1966088 | tf_op jit(solution)/shard_map/ppermute | solution.py:42
  8.1 1.6 %copy-done.1 = bf16[256,4096]{1,0:T(8,128)(2,1)S(1)} copy-done((bf16[256,4096]{1,0:T(8,128)(2,1)S(1)}, bf16[256,4096]{1,0:T(8,128)(2,1)}, u32[]{:S(2)}) %copy-start.1) | copy-done | bytes 2097176
  11.4 1.4 collective-permute-done.2.refs_1_.low.refs_0_
  13.6 2.7 %collective-permute-done.refs_5_.refs_6_ = bf16[256,1280]{1,0:T(8,128)(2,1)S(1)} collective-permute-done((bf16[256,1280]{1,0:T(8,128)(2,1)S(1)}, bf16[256,1280]{1,0:T(8,128)(2,1)S(1)}, u32[]{:S(2)}, u32[]{:S(2)}) %collective-permute-start) | collective-permute-done | bytes 655392 | tf_op jit(solution)/shard_map/ppermute | solution.py:42
  17.5 7.1 %collective-permute-start.8 = (bf16[256,1280]{1,0:T(8,128)(2,1)S(1)}, bf16[256,1280]{1,0:T(8,128)(2,1)S(1)}, u32[]{:S(2)}, u32[]{:S(2)}) collective-permute-start(bf16[256,1280]{1,0:T(8,128)(2,1)S(1)} %collective-permute-done.refs_5_.refs_6_), channel_id=1, source_target_pairs={{0,2},{1,15},{2,0},{3,5},{4,6},{5,3},{6,4},{7,9},{8,10},{9,7},{10,... | collective-permute-start | bytes 1966088 | tf_op jit(solution)/shard_map/ppermute | solution.py:42
  27.2 1.5 %collective-permute-start.6 = (bf16[256,1280]{1,0:T(8,128)(2,1)S(1)}, bf16[256,1280]{1,0:T(8,128)(2,1)S(1)}, u32[]{:S(2)}, u32[]{:S(2)}) collective-permute-start(bf16[256,1280]{1,0:T(8,128)(2,1)S(1)} %collective-permute-done.4.refs_3_.refs_7_), channel_id=1, source_target_pairs={{0,32},{1,49},{2,34},{3,51},{4,36},{5,53},{6,38},{7,55},{8,40},{9,... | collective-permute-start | bytes 1966088 | tf_op jit(solution)/shard_map/ppermute | solution.py:42
  28.7 5.6 %collective-permute-start.7 = (bf16[256,1280]{1,0:T(8,128)(2,1)S(1)}, bf16[256,1280]{1,0:T(8,128)(2,1)S(1)}, u32[]{:S(2)}, u32[]{:S(2)}) collective-permute-start(bf16[256,1280]{1,0:T(8,128)(2,1)S(1)} %collective-permute-done.5.refs_4_.refs_8_), channel_id=1, source_target_pairs={{0,2},{1,15},{2,0},{3,5},{4,6},{5,3},{6,4},{7,9},{8,10},{9,7},{10,... | collective-permute-start | bytes 1966088 | tf_op jit(solution)/shard_map/ppermute | solution.py:42
  35.5 2.4 %collective-permute-done.6.refs_2_.refs_1_.refs_10_ = bf16[256,1280]{1,0:T(8,128)(2,1)S(1)} collective-permute-done((bf16[256,1280]{1,0:T(8,128)(2,1)S(1)}, bf16[256,1280]{1,0:T(8,128)(2,1)S(1)}, u32[]{:S(2)}, u32[]{:S(2)}) %collective-permute-start.6) | collective-permute-done | bytes 655392 | tf_op jit(solution)/shard_map/ppermute | solution.py:42
  37.9 4.4 %collective-permute-done.7.refs_3_.refs_2_.refs_11_ = bf16[256,1280]{1,0:T(8,128)(2,1)S(1)} collective-permute-done((bf16[256,1280]{1,0:T(8,128)(2,1)S(1)}, bf16[256,1280]{1,0:T(8,128)(2,1)S(1)}, u32[]{:S(2)}, u32[]{:S(2)}) %collective-permute-start.7) | collective-permute-done | bytes 655392 | tf_op jit(solution)/shard_map/ppermute | solution.py:42
  43.5 1.6 %collective-permute-done.9.came = bf16[256,1280]{1,0:T(8,128)(2,1)S(1)} collective-permute-done((bf16[256,1280]{1,0:T(8,128)(2,1)S(1)}, bf16[256,1280]{1,0:T(8,128)(2,1)S(1)}, u32[]{:S(2)}, u32[]{:S(2)}) %collective-permute-start.9) | collective-permute-done | bytes 655392 | tf_op jit(solution)/shard_map/ppermute | solution.py:42
  45.0 2.1 %attend_low.1 = (bf16[256,640]{1,0:T(8,128)(2,1)S(1)}, bf16[256,640]{1,0:T(8,128)(2,1)S(1)}, f32[256,128]{1,0:T(8,128)S(1)}, f32[256,128]{1,0:T(8,128)S(1)}) custom-call(f32[256,1280]{1,0:T(8,128)S(1)} %project_late.3.own, bf16[256,1280]{1,0:T(8,128)(2,1)S(1)} %collective-permute-done.9.came, bf16[256,1024]{1,0:T(8,128)(2,1)S(1)} %copy-done.3, ...), custom_call_target="tpu_custom_call" | custom-call | flops 419430400 | bytes 4194304 | tf_op jit(solution)/shard_map/attend_low/pallas_call | solution.py:273
  47.6 1.2 attend_high.1.refs_1_.refs_2_
  50.3 2.6 %collective-permute-start.11 = (bf16[8,128,640]{2,1,0:T(8,128)(2,1)S(1)}, bf16[8,128,640]{2,1,0:T(8,128)(2,1)S(1)}, u32[]{:S(2)}, u32[]{:S(2)}) collective-permute-start(bf16[8,128,640]{2,1,0:T(8,128)(2,1)S(1)} %terms.4), channel_id=1, source_target_pairs={{0,64},{1,193},{2,66},{3,195},{4,68},{5,197},{6,70},{7,199},{8,72}... | collective-permute-start | bytes 3932168 | tf_op jit(solution)/shard_map/ppermute | solution.py:42
  53.8 1.3 collective-permute-start.14
  55.1 3.0 %normed_grad.1 = (f32[256,2048]{1,0:T(8,128)S(1)}, bf16[256,2048]{1,0:T(8,128)(2,1)S(1)}) custom-call(bf16[256,640]{1,0:T(8,128)(2,1)S(1)} %get-tuple-element.91.refs_1_.refs_0_, bf16[256,640]{1,0:T(8,128)(2,1)S(1)} %collective-permute-done.10.refs_2_.refs_1_, bf16[256,640]{1,0:T(8,128)(2,1)S(1)} %attend_high.1.refs_1_.refs_2_, ...), custom_call_target="tpu_custom_call" | custom-call | flops 2684354560 | bytes 8388608 | tf_op jit(solution)/shard_map/normed_grad/pallas_call | solution.py:308
  60.2 7.9 %collective-permute-done.11.refs_1_ = bf16[8,128,640]{2,1,0:T(8,128)(2,1)S(1)} collective-permute-done((bf16[8,128,640]{2,1,0:T(8,128)(2,1)S(1)}, bf16[8,128,640]{2,1,0:T(8,128)(2,1)S(1)}, u32[]{:S(2)}, u32[]{:S(2)}) %collective-permute-start.11) | collective-permute-done | bytes 1310752 | tf_op jit(solution)/shard_map/ppermute | solution.py:42
  68.4 3.1 %collective-permute-done.14.refs_1_ = bf16[8,128,640]{2,1,0:T(8,128)(2,1)S(1)} collective-permute-done((bf16[8,128,640]{2,1,0:T(8,128)(2,1)S(1)}, bf16[8,128,640]{2,1,0:T(8,128)(2,1)S(1)}, u32[]{:S(2)}, u32[]{:S(2)}) %collective-permute-start.14) | collective-permute-done | bytes 1310752 | tf_op jit(solution)/shard_map/ppermute | solution.py:42
  72.0 2.7 %tokens_grad.1 = bf16[256,4096]{1,0:T(8,128)(2,1)} custom-call(f32[256,2048]{1,0:T(8,128)S(1)} %get-tuple-element.100.own, bf16[256,2048]{1,0:T(8,128)(2,1)S(1)} %collective-permute-done.15.came, bf16[256,4096]{1,0:T(8,128)(2,1)S(1)} %copy-done.2, f32[256,1]{1,0:T(8,128)S(1)} %get-tuple-element.105.scale_r), custom_call_target="tpu_custom_call" | custom-call | flops 10485760 | bytes 8388608 | tf_op jit(solution)/shard_map/tokens_grad/pallas_call | solution.py:339
  74.7 3.4 %collective-permute-done.13.refs_1_ = bf16[4,128,640]{2,1,0:T(8,128)(2,1)S(1)} collective-permute-done((bf16[4,128,640]{2,1,0:T(8,128)(2,1)S(1)}, bf16[4,128,640]{2,1,0:T(8,128)(2,1)S(1)}, u32[]{:S(2)}, u32[]{:S(2)}) %collective-permute-start.13) | collective-permute-done | bytes 655392 | tf_op jit(solution)/shard_map/ppermute | solution.py:42
  78.3 1.5 %collective-permute-start.16 = (bf16[2,128,640]{2,1,0:T(8,128)(2,1)S(1)}, bf16[2,128,640]{2,1,0:T(8,128)(2,1)S(1)}, u32[]{:S(2)}, u32[]{:S(2)}) collective-permute-start(bf16[2,128,640]{2,1,0:T(8,128)(2,1)S(1)} %get-tuple-element.110), channel_id=1, source_target_pairs={{0,32},{1,49},{2,34},{3,51},{4,36},{5,53},{6,38},{7,55},{8,40},{9,... | collective-permute-start | bytes 983048 | tf_op jit(solution)/shard_map/ppermute | solution.py:42
  79.8 1.9 %collective-permute-done.18.refs_1_ = bf16[4,128,640]{2,1,0:T(8,128)(2,1)S(1)} collective-permute-done((bf16[4,128,640]{2,1,0:T(8,128)(2,1)S(1)}, bf16[4,128,640]{2,1,0:T(8,128)(2,1)S(1)}, u32[]{:S(2)}, u32[]{:S(2)}) %collective-permute-start.18) | collective-permute-done | bytes 655392 | tf_op jit(solution)/shard_map/ppermute | solution.py:42
  82.6 3.9 %collective-permute-done.16.refs_1_ = bf16[2,128,640]{2,1,0:T(8,128)(2,1)S(1)} collective-permute-done((bf16[2,128,640]{2,1,0:T(8,128)(2,1)S(1)}, bf16[2,128,640]{2,1,0:T(8,128)(2,1)S(1)}, u32[]{:S(2)}, u32[]{:S(2)}) %collective-permute-start.16) | collective-permute-done | bytes 327712 | tf_op jit(solution)/shard_map/ppermute | solution.py:42
  86.6 2.4 %collective-permute-done.19.refs_1_ = bf16[2,128,640]{2,1,0:T(8,128)(2,1)S(1)} collective-permute-done((bf16[2,128,640]{2,1,0:T(8,128)(2,1)S(1)}, bf16[2,128,640]{2,1,0:T(8,128)(2,1)S(1)}, u32[]{:S(2)}, u32[]{:S(2)}) %collective-permute-start.19) | collective-permute-done | bytes 327712 | tf_op jit(solution)/shard_map/ppermute | solution.py:42
  89.3 1.8 %collective-permute-done.17.came_x = bf16[1,128,640]{2,1,0:T(8,128)(2,1)S(1)} collective-permute-done((bf16[1,128,640]{2,1,0:T(8,128)(2,1)S(1)}, bf16[1,128,640]{2,1,0:T(8,128)(2,1)S(1)}, u32[]{:S(2)}, u32[]{:S(2)}) %collective-permute-start.17) | collective-permute-done | bytes 163872 | tf_op jit(solution)/shard_map/ppermute | solution.py:42
  91.1 2.6 %collective-permute-done.20.came_y = bf16[1,128,640]{2,1,0:T(8,128)(2,1)S(1)} collective-permute-done((bf16[1,128,640]{2,1,0:T(8,128)(2,1)S(1)}, bf16[1,128,640]{2,1,0:T(8,128)(2,1)S(1)}, u32[]{:S(2)}, u32[]{:S(2)}) %collective-permute-start.20) | collective-permute-done | bytes 163872 | tf_op jit(solution)/shard_map/ppermute | solution.py:42
  93.8 15.9 %all_to_all.15.parts = bf16[8,16,1280]{2,1,0:T(8,128)(2,1)S(1)} all-to-all(bf16[8,16,1280]{2,1,0:T(8,128)(2,1)S(1)} %join.1), channel_id=1, replica_groups=mesh['x'=4,'y_lo'=2,'y_hi'=2,'z'=8,'core'=2] {'z'}, dimensions={0} | all-to-all | bytes 655360 | tf_op jit(solution)/shard_map/all_to_all | solution.py:538
  109.7 17.2 %all_to_all.16.got.mine = bf16[16,16,1280]{2,1,0:T(8,128)(2,1)S(1)} all-to-all(bf16[16,16,1280]{2,1,0:T(8,128)(2,1)S(1)} %finish.1), channel_id=1, replica_groups=mesh['x'=4,'y_lo'=2,'y_hi'=2,'z'=8,'core'=2] {'y_hi','z'}, dimensions={0} | all-to-all | bytes 1310720 | tf_op jit(solution)/shard_map/all_to_all | solution.py:539
  126.9 7.5 %collective-permute-start.21 = (bf16[16,16,1280]{2,1,0:T(8,128)(2,1)S(1)}, bf16[16,16,1280]{2,1,0:T(8,128)(2,1)S(1)}, u32[]{:S(2)}, u32[]{:S(2)}) collective-permute-start(bf16[16,16,1280]{2,1,0:T(8,128)(2,1)S(1)} %all_to_all.16.got.mine), channel_id=1, source_target_pairs={{0,1},{1,0},{2,3},{3,2},{4,5},{5,4},{6,7},{7,6},{8,9},{9,8},{10,11... | collective-permute-start | bytes 1966088 | tf_op jit(solution)/shard_map/ppermute | solution.py:42
  134.6 8.6 %all_to_all.17.parts = f32[16,8,128]{2,1,0:T(8,128)S(1)} all-to-all(f32[16,8,128]{2,1,0:T(8,128)S(1)} %squares.1), channel_id=1, replica_groups=mesh['x'=4,'y_lo'=2,'y_hi'=2,'z'=8,'core'=2] {'x','y_lo','core'}, dimensions={0} | all-to-all | bytes 131072 | tf_op jit(solution)/shard_map/all_to_all | solution.py:542
  143.1 1.5 %rescale.1 = bf16[512,1280]{1,0:T(8,128)(2,1)} custom-call(f32[16,8,128]{2,1,0:T(8,128)S(1)} %all_to_all.17.parts, bf16[16,16,1280]{2,1,0:T(8,128)(2,1)S(1)} %all_to_all.16.got.mine, bf16[16,16,1280]{2,1,0:T(8,128)(2,1)S(1)} %collective-permute-done.21.theirs), custom_call_target="tpu_custom_call" | custom-call | tf_op jit(solution)/shard_map/rescale/pallas_call | solution.py:463
  (54 shorter events, 16.0 us)
Async XLA Ops:
  0.6 1.3 copy-start
  2.0 11.6 %collective-permute-start.1 = (bf16[256,1280]{1,0:T(8,128)(2,1)S(1)}, bf16[256,1280]{1,0:T(8,128)(2,1)S(1)}, u32[]{:S(2)}, u32[]{:S(2)}) collective-permute-start(bf16[256,1280]{1,0:T(8,128)(2,1)S(1)} %constant_dynamic-slice_fusion.refs_3_.refs_4_), channel_id=1, source_target_pairs={{0,32},{1,49},{2,34},{3,51},{4,36},{5,53},{6,38},{7,55},{8,40},{9,... | collective-permute-start | bytes 1966088 | tf_op jit(solution)/shard_map/ppermute | solution.py:42
  5.6 10.6 %collective-permute-start = (bf16[256,1280]{1,0:T(8,128)(2,1)S(1)}, bf16[256,1280]{1,0:T(8,128)(2,1)S(1)}, u32[]{:S(2)}, u32[]{:S(2)}) collective-permute-start(bf16[256,1280]{1,0:T(8,128)(2,1)S(1)} %constant_dynamic-slice_fusion.refs_3_.refs_4_), channel_id=1, source_target_pairs={{0,64},{1,193},{2,194},{3,67},{4,68},{5,197},{6,198},{7,71},{8,72}... | collective-permute-start | bytes 1966088 | tf_op jit(solution)/shard_map/ppermute | solution.py:42
  8.1 1.6 %copy-start.1 = (bf16[256,4096]{1,0:T(8,128)(2,1)S(1)}, bf16[256,4096]{1,0:T(8,128)(2,1)}, u32[]{:S(2)}) copy-start(bf16[256,4096]{1,0:T(8,128)(2,1)} %tokens.1) | copy-start | bytes 6291460
  10.8 2.0 %collective-permute-start.2 = (bf16[128,2048]{1,0:T(8,128)(2,1)S(1)}, bf16[128,2048]{1,0:T(8,128)(2,1)S(1)}, u32[]{:S(2)}, u32[]{:S(2)}) collective-permute-start(bf16[128,2048]{1,0:T(8,128)(2,1)S(1)} %get-tuple-element.63), channel_id=1, source_target_pairs={{0,1},{1,0},{2,3},{3,2},{4,5},{5,4},{6,7},{7,6},{8,9},{9,8},{10,11... | collective-permute-start | bytes 1572872 | tf_op jit(solution)/shard_map/ppermute | solution.py:42
  10.9 2.6 %collective-permute-start.3 = (bf16[128,2048]{1,0:T(8,128)(2,1)S(1)}, bf16[128,2048]{1,0:T(8,128)(2,1)S(1)}, u32[]{:S(2)}, u32[]{:S(2)}) collective-permute-start(bf16[128,2048]{1,0:T(8,128)(2,1)S(1)} %get-tuple-element.64), channel_id=1, source_target_pairs={{0,1},{1,0},{2,3},{3,2},{4,5},{5,4},{6,7},{7,6},{8,9},{9,8},{10,11... | collective-permute-start | bytes 1572872 | tf_op jit(solution)/shard_map/ppermute | solution.py:42
  16.3 10.9 %collective-permute-start.5 = (bf16[256,1280]{1,0:T(8,128)(2,1)S(1)}, bf16[256,1280]{1,0:T(8,128)(2,1)S(1)}, u32[]{:S(2)}, u32[]{:S(2)}) collective-permute-start(bf16[256,1280]{1,0:T(8,128)(2,1)S(1)} %collective-permute-done.refs_5_.refs_6_), channel_id=1, source_target_pairs={{0,32},{1,49},{2,34},{3,51},{4,36},{5,53},{6,38},{7,55},{8,40},{9,... | collective-permute-start | bytes 1966088 | tf_op jit(solution)/shard_map/ppermute | solution.py:42
  16.4 10.8 %collective-permute-start.4 = (bf16[256,1280]{1,0:T(8,128)(2,1)S(1)}, bf16[256,1280]{1,0:T(8,128)(2,1)S(1)}, u32[]{:S(2)}, u32[]{:S(2)}) collective-permute-start(bf16[256,1280]{1,0:T(8,128)(2,1)S(1)} %collective-permute-done.refs_5_.refs_6_), channel_id=1, source_target_pairs={{0,192},{1,65},{2,66},{3,195},{4,196},{5,69},{6,70},{7,199},{8,200... | collective-permute-start | bytes 1966088 | tf_op jit(solution)/shard_map/ppermute | solution.py:42
  17.5 16.8 %collective-permute-start.8 = (bf16[256,1280]{1,0:T(8,128)(2,1)S(1)}, bf16[256,1280]{1,0:T(8,128)(2,1)S(1)}, u32[]{:S(2)}, u32[]{:S(2)}) collective-permute-start(bf16[256,1280]{1,0:T(8,128)(2,1)S(1)} %collective-permute-done.refs_5_.refs_6_), channel_id=1, source_target_pairs={{0,2},{1,15},{2,0},{3,5},{4,6},{5,3},{6,4},{7,9},{8,10},{9,7},{10,... | collective-permute-start | bytes 1966088 | tf_op jit(solution)/shard_map/ppermute | solution.py:42
  27.2 10.6 %collective-permute-start.6 = (bf16[256,1280]{1,0:T(8,128)(2,1)S(1)}, bf16[256,1280]{1,0:T(8,128)(2,1)S(1)}, u32[]{:S(2)}, u32[]{:S(2)}) collective-permute-start(bf16[256,1280]{1,0:T(8,128)(2,1)S(1)} %collective-permute-done.4.refs_3_.refs_7_), channel_id=1, source_target_pairs={{0,32},{1,49},{2,34},{3,51},{4,36},{5,53},{6,38},{7,55},{8,40},{9,... | collective-permute-start | bytes 1966088 | tf_op jit(solution)/shard_map/ppermute | solution.py:42
  28.7 13.5 %collective-permute-start.7 = (bf16[256,1280]{1,0:T(8,128)(2,1)S(1)}, bf16[256,1280]{1,0:T(8,128)(2,1)S(1)}, u32[]{:S(2)}, u32[]{:S(2)}) collective-permute-start(bf16[256,1280]{1,0:T(8,128)(2,1)S(1)} %collective-permute-done.5.refs_4_.refs_8_), channel_id=1, source_target_pairs={{0,2},{1,15},{2,0},{3,5},{4,6},{5,3},{6,4},{7,9},{8,10},{9,7},{10,... | collective-permute-start | bytes 1966088 | tf_op jit(solution)/shard_map/ppermute | solution.py:42
  42.8 2.2 %copy-start.3 = (bf16[256,1024]{1,0:T(8,128)(2,1)S(1)}, bf16[256,1024]{1,0:T(8,128)(2,1)}, u32[]{:S(2)}) copy-start(bf16[256,1024]{1,0:T(8,128)(2,1)} %grad.3) | copy-start | bytes 1572868
  42.8 2.2 %copy-start.4 = (f32[256,128]{1,0:T(8,128)S(1)}, f32[256,128]{1,0:T(8,128)}, u32[]{:S(2)}) copy-start(f32[256,128]{1,0:T(8,128)} %constant.15.clone.sine) | copy-start | bytes 393220
  42.8 2.2 %copy-start.5 = (f32[256,128]{1,0:T(8,128)S(1)}, f32[256,128]{1,0:T(8,128)}, u32[]{:S(2)}) copy-start(f32[256,128]{1,0:T(8,128)} %constant.14.clone.cosine) | copy-start | bytes 393220
  42.8 2.2 %copy-start.6 = (s32[1,256]{1,0:T(1,128)S(1)}, s32[1,256]{1,0:T(1,128)}, u32[]{:S(2)}) copy-start(s32[1,256]{1,0:T(1,128)} %doc.3) | copy-start | bytes 3076
  42.8 2.2 %collective-permute-start.9 = (bf16[256,1280]{1,0:T(8,128)(2,1)S(1)}, bf16[256,1280]{1,0:T(8,128)(2,1)S(1)}, u32[]{:S(2)}, u32[]{:S(2)}) collective-permute-start(bf16[256,1280]{1,0:T(8,128)(2,1)S(1)} %project_late.2), channel_id=1, source_target_pairs={{0,1},{1,0},{2,3},{3,2},{4,5},{5,4},{6,7},{7,6},{8,9},{9,8},{10,11... | collective-permute-start | bytes 1966088 | tf_op jit(solution)/shard_map/ppermute | solution.py:42
  47.2 1.9 %collective-permute-start.10 = (bf16[256,640]{1,0:T(8,128)(2,1)S(1)}, bf16[256,640]{1,0:T(8,128)(2,1)S(1)}, u32[]{:S(2)}, u32[]{:S(2)}) collective-permute-start(bf16[256,640]{1,0:T(8,128)(2,1)S(1)} %get-tuple-element.91.refs_1_.refs_0_), channel_id=1, source_target_pairs={{0,1},{1,0},{2,3},{3,2},{4,5},{5,4},{6,7},{7,6},{8,9},{9,8},{10,11... | collective-permute-start | bytes 983048 | tf_op jit(solution)/shard_map/ppermute | solution.py:42
  49.1 3.7 %collective-permute-start.12 = (bf16[256,640]{1,0:T(8,128)(2,1)S(1)}, bf16[256,640]{1,0:T(8,128)(2,1)S(1)}, u32[]{:S(2)}, u32[]{:S(2)}) collective-permute-start(bf16[256,640]{1,0:T(8,128)(2,1)S(1)} %attend_high.1.refs_1_.refs_2_), channel_id=1, source_target_pairs={{0,1},{1,0},{2,3},{3,2},{4,5},{5,4},{6,7},{7,6},{8,9},{9,8},{10,11... | collective-permute-start | bytes 983048 | tf_op jit(solution)/shard_map/ppermute | solution.py:42
  50.3 17.8 %collective-permute-start.11 = (bf16[8,128,640]{2,1,0:T(8,128)(2,1)S(1)}, bf16[8,128,640]{2,1,0:T(8,128)(2,1)S(1)}, u32[]{:S(2)}, u32[]{:S(2)}) collective-permute-start(bf16[8,128,640]{2,1,0:T(8,128)(2,1)S(1)} %terms.4), channel_id=1, source_target_pairs={{0,64},{1,193},{2,66},{3,195},{4,68},{5,197},{6,70},{7,199},{8,72}... | collective-permute-start | bytes 3932168 | tf_op jit(solution)/shard_map/ppermute | solution.py:42
  53.8 17.8 %collective-permute-start.14 = (bf16[8,128,640]{2,1,0:T(8,128)(2,1)S(1)}, bf16[8,128,640]{2,1,0:T(8,128)(2,1)S(1)}, u32[]{:S(2)}, u32[]{:S(2)}) collective-permute-start(bf16[8,128,640]{2,1,0:T(8,128)(2,1)S(1)} %terms.5), channel_id=1, source_target_pairs={{0,32},{1,49},{2,34},{3,51},{4,36},{5,53},{6,38},{7,55},{8,40},{9,... | collective-permute-start | bytes 3932168 | tf_op jit(solution)/shard_map/ppermute | solution.py:42
  58.1 13.9 %collective-permute-start.15 = (bf16[256,2048]{1,0:T(8,128)(2,1)S(1)}, bf16[256,2048]{1,0:T(8,128)(2,1)S(1)}, u32[]{:S(2)}, u32[]{:S(2)}) collective-permute-start(bf16[256,2048]{1,0:T(8,128)(2,1)S(1)} %get-tuple-element.103), channel_id=1, source_target_pairs={{0,1},{1,0},{2,3},{3,2},{4,5},{5,4},{6,7},{7,6},{8,9},{9,8},{10,11... | collective-permute-start | bytes 3145736 | tf_op jit(solution)/shard_map/ppermute | solution.py:42
  68.3 3.7 %copy-start.2 = (bf16[256,4096]{1,0:T(8,128)(2,1)S(1)}, bf16[256,4096]{1,0:T(8,128)(2,1)}, u32[]{:S(2)}) copy-start(bf16[256,4096]{1,0:T(8,128)(2,1)} %tokens.1) | copy-start | bytes 6291460
  68.3 9.8 %collective-permute-start.13 = (bf16[4,128,640]{2,1,0:T(8,128)(2,1)S(1)}, bf16[4,128,640]{2,1,0:T(8,128)(2,1)S(1)}, u32[]{:S(2)}, u32[]{:S(2)}) collective-permute-start(bf16[4,128,640]{2,1,0:T(8,128)(2,1)S(1)} %get-tuple-element.99), channel_id=1, source_target_pairs={{0,192},{1,65},{2,194},{3,67},{4,196},{5,69},{6,198},{7,71},{8,200... | collective-permute-start | bytes 1966088 | tf_op jit(solution)/shard_map/ppermute | solution.py:42
  71.9 9.8 %collective-permute-start.18 = (bf16[4,128,640]{2,1,0:T(8,128)(2,1)S(1)}, bf16[4,128,640]{2,1,0:T(8,128)(2,1)S(1)}, u32[]{:S(2)}, u32[]{:S(2)}) collective-permute-start(bf16[4,128,640]{2,1,0:T(8,128)(2,1)S(1)} %get-tuple-element.102), channel_id=1, source_target_pairs={{0,48},{1,33},{2,50},{3,35},{4,52},{5,37},{6,54},{7,39},{8,56},{9,... | collective-permute-start | bytes 1966088 | tf_op jit(solution)/shard_map/ppermute | solution.py:42
  78.3 8.1 %collective-permute-start.16 = (bf16[2,128,640]{2,1,0:T(8,128)(2,1)S(1)}, bf16[2,128,640]{2,1,0:T(8,128)(2,1)S(1)}, u32[]{:S(2)}, u32[]{:S(2)}) collective-permute-start(bf16[2,128,640]{2,1,0:T(8,128)(2,1)S(1)} %get-tuple-element.110), channel_id=1, source_target_pairs={{0,32},{1,49},{2,34},{3,51},{4,36},{5,53},{6,38},{7,55},{8,40},{9,... | collective-permute-start | bytes 983048 | tf_op jit(solution)/shard_map/ppermute | solution.py:42
  81.8 7.2 %collective-permute-start.19 = (bf16[2,128,640]{2,1,0:T(8,128)(2,1)S(1)}, bf16[2,128,640]{2,1,0:T(8,128)(2,1)S(1)}, u32[]{:S(2)}, u32[]{:S(2)}) collective-permute-start(bf16[2,128,640]{2,1,0:T(8,128)(2,1)S(1)} %get-tuple-element.115), channel_id=1, source_target_pairs={{0,64},{1,193},{2,66},{3,195},{4,68},{5,197},{6,70},{7,199},{8,72}... | collective-permute-start | bytes 983048 | tf_op jit(solution)/shard_map/ppermute | solution.py:42
  86.5 4.6 %collective-permute-start.17 = (bf16[1,128,640]{2,1,0:T(8,128)(2,1)S(1)}, bf16[1,128,640]{2,1,0:T(8,128)(2,1)S(1)}, u32[]{:S(2)}, u32[]{:S(2)}) collective-permute-start(bf16[1,128,640]{2,1,0:T(8,128)(2,1)S(1)} %get-tuple-element.112), channel_id=1, source_target_pairs={{0,48},{1,33},{2,50},{3,35},{4,52},{5,37},{6,54},{7,39},{8,56},{9,... | collective-permute-start | bytes 491528 | tf_op jit(solution)/shard_map/ppermute | solution.py:42
  89.2 4.6 %collective-permute-start.20 = (bf16[1,128,640]{2,1,0:T(8,128)(2,1)S(1)}, bf16[1,128,640]{2,1,0:T(8,128)(2,1)S(1)}, u32[]{:S(2)}, u32[]{:S(2)}) collective-permute-start(bf16[1,128,640]{2,1,0:T(8,128)(2,1)S(1)} %get-tuple-element.117), channel_id=1, source_target_pairs={{0,192},{1,65},{2,194},{3,67},{4,196},{5,69},{6,198},{7,71},{8,200... | collective-permute-start | bytes 491528 | tf_op jit(solution)/shard_map/ppermute | solution.py:42
  126.9 16.3 %collective-permute-start.21 = (bf16[16,16,1280]{2,1,0:T(8,128)(2,1)S(1)}, bf16[16,16,1280]{2,1,0:T(8,128)(2,1)S(1)}, u32[]{:S(2)}, u32[]{:S(2)}) collective-permute-start(bf16[16,16,1280]{2,1,0:T(8,128)(2,1)S(1)} %all_to_all.16.got.mine), channel_id=1, source_target_pairs={{0,1},{1,0},{2,3},{3,2},{4,5},{5,4},{6,7},{7,6},{8,9},{9,8},{10,11... | collective-permute-start | bytes 1966088 | tf_op jit(solution)/shard_map/ppermute | solution.py:42

commit v4 on v3

--- a/solution.py
+++ b/solution.py
@@ -379,23 +379,23 @@
     )(*made)
 
 
-def split_body(count, old, came, kept, sent):
-    part = (old[...].astype(F32) + came[...].astype(F32)).astype(BF16)
-    kept[...] = part[: count // 2]
-    sent[...] = part[count // 2 :]
-
-
-def split(old, came):
-    count = old.shape[0]
-    half = jax.ShapeDtypeStruct((count // 2, QUART, COLS), BF16)
-    return pl.pallas_call(
-        lambda *refs: split_body(count, *refs),
-        out_shape=(half, half),
-        in_specs=[VM, VM],
-        out_specs=(VM, VM),
+def add_body(parts, cuts, *refs):
+    total = sum(ref[first : first + count].astype(F32) for ref, (first, count) in zip(refs, parts)).astype(BF16)
+    for out, (first, count) in zip(refs[len(parts) :], cuts):
+        out[...] = total[first : first + count]
+
+
+def add(parts, cuts):
+    arrays, spans = [part[0] for part in parts], [part[1:] for part in parts]
+    return pl.pallas_call(
+        lambda *refs: add_body(spans, cuts, *refs),
+        out_shape=tuple(jax.ShapeDtypeStruct((count, QUART, COLS), BF16) for _, count in cuts),
+        in_specs=[VM] * len(parts),
+        out_specs=(VM,) * len(cuts),
         compiler_params=pltpu.CompilerParams(vmem_limit_bytes=6 << 20),
-        name="split",
-    )(old, came)
+        cost_estimate=pl.CostEstimate(flops=1 << 20, bytes_accessed=1 << 20, transcendentals=0),
+        name="add",
+    )(*arrays)
 
 
 def join_body(old_x, came_x, old_y, came_y, out):
@@ -521,18 +521,21 @@
     normed_own, normed_send = normed_grad(spots, (*lows[1:], *highs[1:]), pieces)
     normed_came = swap(normed_send, other_core)
     came_x, sum_x, sum_y, normed_own = lax.optimization_barrier((came_x, sum_x, sum_y, normed_own))
-    sum_x, sent_x = split(sum_x, came_x)
-    came_x = swap(sent_x, x_2)
-    sum_y, sent_y = split(sum_y, came_y)
-    came_y = swap(sent_y, y_2)
-    sent_y, normed_came = lax.optimization_barrier((sent_y, normed_came))
+    first, second = add([(sum_x, 4, 4), (came_x, 4, 4)], [(2, 2), (0, 2)])
+    pass_x, keep_x = swap(first, x_2), swap(second, x_2)
+    first, second = add([(sum_y, 4, 4), (came_y, 4, 4)], [(2, 2), (0, 2)])
+    pass_y, keep_y = swap(first, y_2), swap(second, y_2)
+    first, normed_came = lax.optimization_barrier((first, normed_came))
     d_tokens = tokens_grad(normed_own, normed_came, tokens, scale_r)
-    came_x, d_tokens = lax.optimization_barrier((came_x, d_tokens))
-    for step_x, step_y in ((y_1, x_1), (y_2, x_2)):
-        sum_x, sent_x = split(sum_x, came_x)
-        came_x = swap(sent_x, step_x)
-        sum_y, sent_y = split(sum_y, came_y)
-        came_y = swap(sent_y, step_y)
+    pass_x, d_tokens = lax.optimization_barrier((pass_x, d_tokens))
+    (sent,) = add([(sum_x, 2, 2), (came_x, 2, 2), (pass_x, 0, 2)], [(0, 2)])
+    pass_x = swap(sent, y_1)
+    (sent,) = add([(sum_y, 2, 2), (came_y, 2, 2), (pass_y, 0, 2)], [(0, 2)])
+    pass_y = swap(sent, x_1)
+    sum_x, sent = add([(sum_x, 0, 2), (came_x, 0, 2), (keep_x, 0, 2), (pass_x, 0, 2)], [(0, 1), (1, 1)])
+    came_x = swap(sent, y_2)
+    sum_y, sent = add([(sum_y, 0, 2), (came_y, 0, 2), (keep_y, 0, 2), (pass_y, 0, 2)], [(0, 1), (1, 1)])
+    came_y = swap(sent, x_2)
 
     total = join(sum_x, came_x, sum_y, came_y)
     got = finish(lax.all_to_all(total, "z", 0, 0))

time: 145 us -> 144 us (level)
  waiting for transfers between devices: 41.3 us -> 36.3 us
  starting transfers between devices: 36.9 us -> 39.4 us
  blocking collectives: 41.6 us -> 43.4 us
    ppermute x22 -> x24, waiting for transfers between devices: 41.3 us -> 36.3 us  [swap(): return lax.ppermute(value, AXES, pairs)]
    ppermute x22 -> x24, starting transfers between devices: 36.9 us -> 39.4 us  [swap(): return lax.ppermute(value, AXES, pairs)]
  transfers between devices with their start and end apart: 22 -> 24, of which waited for: 17 -> 17; matrix products, arithmetic and copies ran while one was open for 0% -> 0% of each run, Pallas kernels for 12% -> 11%
where the time goes in v4:
time: 144 us
  blocking collectives  43.4 us (30%)
  starting transfers between devices  39.4 us (27%)
  waiting for transfers between devices  36.3 us (25%)
  Pallas kernels  20.8 us (14%)
  local copies, waits for them, and re-layouts  2.98 us (2%)
    ppermute x24, starting transfers between devices, swap(): return lax.ppermute(value, AXES, pairs)  39.4 us
    ppermute x24, waiting for transfers between devices, swap(): return lax.ppermute(value, AXES, pairs)  36.3 us
    all_to_all x1, blocking collectives, on_device(): got = lax.all_to_all(got, ('y_hi', 'z'), 0, 0)  17.3 us
    all_to_all x1, blocking collectives, on_device(): got = finish(lax.all_to_all(total, 'z', 0, 0))  16.3 us
    all_to_all x1, blocking collectives, on_device(): parts = lax.all_to_all(squares(got), ('x', 'y_lo', 'core'), 0, 0)  9.77 us
    pallas_call x4, Pallas kernels, terms(): pl.pallas_call(lambda *refs: term_body(along_x, level, *refs), out_shape=...  3.91 us
    pallas_call x1, Pallas kernels, normed_grad(): pl.pallas_call(lambda *refs: normed_body(spots, *refs), out_shape=(jax.Sh...  2.98 us
    unnamed x14, local copies, waits for them, and re-layouts  2.93 us
  transfers between devices with their start and end apart: 24, of which 17 were waited for; matrix products, arithmetic and copies ran while one was open for 0% of the time, Pallas kernels for 11%

profile of v4, /device:TPU:1, one launch (start us, length us, event | category | flops | bytes accessed | tf_op | source)
XLA Modules:
  0.0 143.7 jit_solution(11198435594038382117)
XLA Ops:
  0.6 1.3 copy-done
  2.0 3.7 %collective-permute-start.1 = (bf16[256,1280]{1,0:T(8,128)(2,1)S(1)}, bf16[256,1280]{1,0:T(8,128)(2,1)S(1)}, u32[]{:S(2)}, u32[]{:S(2)}) collective-permute-start(bf16[256,1280]{1,0:T(8,128)(2,1)S(1)} %constant_dynamic-slice_fusion.refs_3_.refs_4_), channel_id=1, source_target_pairs={{0,32},{1,49},{2,34},{3,51},{4,36},{5,53},{6,38},{7,55},{8,40},{9,... | collective-permute-start | bytes 1966088 | tf_op jit(solution)/shard_map/ppermute | solution.py:42
  5.6 2.5 %collective-permute-start = (bf16[256,1280]{1,0:T(8,128)(2,1)S(1)}, bf16[256,1280]{1,0:T(8,128)(2,1)S(1)}, u32[]{:S(2)}, u32[]{:S(2)}) collective-permute-start(bf16[256,1280]{1,0:T(8,128)(2,1)S(1)} %constant_dynamic-slice_fusion.refs_3_.refs_4_), channel_id=1, source_target_pairs={{0,64},{1,193},{2,194},{3,67},{4,68},{5,197},{6,198},{7,71},{8,72}... | collective-permute-start | bytes 1966088 | tf_op jit(solution)/shard_map/ppermute | solution.py:42
  8.1 1.6 %copy-done.1 = bf16[256,4096]{1,0:T(8,128)(2,1)S(1)} copy-done((bf16[256,4096]{1,0:T(8,128)(2,1)S(1)}, bf16[256,4096]{1,0:T(8,128)(2,1)}, u32[]{:S(2)}) %copy-start.1) | copy-done | bytes 2097176
  11.4 1.4 collective-permute-done.2.refs_1_.low.refs_0_
  13.6 2.7 %collective-permute-done.refs_5_.refs_6_ = bf16[256,1280]{1,0:T(8,128)(2,1)S(1)} collective-permute-done((bf16[256,1280]{1,0:T(8,128)(2,1)S(1)}, bf16[256,1280]{1,0:T(8,128)(2,1)S(1)}, u32[]{:S(2)}, u32[]{:S(2)}) %collective-permute-start) | collective-permute-done | bytes 655392 | tf_op jit(solution)/shard_map/ppermute | solution.py:42
  17.5 7.1 %collective-permute-start.8 = (bf16[256,1280]{1,0:T(8,128)(2,1)S(1)}, bf16[256,1280]{1,0:T(8,128)(2,1)S(1)}, u32[]{:S(2)}, u32[]{:S(2)}) collective-permute-start(bf16[256,1280]{1,0:T(8,128)(2,1)S(1)} %collective-permute-done.refs_5_.refs_6_), channel_id=1, source_target_pairs={{0,2},{1,15},{2,0},{3,5},{4,6},{5,3},{6,4},{7,9},{8,10},{9,7},{10,... | collective-permute-start | bytes 1966088 | tf_op jit(solution)/shard_map/ppermute | solution.py:42
  25.3 1.2 project.2
  27.2 1.5 %collective-permute-start.6 = (bf16[256,1280]{1,0:T(8,128)(2,1)S(1)}, bf16[256,1280]{1,0:T(8,128)(2,1)S(1)}, u32[]{:S(2)}, u32[]{:S(2)}) collective-permute-start(bf16[256,1280]{1,0:T(8,128)(2,1)S(1)} %collective-permute-done.4.refs_3_.refs_7_), channel_id=1, source_target_pairs={{0,32},{1,49},{2,34},{3,51},{4,36},{5,53},{6,38},{7,55},{8,40},{9,... | collective-permute-start | bytes 1966088 | tf_op jit(solution)/shard_map/ppermute | solution.py:42
  28.7 5.6 %collective-permute-start.7 = (bf16[256,1280]{1,0:T(8,128)(2,1)S(1)}, bf16[256,1280]{1,0:T(8,128)(2,1)S(1)}, u32[]{:S(2)}, u32[]{:S(2)}) collective-permute-start(bf16[256,1280]{1,0:T(8,128)(2,1)S(1)} %collective-permute-done.5.refs_4_.refs_8_), channel_id=1, source_target_pairs={{0,2},{1,15},{2,0},{3,5},{4,6},{5,3},{6,4},{7,9},{8,10},{9,7},{10,... | collective-permute-start | bytes 1966088 | tf_op jit(solution)/shard_map/ppermute | solution.py:42
  34.3 1.2 project.3
  35.5 2.4 %collective-permute-done.6.refs_2_.refs_1_.refs_10_ = bf16[256,1280]{1,0:T(8,128)(2,1)S(1)} collective-permute-done((bf16[256,1280]{1,0:T(8,128)(2,1)S(1)}, bf16[256,1280]{1,0:T(8,128)(2,1)S(1)}, u32[]{:S(2)}, u32[]{:S(2)}) %collective-permute-start.6) | collective-permute-done | bytes 655392 | tf_op jit(solution)/shard_map/ppermute | solution.py:42
  37.9 4.4 %collective-permute-done.7.refs_3_.refs_2_.refs_11_ = bf16[256,1280]{1,0:T(8,128)(2,1)S(1)} collective-permute-done((bf16[256,1280]{1,0:T(8,128)(2,1)S(1)}, bf16[256,1280]{1,0:T(8,128)(2,1)S(1)}, u32[]{:S(2)}, u32[]{:S(2)}) %collective-permute-start.7) | collective-permute-done | bytes 655392 | tf_op jit(solution)/shard_map/ppermute | solution.py:42
  43.5 1.6 %collective-permute-done.9.came = bf16[256,1280]{1,0:T(8,128)(2,1)S(1)} collective-permute-done((bf16[256,1280]{1,0:T(8,128)(2,1)S(1)}, bf16[256,1280]{1,0:T(8,128)(2,1)S(1)}, u32[]{:S(2)}, u32[]{:S(2)}) %collective-permute-start.9) | collective-permute-done | bytes 655392 | tf_op jit(solution)/shard_map/ppermute | solution.py:42
  45.0 2.1 %attend_low.1 = (bf16[256,640]{1,0:T(8,128)(2,1)S(1)}, bf16[256,640]{1,0:T(8,128)(2,1)S(1)}, f32[256,128]{1,0:T(8,128)S(1)}, f32[256,128]{1,0:T(8,128)S(1)}) custom-call(f32[256,1280]{1,0:T(8,128)S(1)} %project_late.3.own, bf16[256,1280]{1,0:T(8,128)(2,1)S(1)} %collective-permute-done.9.came, bf16[256,1024]{1,0:T(8,128)(2,1)S(1)} %copy-done.3, ...), custom_call_target="tpu_custom_call" | custom-call | flops 419430400 | bytes 4194304 | tf_op jit(solution)/shard_map/attend_low/pallas_call | solution.py:273
  47.6 1.2 attend_high.1.refs_1_.refs_2_
  50.2 2.6 %collective-permute-start.11 = (bf16[8,128,640]{2,1,0:T(8,128)(2,1)S(1)}, bf16[8,128,640]{2,1,0:T(8,128)(2,1)S(1)}, u32[]{:S(2)}, u32[]{:S(2)}) collective-permute-start(bf16[8,128,640]{2,1,0:T(8,128)(2,1)S(1)} %terms.4), channel_id=1, source_target_pairs={{0,64},{1,193},{2,66},{3,195},{4,68},{5,197},{6,70},{7,199},{8,72}... | collective-permute-start | bytes 3932168 | tf_op jit(solution)/shard_map/ppermute | solution.py:42
  53.8 1.3 collective-permute-start.14
  55.1 3.0 %normed_grad.1 = (f32[256,2048]{1,0:T(8,128)S(1)}, bf16[256,2048]{1,0:T(8,128)(2,1)S(1)}) custom-call(bf16[256,640]{1,0:T(8,128)(2,1)S(1)} %get-tuple-element.87.refs_1_.refs_0_, bf16[256,640]{1,0:T(8,128)(2,1)S(1)} %collective-permute-done.10.refs_2_.refs_1_, bf16[256,640]{1,0:T(8,128)(2,1)S(1)} %attend_high.1.refs_1_.refs_2_, ...), custom_call_target="tpu_custom_call" | custom-call | flops 2684354560 | bytes 8388608 | tf_op jit(solution)/shard_map/normed_grad/pallas_call | solution.py:308
  60.2 7.8 %collective-permute-done.11.refs_1_ = bf16[8,128,640]{2,1,0:T(8,128)(2,1)S(1)} collective-permute-done((bf16[8,128,640]{2,1,0:T(8,128)(2,1)S(1)}, bf16[8,128,640]{2,1,0:T(8,128)(2,1)S(1)}, u32[]{:S(2)}, u32[]{:S(2)}) %collective-permute-start.11) | collective-permute-done | bytes 1310752 | tf_op jit(solution)/shard_map/ppermute | solution.py:42
  68.3 3.3 %collective-permute-done.14.refs_1_ = bf16[8,128,640]{2,1,0:T(8,128)(2,1)S(1)} collective-permute-done((bf16[8,128,640]{2,1,0:T(8,128)(2,1)S(1)}, bf16[8,128,640]{2,1,0:T(8,128)(2,1)S(1)}, u32[]{:S(2)}, u32[]{:S(2)}) %collective-permute-start.14) | collective-permute-done | bytes 1310752 | tf_op jit(solution)/shard_map/ppermute | solution.py:42
  72.2 2.7 %tokens_grad.1 = bf16[256,4096]{1,0:T(8,128)(2,1)} custom-call(f32[256,2048]{1,0:T(8,128)S(1)} %get-tuple-element.96.own, bf16[256,2048]{1,0:T(8,128)(2,1)S(1)} %collective-permute-done.15.came, bf16[256,4096]{1,0:T(8,128)(2,1)S(1)} %copy-done.2, f32[256,1]{1,0:T(8,128)S(1)} %get-tuple-element.101.scale_r), custom_call_target="tpu_custom_call" | custom-call | flops 10485760 | bytes 8388608 | tf_op jit(solution)/shard_map/tokens_grad/pallas_call | solution.py:339
  75.0 1.3 collective-permute-start.17
  78.6 5.6 %collective-permute-done.17.refs_3_ = bf16[2,128,640]{2,1,0:T(8,128)(2,1)S(1)} collective-permute-done((bf16[2,128,640]{2,1,0:T(8,128)(2,1)S(1)}, bf16[2,128,640]{2,1,0:T(8,128)(2,1)S(1)}, u32[]{:S(2)}, u32[]{:S(2)}) %collective-permute-start.17) | collective-permute-done | bytes 327712 | tf_op jit(solution)/shard_map/ppermute | solution.py:42
  85.8 1.3 collective-permute-start.22
  87.2 1.5 %collective-permute-done.18.came_x = bf16[1,128,640]{2,1,0:T(8,128)(2,1)S(1)} collective-permute-done((bf16[1,128,640]{2,1,0:T(8,128)(2,1)S(1)}, bf16[1,128,640]{2,1,0:T(8,128)(2,1)S(1)}, u32[]{:S(2)}, u32[]{:S(2)}) %collective-permute-start.18) | collective-permute-done | bytes 163872 | tf_op jit(solution)/shard_map/ppermute | solution.py:42
  88.7 1.4 collective-permute-done.22.came_y
  90.2 16.3 %all_to_all.15.parts = bf16[8,16,1280]{2,1,0:T(8,128)(2,1)S(1)} all-to-all(bf16[8,16,1280]{2,1,0:T(8,128)(2,1)S(1)} %join.1), channel_id=1, replica_groups=mesh['x'=4,'y_lo'=2,'y_hi'=2,'z'=8,'core'=2] {'z'}, dimensions={0} | all-to-all | bytes 655360 | tf_op jit(solution)/shard_map/all_to_all | solution.py:541
  106.6 17.3 %all_to_all.16.got.mine = bf16[16,16,1280]{2,1,0:T(8,128)(2,1)S(1)} all-to-all(bf16[16,16,1280]{2,1,0:T(8,128)(2,1)S(1)} %finish.1), channel_id=1, replica_groups=mesh['x'=4,'y_lo'=2,'y_hi'=2,'z'=8,'core'=2] {'y_hi','z'}, dimensions={0} | all-to-all | bytes 1310720 | tf_op jit(solution)/shard_map/all_to_all | solution.py:542
  123.8 8.4 %collective-permute-start.23 = (bf16[16,16,1280]{2,1,0:T(8,128)(2,1)S(1)}, bf16[16,16,1280]{2,1,0:T(8,128)(2,1)S(1)}, u32[]{:S(2)}, u32[]{:S(2)}) collective-permute-start(bf16[16,16,1280]{2,1,0:T(8,128)(2,1)S(1)} %all_to_all.16.got.mine), channel_id=1, source_target_pairs={{0,1},{1,0},{2,3},{3,2},{4,5},{5,4},{6,7},{7,6},{8,9},{9,8},{10,11... | collective-permute-start | bytes 1966088 | tf_op jit(solution)/shard_map/ppermute | solution.py:42
  132.4 9.8 %all_to_all.17.parts = f32[16,8,128]{2,1,0:T(8,128)S(1)} all-to-all(f32[16,8,128]{2,1,0:T(8,128)S(1)} %squares.1), channel_id=1, replica_groups=mesh['x'=4,'y_lo'=2,'y_hi'=2,'z'=8,'core'=2] {'x','y_lo','core'}, dimensions={0} | all-to-all | bytes 131072 | tf_op jit(solution)/shard_map/all_to_all | solution.py:545
  142.2 1.5 %rescale.1 = bf16[512,1280]{1,0:T(8,128)(2,1)} custom-call(f32[16,8,128]{2,1,0:T(8,128)S(1)} %all_to_all.17.parts, bf16[16,16,1280]{2,1,0:T(8,128)(2,1)S(1)} %all_to_all.16.got.mine, bf16[16,16,1280]{2,1,0:T(8,128)(2,1)S(1)} %collective-permute-done.23.theirs), custom_call_target="tpu_custom_call" | custom-call | tf_op jit(solution)/shard_map/rescale/pallas_call | solution.py:463
  (58 shorter events, 16.3 us)
Async XLA Ops:
  0.6 1.3 copy-start
  2.0 11.6 %collective-permute-start.1 = (bf16[256,1280]{1,0:T(8,128)(2,1)S(1)}, bf16[256,1280]{1,0:T(8,128)(2,1)S(1)}, u32[]{:S(2)}, u32[]{:S(2)}) collective-permute-start(bf16[256,1280]{1,0:T(8,128)(2,1)S(1)} %constant_dynamic-slice_fusion.refs_3_.refs_4_), channel_id=1, source_target_pairs={{0,32},{1,49},{2,34},{3,51},{4,36},{5,53},{6,38},{7,55},{8,40},{9,... | collective-permute-start | bytes 1966088 | tf_op jit(solution)/shard_map/ppermute | solution.py:42
  5.6 10.6 %collective-permute-start = (bf16[256,1280]{1,0:T(8,128)(2,1)S(1)}, bf16[256,1280]{1,0:T(8,128)(2,1)S(1)}, u32[]{:S(2)}, u32[]{:S(2)}) collective-permute-start(bf16[256,1280]{1,0:T(8,128)(2,1)S(1)} %constant_dynamic-slice_fusion.refs_3_.refs_4_), channel_id=1, source_target_pairs={{0,64},{1,193},{2,194},{3,67},{4,68},{5,197},{6,198},{7,71},{8,72}... | collective-permute-start | bytes 1966088 | tf_op jit(solution)/shard_map/ppermute | solution.py:42
  8.1 1.6 %copy-start.1 = (bf16[256,4096]{1,0:T(8,128)(2,1)S(1)}, bf16[256,4096]{1,0:T(8,128)(2,1)}, u32[]{:S(2)}) copy-start(bf16[256,4096]{1,0:T(8,128)(2,1)} %tokens.1) | copy-start | bytes 6291460
  10.8 2.0 %collective-permute-start.2 = (bf16[128,2048]{1,0:T(8,128)(2,1)S(1)}, bf16[128,2048]{1,0:T(8,128)(2,1)S(1)}, u32[]{:S(2)}, u32[]{:S(2)}) collective-permute-start(bf16[128,2048]{1,0:T(8,128)(2,1)S(1)} %get-tuple-element.59), channel_id=1, source_target_pairs={{0,1},{1,0},{2,3},{3,2},{4,5},{5,4},{6,7},{7,6},{8,9},{9,8},{10,11... | collective-permute-start | bytes 1572872 | tf_op jit(solution)/shard_map/ppermute | solution.py:42
  10.9 2.6 %collective-permute-start.3 = (bf16[128,2048]{1,0:T(8,128)(2,1)S(1)}, bf16[128,2048]{1,0:T(8,128)(2,1)S(1)}, u32[]{:S(2)}, u32[]{:S(2)}) collective-permute-start(bf16[128,2048]{1,0:T(8,128)(2,1)S(1)} %get-tuple-element.60), channel_id=1, source_target_pairs={{0,1},{1,0},{2,3},{3,2},{4,5},{5,4},{6,7},{7,6},{8,9},{9,8},{10,11... | collective-permute-start | bytes 1572872 | tf_op jit(solution)/shard_map/ppermute | solution.py:42
  16.3 10.9 %collective-permute-start.5 = (bf16[256,1280]{1,0:T(8,128)(2,1)S(1)}, bf16[256,1280]{1,0:T(8,128)(2,1)S(1)}, u32[]{:S(2)}, u32[]{:S(2)}) collective-permute-start(bf16[256,1280]{1,0:T(8,128)(2,1)S(1)} %collective-permute-done.refs_5_.refs_6_), channel_id=1, source_target_pairs={{0,32},{1,49},{2,34},{3,51},{4,36},{5,53},{6,38},{7,55},{8,40},{9,... | collective-permute-start | bytes 1966088 | tf_op jit(solution)/shard_map/ppermute | solution.py:42
  16.4 10.8 %collective-permute-start.4 = (bf16[256,1280]{1,0:T(8,128)(2,1)S(1)}, bf16[256,1280]{1,0:T(8,128)(2,1)S(1)}, u32[]{:S(2)}, u32[]{:S(2)}) collective-permute-start(bf16[256,1280]{1,0:T(8,128)(2,1)S(1)} %collective-permute-done.refs_5_.refs_6_), channel_id=1, source_target_pairs={{0,192},{1,65},{2,66},{3,195},{4,196},{5,69},{6,70},{7,199},{8,200... | collective-permute-start | bytes 1966088 | tf_op jit(solution)/shard_map/ppermute | solution.py:42
  17.5 16.8 %collective-permute-start.8 = (bf16[256,1280]{1,0:T(8,128)(2,1)S(1)}, bf16[256,1280]{1,0:T(8,128)(2,1)S(1)}, u32[]{:S(2)}, u32[]{:S(2)}) collective-permute-start(bf16[256,1280]{1,0:T(8,128)(2,1)S(1)} %collective-permute-done.refs_5_.refs_6_), channel_id=1, source_target_pairs={{0,2},{1,15},{2,0},{3,5},{4,6},{5,3},{6,4},{7,9},{8,10},{9,7},{10,... | collective-permute-start | bytes 1966088 | tf_op jit(solution)/shard_map/ppermute | solution.py:42
  27.2 10.6 %collective-permute-start.6 = (bf16[256,1280]{1,0:T(8,128)(2,1)S(1)}, bf16[256,1280]{1,0:T(8,128)(2,1)S(1)}, u32[]{:S(2)}, u32[]{:S(2)}) collective-permute-start(bf16[256,1280]{1,0:T(8,128)(2,1)S(1)} %collective-permute-done.4.refs_3_.refs_7_), channel_id=1, source_target_pairs={{0,32},{1,49},{2,34},{3,51},{4,36},{5,53},{6,38},{7,55},{8,40},{9,... | collective-permute-start | bytes 1966088 | tf_op jit(solution)/shard_map/ppermute | solution.py:42
  28.7 13.5 %collective-permute-start.7 = (bf16[256,1280]{1,0:T(8,128)(2,1)S(1)}, bf16[256,1280]{1,0:T(8,128)(2,1)S(1)}, u32[]{:S(2)}, u32[]{:S(2)}) collective-permute-start(bf16[256,1280]{1,0:T(8,128)(2,1)S(1)} %collective-permute-done.5.refs_4_.refs_8_), channel_id=1, source_target_pairs={{0,2},{1,15},{2,0},{3,5},{4,6},{5,3},{6,4},{7,9},{8,10},{9,7},{10,... | collective-permute-start | bytes 1966088 | tf_op jit(solution)/shard_map/ppermute | solution.py:42
  42.8 2.2 %copy-start.3 = (bf16[256,1024]{1,0:T(8,128)(2,1)S(1)}, bf16[256,1024]{1,0:T(8,128)(2,1)}, u32[]{:S(2)}) copy-start(bf16[256,1024]{1,0:T(8,128)(2,1)} %grad.3) | copy-start | bytes 1572868
  42.8 2.2 %copy-start.4 = (f32[256,128]{1,0:T(8,128)S(1)}, f32[256,128]{1,0:T(8,128)}, u32[]{:S(2)}) copy-start(f32[256,128]{1,0:T(8,128)} %constant.15.clone.sine) | copy-start | bytes 393220
  42.8 2.2 %copy-start.5 = (f32[256,128]{1,0:T(8,128)S(1)}, f32[256,128]{1,0:T(8,128)}, u32[]{:S(2)}) copy-start(f32[256,128]{1,0:T(8,128)} %constant.14.clone.cosine) | copy-start | bytes 393220
  42.8 2.2 %copy-start.6 = (s32[1,256]{1,0:T(1,128)S(1)}, s32[1,256]{1,0:T(1,128)}, u32[]{:S(2)}) copy-start(s32[1,256]{1,0:T(1,128)} %doc.3) | copy-start | bytes 3076
  42.8 2.2 %collective-permute-start.9 = (bf16[256,1280]{1,0:T(8,128)(2,1)S(1)}, bf16[256,1280]{1,0:T(8,128)(2,1)S(1)}, u32[]{:S(2)}, u32[]{:S(2)}) collective-permute-start(bf16[256,1280]{1,0:T(8,128)(2,1)S(1)} %project_late.2), channel_id=1, source_target_pairs={{0,1},{1,0},{2,3},{3,2},{4,5},{5,4},{6,7},{7,6},{8,9},{9,8},{10,11... | collective-permute-start | bytes 1966088 | tf_op jit(solution)/shard_map/ppermute | solution.py:42
  47.2 1.9 %collective-permute-start.10 = (bf16[256,640]{1,0:T(8,128)(2,1)S(1)}, bf16[256,640]{1,0:T(8,128)(2,1)S(1)}, u32[]{:S(2)}, u32[]{:S(2)}) collective-permute-start(bf16[256,640]{1,0:T(8,128)(2,1)S(1)} %get-tuple-element.87.refs_1_.refs_0_), channel_id=1, source_target_pairs={{0,1},{1,0},{2,3},{3,2},{4,5},{5,4},{6,7},{7,6},{8,9},{9,8},{10,11... | collective-permute-start | bytes 983048 | tf_op jit(solution)/shard_map/ppermute | solution.py:42
  49.1 3.7 %collective-permute-start.12 = (bf16[256,640]{1,0:T(8,128)(2,1)S(1)}, bf16[256,640]{1,0:T(8,128)(2,1)S(1)}, u32[]{:S(2)}, u32[]{:S(2)}) collective-permute-start(bf16[256,640]{1,0:T(8,128)(2,1)S(1)} %attend_high.1.refs_1_.refs_2_), channel_id=1, source_target_pairs={{0,1},{1,0},{2,3},{3,2},{4,5},{5,4},{6,7},{7,6},{8,9},{9,8},{10,11... | collective-permute-start | bytes 983048 | tf_op jit(solution)/shard_map/ppermute | solution.py:42
  50.2 17.8 %collective-permute-start.11 = (bf16[8,128,640]{2,1,0:T(8,128)(2,1)S(1)}, bf16[8,128,640]{2,1,0:T(8,128)(2,1)S(1)}, u32[]{:S(2)}, u32[]{:S(2)}) collective-permute-start(bf16[8,128,640]{2,1,0:T(8,128)(2,1)S(1)} %terms.4), channel_id=1, source_target_pairs={{0,64},{1,193},{2,66},{3,195},{4,68},{5,197},{6,70},{7,199},{8,72}... | collective-permute-start | bytes 3932168 | tf_op jit(solution)/shard_map/ppermute | solution.py:42
  53.8 17.8 %collective-permute-start.14 = (bf16[8,128,640]{2,1,0:T(8,128)(2,1)S(1)}, bf16[8,128,640]{2,1,0:T(8,128)(2,1)S(1)}, u32[]{:S(2)}, u32[]{:S(2)}) collective-permute-start(bf16[8,128,640]{2,1,0:T(8,128)(2,1)S(1)} %terms.5), channel_id=1, source_target_pairs={{0,32},{1,49},{2,34},{3,51},{4,36},{5,53},{6,38},{7,55},{8,40},{9,... | collective-permute-start | bytes 3932168 | tf_op jit(solution)/shard_map/ppermute | solution.py:42
  58.1 14.0 %collective-permute-start.15 = (bf16[256,2048]{1,0:T(8,128)(2,1)S(1)}, bf16[256,2048]{1,0:T(8,128)(2,1)S(1)}, u32[]{:S(2)}, u32[]{:S(2)}) collective-permute-start(bf16[256,2048]{1,0:T(8,128)(2,1)S(1)} %get-tuple-element.99), channel_id=1, source_target_pairs={{0,1},{1,0},{2,3},{3,2},{4,5},{5,4},{6,7},{7,6},{8,9},{9,8},{10,11... | collective-permute-start | bytes 3145736 | tf_op jit(solution)/shard_map/ppermute | solution.py:42
  68.2 4.0 %copy-start.2 = (bf16[256,4096]{1,0:T(8,128)(2,1)S(1)}, bf16[256,4096]{1,0:T(8,128)(2,1)}, u32[]{:S(2)}) copy-start(bf16[256,4096]{1,0:T(8,128)(2,1)} %tokens.1) | copy-start | bytes 6291460
  68.2 6.7 %collective-permute-start.13 = (bf16[2,128,640]{2,1,0:T(8,128)(2,1)S(1)}, bf16[2,128,640]{2,1,0:T(8,128)(2,1)S(1)}, u32[]{:S(2)}, u32[]{:S(2)}) collective-permute-start(bf16[2,128,640]{2,1,0:T(8,128)(2,1)S(1)} %get-tuple-element.95), channel_id=1, source_target_pairs={{0,192},{1,65},{2,194},{3,67},{4,196},{5,69},{6,198},{7,71},{8,200... | collective-permute-start | bytes 983048 | tf_op jit(solution)/shard_map/ppermute | solution.py:42
  71.7 6.3 %collective-permute-start.20 = (bf16[2,128,640]{2,1,0:T(8,128)(2,1)S(1)}, bf16[2,128,640]{2,1,0:T(8,128)(2,1)S(1)}, u32[]{:S(2)}, u32[]{:S(2)}) collective-permute-start(bf16[2,128,640]{2,1,0:T(8,128)(2,1)S(1)} %get-tuple-element.98), channel_id=1, source_target_pairs={{0,48},{1,33},{2,50},{3,35},{4,52},{5,37},{6,54},{7,39},{8,56},{9,... | collective-permute-start | bytes 983048 | tf_op jit(solution)/shard_map/ppermute | solution.py:42
  71.8 6.8 %collective-permute-start.16 = (bf16[2,128,640]{2,1,0:T(8,128)(2,1)S(1)}, bf16[2,128,640]{2,1,0:T(8,128)(2,1)S(1)}, u32[]{:S(2)}, u32[]{:S(2)}) collective-permute-start(bf16[2,128,640]{2,1,0:T(8,128)(2,1)S(1)} %get-tuple-element.103), channel_id=1, source_target_pairs={{0,192},{1,65},{2,194},{3,67},{4,196},{5,69},{6,198},{7,71},{8,200... | collective-permute-start | bytes 983048 | tf_op jit(solution)/shard_map/ppermute | solution.py:42
  75.0 9.2 %collective-permute-start.17 = (bf16[2,128,640]{2,1,0:T(8,128)(2,1)S(1)}, bf16[2,128,640]{2,1,0:T(8,128)(2,1)S(1)}, u32[]{:S(2)}, u32[]{:S(2)}) collective-permute-start(bf16[2,128,640]{2,1,0:T(8,128)(2,1)S(1)} %add.12), channel_id=1, source_target_pairs={{0,32},{1,49},{2,34},{3,51},{4,36},{5,53},{6,38},{7,55},{8,40},{9,... | collective-permute-start | bytes 983048 | tf_op jit(solution)/shard_map/ppermute | solution.py:42
  76.3 8.5 %collective-permute-start.19 = (bf16[2,128,640]{2,1,0:T(8,128)(2,1)S(1)}, bf16[2,128,640]{2,1,0:T(8,128)(2,1)S(1)}, u32[]{:S(2)}, u32[]{:S(2)}) collective-permute-start(bf16[2,128,640]{2,1,0:T(8,128)(2,1)S(1)} %get-tuple-element.107), channel_id=1, source_target_pairs={{0,48},{1,33},{2,50},{3,35},{4,52},{5,37},{6,54},{7,39},{8,56},{9,... | collective-permute-start | bytes 983048 | tf_op jit(solution)/shard_map/ppermute | solution.py:42
  78.1 7.5 %collective-permute-start.21 = (bf16[2,128,640]{2,1,0:T(8,128)(2,1)S(1)}, bf16[2,128,640]{2,1,0:T(8,128)(2,1)S(1)}, u32[]{:S(2)}, u32[]{:S(2)}) collective-permute-start(bf16[2,128,640]{2,1,0:T(8,128)(2,1)S(1)} %add.14), channel_id=1, source_target_pairs={{0,64},{1,193},{2,66},{3,195},{4,68},{5,197},{6,70},{7,199},{8,72}... | collective-permute-start | bytes 983048 | tf_op jit(solution)/shard_map/ppermute | solution.py:42
  84.4 4.3 %collective-permute-start.18 = (bf16[1,128,640]{2,1,0:T(8,128)(2,1)S(1)}, bf16[1,128,640]{2,1,0:T(8,128)(2,1)S(1)}, u32[]{:S(2)}, u32[]{:S(2)}) collective-permute-start(bf16[1,128,640]{2,1,0:T(8,128)(2,1)S(1)} %get-tuple-element.106), channel_id=1, source_target_pairs={{0,48},{1,33},{2,50},{3,35},{4,52},{5,37},{6,54},{7,39},{8,56},{9,... | collective-permute-start | bytes 491528 | tf_op jit(solution)/shard_map/ppermute | solution.py:42
  85.8 4.3 %collective-permute-start.22 = (bf16[1,128,640]{2,1,0:T(8,128)(2,1)S(1)}, bf16[1,128,640]{2,1,0:T(8,128)(2,1)S(1)}, u32[]{:S(2)}, u32[]{:S(2)}) collective-permute-start(bf16[1,128,640]{2,1,0:T(8,128)(2,1)S(1)} %get-tuple-element.109), channel_id=1, source_target_pairs={{0,192},{1,65},{2,194},{3,67},{4,196},{5,69},{6,198},{7,71},{8,200... | collective-permute-start | bytes 491528 | tf_op jit(solution)/shard_map/ppermute | solution.py:42
  123.8 18.4 %collective-permute-start.23 = (bf16[16,16,1280]{2,1,0:T(8,128)(2,1)S(1)}, bf16[16,16,1280]{2,1,0:T(8,128)(2,1)S(1)}, u32[]{:S(2)}, u32[]{:S(2)}) collective-permute-start(bf16[16,16,1280]{2,1,0:T(8,128)(2,1)S(1)} %all_to_all.16.got.mine), channel_id=1, source_target_pairs={{0,1},{1,0},{2,3},{3,2},{4,5},{5,4},{6,7},{7,6},{8,9},{9,8},{10,11... | collective-permute-start | bytes 1966088 | tf_op jit(solution)/shard_map/ppermute | solution.py:42

commit v5 on v4

--- a/solution.py
+++ b/solution.py
@@ -432,12 +432,13 @@
 
 
 def squares_body(got, out):
-    total = jnp.zeros((PIECE, QKV), F32)
+    total = jnp.zeros((PIECE, 128), F32)
     for i in range(16):
         value = got[i].astype(F32)
-        total = total + value * value
-    total = jnp.sum(jnp.sum(total, axis=1, keepdims=True), axis=0, keepdims=True)
-    out[...] = jnp.broadcast_to(total.reshape(1, 1, 1), (16, 8, 128))
+        value = value * value
+        for k in range(0, QKV, 128):
+            total = total + value[:, k : k + 128]
+    out[...] = jnp.broadcast_to((total[:8] + total[8:])[None], (16, 8, 128))
 
 
 def squares(got):
@@ -451,12 +452,22 @@
     )(got)
 
 
-def rescale_body(parts, mine, theirs, out):
+def rescale_body(parts, mine, theirs, out, held, sems):
     total = sum(parts[i] for i in range(16))
-    factor = (target_rms * lax.rsqrt(total * (1.0 / (D * QKV)) + 1e-06))[:1, :1]
+    total = jnp.sum(jnp.sum(total, axis=1, keepdims=True), axis=0, keepdims=True)
+    factor = target_rms * lax.rsqrt(total * (1.0 / (D * QKV)) + 1e-06)
     c = lax.axis_index("core")
+    copies = []
     for side, half in ((c, mine), (1 - c, theirs)):
-        out[aligned(side * HALF, HALF), :] = (half[...].reshape(HALF, QKV).astype(F32) * factor).astype(BF16)
+        for k in range(2):
+            i = len(copies)
+            part = half[8 * k : 8 * (k + 1)].reshape(QUART, QKV)
+            held[i] = (part.astype(F32) * factor).astype(BF16)
+            rows = aligned(side * HALF + k * QUART, QUART)
+            copies.append(pltpu.make_async_copy(held.at[i], out.at[rows, :], sems.at[i]))
+            copies[-1].start()
+    for copy in copies:
+        copy.wait()
 
 
 def rescale(parts, mine, theirs):
@@ -464,7 +475,8 @@
         rescale_body,
         out_shape=jax.ShapeDtypeStruct((BLK, QKV), BF16),
         in_specs=[VM] * 3,
-        out_specs=VM,
+        out_specs=pl.BlockSpec(memory_space=pl.ANY),
+        scratch_shapes=[pltpu.VMEM((4, QUART, QKV), BF16), pltpu.SemaphoreType.DMA((4,))],
         compiler_params=pltpu.CompilerParams(vmem_limit_bytes=8 << 20),
         name="rescale",
     )(parts, mine, theirs)

time: 144 us -> 144 us (level)
  no operation moved by 1% of the time
where the time goes in v5:
time: 144 us
  blocking collectives  43.4 us (30%)
  starting transfers between devices  39.4 us (27%)
  waiting for transfers between devices  36.3 us (25%)
  Pallas kernels  20.5 us (14%)
  local copies, waits for them, and re-layouts  2.98 us (2%)
    ppermute x24, starting transfers between devices, swap(): return lax.ppermute(value, AXES, pairs)  39.4 us
    ppermute x24, waiting for transfers between devices, swap(): return lax.ppermute(value, AXES, pairs)  36.3 us
    all_to_all x1, blocking collectives, on_device(): got = lax.all_to_all(got, ('y_hi', 'z'), 0, 0)  17.3 us
    all_to_all x1, blocking collectives, on_device(): got = finish(lax.all_to_all(total, 'z', 0, 0))  16.3 us
    all_to_all x1, blocking collectives, on_device(): parts = lax.all_to_all(squares(got), ('x', 'y_lo', 'core'), 0, 0)  9.78 us
    pallas_call x4, Pallas kernels, terms(): pl.pallas_call(lambda *refs: term_body(along_x, level, *refs), out_shape=...  3.91 us
    pallas_call x1, Pallas kernels, normed_grad(): pl.pallas_call(lambda *refs: normed_body(spots, *refs), out_shape=(jax.Sh...  2.98 us
    unnamed x14, local copies, waits for them, and re-layouts  2.93 us
  transfers between devices with their start and end apart: 24, of which 17 were waited for; matrix products, arithmetic and copies ran while one was open for 0% of the time, Pallas kernels for 11%

profile of v5, /device:TPU:1, one launch (start us, length us, event | category | flops | bytes accessed | tf_op | source)
XLA Modules:
  0.0 143.7 jit_solution(12699498724501145076)
XLA Ops:
  0.6 1.3 copy-done
  2.0 3.7 %collective-permute-start.1 = (bf16[256,1280]{1,0:T(8,128)(2,1)S(1)}, bf16[256,1280]{1,0:T(8,128)(2,1)S(1)}, u32[]{:S(2)}, u32[]{:S(2)}) collective-permute-start(bf16[256,1280]{1,0:T(8,128)(2,1)S(1)} %constant_dynamic-slice_fusion.refs_3_.refs_4_), channel_id=1, source_target_pairs={{0,32},{1,49},{2,34},{3,51},{4,36},{5,53},{6,38},{7,55},{8,40},{9,... | collective-permute-start | bytes 1966088 | tf_op jit(solution)/shard_map/ppermute | solution.py:42
  5.6 2.5 %collective-permute-start = (bf16[256,1280]{1,0:T(8,128)(2,1)S(1)}, bf16[256,1280]{1,0:T(8,128)(2,1)S(1)}, u32[]{:S(2)}, u32[]{:S(2)}) collective-permute-start(bf16[256,1280]{1,0:T(8,128)(2,1)S(1)} %constant_dynamic-slice_fusion.refs_3_.refs_4_), channel_id=1, source_target_pairs={{0,64},{1,193},{2,194},{3,67},{4,68},{5,197},{6,198},{7,71},{8,72}... | collective-permute-start | bytes 1966088 | tf_op jit(solution)/shard_map/ppermute | solution.py:42
  8.1 1.6 %copy-done.1 = bf16[256,4096]{1,0:T(8,128)(2,1)S(1)} copy-done((bf16[256,4096]{1,0:T(8,128)(2,1)S(1)}, bf16[256,4096]{1,0:T(8,128)(2,1)}, u32[]{:S(2)}) %copy-start.1) | copy-done | bytes 2097176
  11.4 1.4 collective-permute-done.2.refs_1_.low.refs_0_
  13.6 2.7 %collective-permute-done.refs_5_.refs_6_ = bf16[256,1280]{1,0:T(8,128)(2,1)S(1)} collective-permute-done((bf16[256,1280]{1,0:T(8,128)(2,1)S(1)}, bf16[256,1280]{1,0:T(8,128)(2,1)S(1)}, u32[]{:S(2)}, u32[]{:S(2)}) %collective-permute-start) | collective-permute-done | bytes 655392 | tf_op jit(solution)/shard_map/ppermute | solution.py:42
  17.5 7.1 %collective-permute-start.8 = (bf16[256,1280]{1,0:T(8,128)(2,1)S(1)}, bf16[256,1280]{1,0:T(8,128)(2,1)S(1)}, u32[]{:S(2)}, u32[]{:S(2)}) collective-permute-start(bf16[256,1280]{1,0:T(8,128)(2,1)S(1)} %collective-permute-done.refs_5_.refs_6_), channel_id=1, source_target_pairs={{0,2},{1,15},{2,0},{3,5},{4,6},{5,3},{6,4},{7,9},{8,10},{9,7},{10,... | collective-permute-start | bytes 1966088 | tf_op jit(solution)/shard_map/ppermute | solution.py:42
  25.3 1.2 project.2
  27.2 1.5 %collective-permute-start.6 = (bf16[256,1280]{1,0:T(8,128)(2,1)S(1)}, bf16[256,1280]{1,0:T(8,128)(2,1)S(1)}, u32[]{:S(2)}, u32[]{:S(2)}) collective-permute-start(bf16[256,1280]{1,0:T(8,128)(2,1)S(1)} %collective-permute-done.4.refs_3_.refs_7_), channel_id=1, source_target_pairs={{0,32},{1,49},{2,34},{3,51},{4,36},{5,53},{6,38},{7,55},{8,40},{9,... | collective-permute-start | bytes 1966088 | tf_op jit(solution)/shard_map/ppermute | solution.py:42
  28.7 5.6 %collective-permute-start.7 = (bf16[256,1280]{1,0:T(8,128)(2,1)S(1)}, bf16[256,1280]{1,0:T(8,128)(2,1)S(1)}, u32[]{:S(2)}, u32[]{:S(2)}) collective-permute-start(bf16[256,1280]{1,0:T(8,128)(2,1)S(1)} %collective-permute-done.5.refs_4_.refs_8_), channel_id=1, source_target_pairs={{0,2},{1,15},{2,0},{3,5},{4,6},{5,3},{6,4},{7,9},{8,10},{9,7},{10,... | collective-permute-start | bytes 1966088 | tf_op jit(solution)/shard_map/ppermute | solution.py:42
  34.3 1.2 project.3
  35.5 2.4 %collective-permute-done.6.refs_2_.refs_1_.refs_10_ = bf16[256,1280]{1,0:T(8,128)(2,1)S(1)} collective-permute-done((bf16[256,1280]{1,0:T(8,128)(2,1)S(1)}, bf16[256,1280]{1,0:T(8,128)(2,1)S(1)}, u32[]{:S(2)}, u32[]{:S(2)}) %collective-permute-start.6) | collective-permute-done | bytes 655392 | tf_op jit(solution)/shard_map/ppermute | solution.py:42
  37.9 4.4 %collective-permute-done.7.refs_3_.refs_2_.refs_11_ = bf16[256,1280]{1,0:T(8,128)(2,1)S(1)} collective-permute-done((bf16[256,1280]{1,0:T(8,128)(2,1)S(1)}, bf16[256,1280]{1,0:T(8,128)(2,1)S(1)}, u32[]{:S(2)}, u32[]{:S(2)}) %collective-permute-start.7) | collective-permute-done | bytes 655392 | tf_op jit(solution)/shard_map/ppermute | solution.py:42
  43.5 1.6 %collective-permute-done.9.came = bf16[256,1280]{1,0:T(8,128)(2,1)S(1)} collective-permute-done((bf16[256,1280]{1,0:T(8,128)(2,1)S(1)}, bf16[256,1280]{1,0:T(8,128)(2,1)S(1)}, u32[]{:S(2)}, u32[]{:S(2)}) %collective-permute-start.9) | collective-permute-done | bytes 655392 | tf_op jit(solution)/shard_map/ppermute | solution.py:42
  45.0 2.1 %attend_low.1 = (bf16[256,640]{1,0:T(8,128)(2,1)S(1)}, bf16[256,640]{1,0:T(8,128)(2,1)S(1)}, f32[256,128]{1,0:T(8,128)S(1)}, f32[256,128]{1,0:T(8,128)S(1)}) custom-call(f32[256,1280]{1,0:T(8,128)S(1)} %project_late.3.own, bf16[256,1280]{1,0:T(8,128)(2,1)S(1)} %collective-permute-done.9.came, bf16[256,1024]{1,0:T(8,128)(2,1)S(1)} %copy-done.3, ...), custom_call_target="tpu_custom_call" | custom-call | flops 419430400 | bytes 4194304 | tf_op jit(solution)/shard_map/attend_low/pallas_call | solution.py:273
  47.6 1.2 attend_high.1.refs_1_.refs_2_
  50.2 2.6 %collective-permute-start.11 = (bf16[8,128,640]{2,1,0:T(8,128)(2,1)S(1)}, bf16[8,128,640]{2,1,0:T(8,128)(2,1)S(1)}, u32[]{:S(2)}, u32[]{:S(2)}) collective-permute-start(bf16[8,128,640]{2,1,0:T(8,128)(2,1)S(1)} %terms.4), channel_id=1, source_target_pairs={{0,64},{1,193},{2,66},{3,195},{4,68},{5,197},{6,70},{7,199},{8,72}... | collective-permute-start | bytes 3932168 | tf_op jit(solution)/shard_map/ppermute | solution.py:42
  53.8 1.3 collective-permute-start.14
  55.1 3.0 %normed_grad.1 = (f32[256,2048]{1,0:T(8,128)S(1)}, bf16[256,2048]{1,0:T(8,128)(2,1)S(1)}) custom-call(bf16[256,640]{1,0:T(8,128)(2,1)S(1)} %get-tuple-element.87.refs_1_.refs_0_, bf16[256,640]{1,0:T(8,128)(2,1)S(1)} %collective-permute-done.10.refs_2_.refs_1_, bf16[256,640]{1,0:T(8,128)(2,1)S(1)} %attend_high.1.refs_1_.refs_2_, ...), custom_call_target="tpu_custom_call" | custom-call | flops 2684354560 | bytes 8388608 | tf_op jit(solution)/shard_map/normed_grad/pallas_call | solution.py:308
  60.2 7.8 %collective-permute-done.11.refs_1_ = bf16[8,128,640]{2,1,0:T(8,128)(2,1)S(1)} collective-permute-done((bf16[8,128,640]{2,1,0:T(8,128)(2,1)S(1)}, bf16[8,128,640]{2,1,0:T(8,128)(2,1)S(1)}, u32[]{:S(2)}, u32[]{:S(2)}) %collective-permute-start.11) | collective-permute-done | bytes 1310752 | tf_op jit(solution)/shard_map/ppermute | solution.py:42
  68.3 3.3 %collective-permute-done.14.refs_1_ = bf16[8,128,640]{2,1,0:T(8,128)(2,1)S(1)} collective-permute-done((bf16[8,128,640]{2,1,0:T(8,128)(2,1)S(1)}, bf16[8,128,640]{2,1,0:T(8,128)(2,1)S(1)}, u32[]{:S(2)}, u32[]{:S(2)}) %collective-permute-start.14) | collective-permute-done | bytes 1310752 | tf_op jit(solution)/shard_map/ppermute | solution.py:42
  72.2 2.7 %tokens_grad.1 = bf16[256,4096]{1,0:T(8,128)(2,1)} custom-call(f32[256,2048]{1,0:T(8,128)S(1)} %get-tuple-element.96.own, bf16[256,2048]{1,0:T(8,128)(2,1)S(1)} %collective-permute-done.15.came, bf16[256,4096]{1,0:T(8,128)(2,1)S(1)} %copy-done.2, f32[256,1]{1,0:T(8,128)S(1)} %get-tuple-element.101.scale_r), custom_call_target="tpu_custom_call" | custom-call | flops 10485760 | bytes 8388608 | tf_op jit(solution)/shard_map/tokens_grad/pallas_call | solution.py:339
  75.0 1.3 collective-permute-start.17
  78.6 5.6 %collective-permute-done.17.refs_3_ = bf16[2,128,640]{2,1,0:T(8,128)(2,1)S(1)} collective-permute-done((bf16[2,128,640]{2,1,0:T(8,128)(2,1)S(1)}, bf16[2,128,640]{2,1,0:T(8,128)(2,1)S(1)}, u32[]{:S(2)}, u32[]{:S(2)}) %collective-permute-start.17) | collective-permute-done | bytes 327712 | tf_op jit(solution)/shard_map/ppermute | solution.py:42
  85.8 1.3 collective-permute-start.22
  87.2 1.5 %collective-permute-done.18.came_x = bf16[1,128,640]{2,1,0:T(8,128)(2,1)S(1)} collective-permute-done((bf16[1,128,640]{2,1,0:T(8,128)(2,1)S(1)}, bf16[1,128,640]{2,1,0:T(8,128)(2,1)S(1)}, u32[]{:S(2)}, u32[]{:S(2)}) %collective-permute-start.18) | collective-permute-done | bytes 163872 | tf_op jit(solution)/shard_map/ppermute | solution.py:42
  88.7 1.4 collective-permute-done.22.came_y
  90.2 16.3 %all_to_all.15.parts = bf16[8,16,1280]{2,1,0:T(8,128)(2,1)S(1)} all-to-all(bf16[8,16,1280]{2,1,0:T(8,128)(2,1)S(1)} %join.1), channel_id=1, replica_groups=mesh['x'=4,'y_lo'=2,'y_hi'=2,'z'=8,'core'=2] {'z'}, dimensions={0} | all-to-all | bytes 655360 | tf_op jit(solution)/shard_map/all_to_all | solution.py:553
  106.6 17.3 %all_to_all.16.got.mine = bf16[16,16,1280]{2,1,0:T(8,128)(2,1)S(1)} all-to-all(bf16[16,16,1280]{2,1,0:T(8,128)(2,1)S(1)} %finish.1), channel_id=1, replica_groups=mesh['x'=4,'y_lo'=2,'y_hi'=2,'z'=8,'core'=2] {'y_hi','z'}, dimensions={0} | all-to-all | bytes 1310720 | tf_op jit(solution)/shard_map/all_to_all | solution.py:554
  123.8 8.4 %collective-permute-start.23 = (bf16[16,16,1280]{2,1,0:T(8,128)(2,1)S(1)}, bf16[16,16,1280]{2,1,0:T(8,128)(2,1)S(1)}, u32[]{:S(2)}, u32[]{:S(2)}) collective-permute-start(bf16[16,16,1280]{2,1,0:T(8,128)(2,1)S(1)} %all_to_all.16.got.mine), channel_id=1, source_target_pairs={{0,1},{1,0},{2,3},{3,2},{4,5},{5,4},{6,7},{7,6},{8,9},{9,8},{10,11... | collective-permute-start | bytes 1966088 | tf_op jit(solution)/shard_map/ppermute | solution.py:42
  132.4 9.8 %all_to_all.17.parts = f32[16,8,128]{2,1,0:T(8,128)S(1)} all-to-all(f32[16,8,128]{2,1,0:T(8,128)S(1)} %squares.1), channel_id=1, replica_groups=mesh['x'=4,'y_lo'=2,'y_hi'=2,'z'=8,'core'=2] {'x','y_lo','core'}, dimensions={0} | all-to-all | bytes 131072 | tf_op jit(solution)/shard_map/all_to_all | solution.py:557
  142.2 1.3 rescale.1
  (58 shorter events, 16.3 us)
Async XLA Ops:
  0.6 1.3 copy-start
  2.0 11.6 %collective-permute-start.1 = (bf16[256,1280]{1,0:T(8,128)(2,1)S(1)}, bf16[256,1280]{1,0:T(8,128)(2,1)S(1)}, u32[]{:S(2)}, u32[]{:S(2)}) collective-permute-start(bf16[256,1280]{1,0:T(8,128)(2,1)S(1)} %constant_dynamic-slice_fusion.refs_3_.refs_4_), channel_id=1, source_target_pairs={{0,32},{1,49},{2,34},{3,51},{4,36},{5,53},{6,38},{7,55},{8,40},{9,... | collective-permute-start | bytes 1966088 | tf_op jit(solution)/shard_map/ppermute | solution.py:42
  5.6 10.6 %collective-permute-start = (bf16[256,1280]{1,0:T(8,128)(2,1)S(1)}, bf16[256,1280]{1,0:T(8,128)(2,1)S(1)}, u32[]{:S(2)}, u32[]{:S(2)}) collective-permute-start(bf16[256,1280]{1,0:T(8,128)(2,1)S(1)} %constant_dynamic-slice_fusion.refs_3_.refs_4_), channel_id=1, source_target_pairs={{0,64},{1,193},{2,194},{3,67},{4,68},{5,197},{6,198},{7,71},{8,72}... | collective-permute-start | bytes 1966088 | tf_op jit(solution)/shard_map/ppermute | solution.py:42
  8.1 1.6 %copy-start.1 = (bf16[256,4096]{1,0:T(8,128)(2,1)S(1)}, bf16[256,4096]{1,0:T(8,128)(2,1)}, u32[]{:S(2)}) copy-start(bf16[256,4096]{1,0:T(8,128)(2,1)} %tokens.1) | copy-start | bytes 6291460
  10.8 2.0 %collective-permute-start.2 = (bf16[128,2048]{1,0:T(8,128)(2,1)S(1)}, bf16[128,2048]{1,0:T(8,128)(2,1)S(1)}, u32[]{:S(2)}, u32[]{:S(2)}) collective-permute-start(bf16[128,2048]{1,0:T(8,128)(2,1)S(1)} %get-tuple-element.59), channel_id=1, source_target_pairs={{0,1},{1,0},{2,3},{3,2},{4,5},{5,4},{6,7},{7,6},{8,9},{9,8},{10,11... | collective-permute-start | bytes 1572872 | tf_op jit(solution)/shard_map/ppermute | solution.py:42
  10.9 2.6 %collective-permute-start.3 = (bf16[128,2048]{1,0:T(8,128)(2,1)S(1)}, bf16[128,2048]{1,0:T(8,128)(2,1)S(1)}, u32[]{:S(2)}, u32[]{:S(2)}) collective-permute-start(bf16[128,2048]{1,0:T(8,128)(2,1)S(1)} %get-tuple-element.60), channel_id=1, source_target_pairs={{0,1},{1,0},{2,3},{3,2},{4,5},{5,4},{6,7},{7,6},{8,9},{9,8},{10,11... | collective-permute-start | bytes 1572872 | tf_op jit(solution)/shard_map/ppermute | solution.py:42
  16.3 10.9 %collective-permute-start.5 = (bf16[256,1280]{1,0:T(8,128)(2,1)S(1)}, bf16[256,1280]{1,0:T(8,128)(2,1)S(1)}, u32[]{:S(2)}, u32[]{:S(2)}) collective-permute-start(bf16[256,1280]{1,0:T(8,128)(2,1)S(1)} %collective-permute-done.refs_5_.refs_6_), channel_id=1, source_target_pairs={{0,32},{1,49},{2,34},{3,51},{4,36},{5,53},{6,38},{7,55},{8,40},{9,... | collective-permute-start | bytes 1966088 | tf_op jit(solution)/shard_map/ppermute | solution.py:42
  16.4 10.8 %collective-permute-start.4 = (bf16[256,1280]{1,0:T(8,128)(2,1)S(1)}, bf16[256,1280]{1,0:T(8,128)(2,1)S(1)}, u32[]{:S(2)}, u32[]{:S(2)}) collective-permute-start(bf16[256,1280]{1,0:T(8,128)(2,1)S(1)} %collective-permute-done.refs_5_.refs_6_), channel_id=1, source_target_pairs={{0,192},{1,65},{2,66},{3,195},{4,196},{5,69},{6,70},{7,199},{8,200... | collective-permute-start | bytes 1966088 | tf_op jit(solution)/shard_map/ppermute | solution.py:42
  17.5 16.8 %collective-permute-start.8 = (bf16[256,1280]{1,0:T(8,128)(2,1)S(1)}, bf16[256,1280]{1,0:T(8,128)(2,1)S(1)}, u32[]{:S(2)}, u32[]{:S(2)}) collective-permute-start(bf16[256,1280]{1,0:T(8,128)(2,1)S(1)} %collective-permute-done.refs_5_.refs_6_), channel_id=1, source_target_pairs={{0,2},{1,15},{2,0},{3,5},{4,6},{5,3},{6,4},{7,9},{8,10},{9,7},{10,... | collective-permute-start | bytes 1966088 | tf_op jit(solution)/shard_map/ppermute | solution.py:42
  27.2 10.6 %collective-permute-start.6 = (bf16[256,1280]{1,0:T(8,128)(2,1)S(1)}, bf16[256,1280]{1,0:T(8,128)(2,1)S(1)}, u32[]{:S(2)}, u32[]{:S(2)}) collective-permute-start(bf16[256,1280]{1,0:T(8,128)(2,1)S(1)} %collective-permute-done.4.refs_3_.refs_7_), channel_id=1, source_target_pairs={{0,32},{1,49},{2,34},{3,51},{4,36},{5,53},{6,38},{7,55},{8,40},{9,... | collective-permute-start | bytes 1966088 | tf_op jit(solution)/shard_map/ppermute | solution.py:42
  28.7 13.5 %collective-permute-start.7 = (bf16[256,1280]{1,0:T(8,128)(2,1)S(1)}, bf16[256,1280]{1,0:T(8,128)(2,1)S(1)}, u32[]{:S(2)}, u32[]{:S(2)}) collective-permute-start(bf16[256,1280]{1,0:T(8,128)(2,1)S(1)} %collective-permute-done.5.refs_4_.refs_8_), channel_id=1, source_target_pairs={{0,2},{1,15},{2,0},{3,5},{4,6},{5,3},{6,4},{7,9},{8,10},{9,7},{10,... | collective-permute-start | bytes 1966088 | tf_op jit(solution)/shard_map/ppermute | solution.py:42
  42.8 2.2 %copy-start.3 = (bf16[256,1024]{1,0:T(8,128)(2,1)S(1)}, bf16[256,1024]{1,0:T(8,128)(2,1)}, u32[]{:S(2)}) copy-start(bf16[256,1024]{1,0:T(8,128)(2,1)} %grad.3) | copy-start | bytes 1572868
  42.8 2.2 %copy-start.4 = (f32[256,128]{1,0:T(8,128)S(1)}, f32[256,128]{1,0:T(8,128)}, u32[]{:S(2)}) copy-start(f32[256,128]{1,0:T(8,128)} %constant.15.clone.sine) | copy-start | bytes 393220
  42.8 2.2 %copy-start.5 = (f32[256,128]{1,0:T(8,128)S(1)}, f32[256,128]{1,0:T(8,128)}, u32[]{:S(2)}) copy-start(f32[256,128]{1,0:T(8,128)} %constant.14.clone.cosine) | copy-start | bytes 393220
  42.8 2.2 %copy-start.6 = (s32[1,256]{1,0:T(1,128)S(1)}, s32[1,256]{1,0:T(1,128)}, u32[]{:S(2)}) copy-start(s32[1,256]{1,0:T(1,128)} %doc.3) | copy-start | bytes 3076
  42.8 2.2 %collective-permute-start.9 = (bf16[256,1280]{1,0:T(8,128)(2,1)S(1)}, bf16[256,1280]{1,0:T(8,128)(2,1)S(1)}, u32[]{:S(2)}, u32[]{:S(2)}) collective-permute-start(bf16[256,1280]{1,0:T(8,128)(2,1)S(1)} %project_late.2), channel_id=1, source_target_pairs={{0,1},{1,0},{2,3},{3,2},{4,5},{5,4},{6,7},{7,6},{8,9},{9,8},{10,11... | collective-permute-start | bytes 1966088 | tf_op jit(solution)/shard_map/ppermute | solution.py:42
  47.2 1.9 %collective-permute-start.10 = (bf16[256,640]{1,0:T(8,128)(2,1)S(1)}, bf16[256,640]{1,0:T(8,128)(2,1)S(1)}, u32[]{:S(2)}, u32[]{:S(2)}) collective-permute-start(bf16[256,640]{1,0:T(8,128)(2,1)S(1)} %get-tuple-element.87.refs_1_.refs_0_), channel_id=1, source_target_pairs={{0,1},{1,0},{2,3},{3,2},{4,5},{5,4},{6,7},{7,6},{8,9},{9,8},{10,11... | collective-permute-start | bytes 983048 | tf_op jit(solution)/shard_map/ppermute | solution.py:42
  49.1 3.7 %collective-permute-start.12 = (bf16[256,640]{1,0:T(8,128)(2,1)S(1)}, bf16[256,640]{1,0:T(8,128)(2,1)S(1)}, u32[]{:S(2)}, u32[]{:S(2)}) collective-permute-start(bf16[256,640]{1,0:T(8,128)(2,1)S(1)} %attend_high.1.refs_1_.refs_2_), channel_id=1, source_target_pairs={{0,1},{1,0},{2,3},{3,2},{4,5},{5,4},{6,7},{7,6},{8,9},{9,8},{10,11... | collective-permute-start | bytes 983048 | tf_op jit(solution)/shard_map/ppermute | solution.py:42
  50.2 17.8 %collective-permute-start.11 = (bf16[8,128,640]{2,1,0:T(8,128)(2,1)S(1)}, bf16[8,128,640]{2,1,0:T(8,128)(2,1)S(1)}, u32[]{:S(2)}, u32[]{:S(2)}) collective-permute-start(bf16[8,128,640]{2,1,0:T(8,128)(2,1)S(1)} %terms.4), channel_id=1, source_target_pairs={{0,64},{1,193},{2,66},{3,195},{4,68},{5,197},{6,70},{7,199},{8,72}... | collective-permute-start | bytes 3932168 | tf_op jit(solution)/shard_map/ppermute | solution.py:42
  53.8 17.8 %collective-permute-start.14 = (bf16[8,128,640]{2,1,0:T(8,128)(2,1)S(1)}, bf16[8,128,640]{2,1,0:T(8,128)(2,1)S(1)}, u32[]{:S(2)}, u32[]{:S(2)}) collective-permute-start(bf16[8,128,640]{2,1,0:T(8,128)(2,1)S(1)} %terms.5), channel_id=1, source_target_pairs={{0,32},{1,49},{2,34},{3,51},{4,36},{5,53},{6,38},{7,55},{8,40},{9,... | collective-permute-start | bytes 3932168 | tf_op jit(solution)/shard_map/ppermute | solution.py:42
  58.1 14.0 %collective-permute-start.15 = (bf16[256,2048]{1,0:T(8,128)(2,1)S(1)}, bf16[256,2048]{1,0:T(8,128)(2,1)S(1)}, u32[]{:S(2)}, u32[]{:S(2)}) collective-permute-start(bf16[256,2048]{1,0:T(8,128)(2,1)S(1)} %get-tuple-element.99), channel_id=1, source_target_pairs={{0,1},{1,0},{2,3},{3,2},{4,5},{5,4},{6,7},{7,6},{8,9},{9,8},{10,11... | collective-permute-start | bytes 3145736 | tf_op jit(solution)/shard_map/ppermute | solution.py:42
  68.2 4.0 %copy-start.2 = (bf16[256,4096]{1,0:T(8,128)(2,1)S(1)}, bf16[256,4096]{1,0:T(8,128)(2,1)}, u32[]{:S(2)}) copy-start(bf16[256,4096]{1,0:T(8,128)(2,1)} %tokens.1) | copy-start | bytes 6291460
  68.2 6.7 %collective-permute-start.13 = (bf16[2,128,640]{2,1,0:T(8,128)(2,1)S(1)}, bf16[2,128,640]{2,1,0:T(8,128)(2,1)S(1)}, u32[]{:S(2)}, u32[]{:S(2)}) collective-permute-start(bf16[2,128,640]{2,1,0:T(8,128)(2,1)S(1)} %get-tuple-element.95), channel_id=1, source_target_pairs={{0,192},{1,65},{2,194},{3,67},{4,196},{5,69},{6,198},{7,71},{8,200... | collective-permute-start | bytes 983048 | tf_op jit(solution)/shard_map/ppermute | solution.py:42
  71.7 6.3 %collective-permute-start.20 = (bf16[2,128,640]{2,1,0:T(8,128)(2,1)S(1)}, bf16[2,128,640]{2,1,0:T(8,128)(2,1)S(1)}, u32[]{:S(2)}, u32[]{:S(2)}) collective-permute-start(bf16[2,128,640]{2,1,0:T(8,128)(2,1)S(1)} %get-tuple-element.98), channel_id=1, source_target_pairs={{0,48},{1,33},{2,50},{3,35},{4,52},{5,37},{6,54},{7,39},{8,56},{9,... | collective-permute-start | bytes 983048 | tf_op jit(solution)/shard_map/ppermute | solution.py:42
  71.8 6.8 %collective-permute-start.16 = (bf16[2,128,640]{2,1,0:T(8,128)(2,1)S(1)}, bf16[2,128,640]{2,1,0:T(8,128)(2,1)S(1)}, u32[]{:S(2)}, u32[]{:S(2)}) collective-permute-start(bf16[2,128,640]{2,1,0:T(8,128)(2,1)S(1)} %get-tuple-element.103), channel_id=1, source_target_pairs={{0,192},{1,65},{2,194},{3,67},{4,196},{5,69},{6,198},{7,71},{8,200... | collective-permute-start | bytes 983048 | tf_op jit(solution)/shard_map/ppermute | solution.py:42
  75.0 9.2 %collective-permute-start.17 = (bf16[2,128,640]{2,1,0:T(8,128)(2,1)S(1)}, bf16[2,128,640]{2,1,0:T(8,128)(2,1)S(1)}, u32[]{:S(2)}, u32[]{:S(2)}) collective-permute-start(bf16[2,128,640]{2,1,0:T(8,128)(2,1)S(1)} %add.12), channel_id=1, source_target_pairs={{0,32},{1,49},{2,34},{3,51},{4,36},{5,53},{6,38},{7,55},{8,40},{9,... | collective-permute-start | bytes 983048 | tf_op jit(solution)/shard_map/ppermute | solution.py:42
  76.3 8.5 %collective-permute-start.19 = (bf16[2,128,640]{2,1,0:T(8,128)(2,1)S(1)}, bf16[2,128,640]{2,1,0:T(8,128)(2,1)S(1)}, u32[]{:S(2)}, u32[]{:S(2)}) collective-permute-start(bf16[2,128,640]{2,1,0:T(8,128)(2,1)S(1)} %get-tuple-element.107), channel_id=1, source_target_pairs={{0,48},{1,33},{2,50},{3,35},{4,52},{5,37},{6,54},{7,39},{8,56},{9,... | collective-permute-start | bytes 983048 | tf_op jit(solution)/shard_map/ppermute | solution.py:42
  78.1 7.5 %collective-permute-start.21 = (bf16[2,128,640]{2,1,0:T(8,128)(2,1)S(1)}, bf16[2,128,640]{2,1,0:T(8,128)(2,1)S(1)}, u32[]{:S(2)}, u32[]{:S(2)}) collective-permute-start(bf16[2,128,640]{2,1,0:T(8,128)(2,1)S(1)} %add.14), channel_id=1, source_target_pairs={{0,64},{1,193},{2,66},{3,195},{4,68},{5,197},{6,70},{7,199},{8,72}... | collective-permute-start | bytes 983048 | tf_op jit(solution)/shard_map/ppermute | solution.py:42
  84.4 4.3 %collective-permute-start.18 = (bf16[1,128,640]{2,1,0:T(8,128)(2,1)S(1)}, bf16[1,128,640]{2,1,0:T(8,128)(2,1)S(1)}, u32[]{:S(2)}, u32[]{:S(2)}) collective-permute-start(bf16[1,128,640]{2,1,0:T(8,128)(2,1)S(1)} %get-tuple-element.106), channel_id=1, source_target_pairs={{0,48},{1,33},{2,50},{3,35},{4,52},{5,37},{6,54},{7,39},{8,56},{9,... | collective-permute-start | bytes 491528 | tf_op jit(solution)/shard_map/ppermute | solution.py:42
  85.8 4.3 %collective-permute-start.22 = (bf16[1,128,640]{2,1,0:T(8,128)(2,1)S(1)}, bf16[1,128,640]{2,1,0:T(8,128)(2,1)S(1)}, u32[]{:S(2)}, u32[]{:S(2)}) collective-permute-start(bf16[1,128,640]{2,1,0:T(8,128)(2,1)S(1)} %get-tuple-element.109), channel_id=1, source_target_pairs={{0,192},{1,65},{2,194},{3,67},{4,196},{5,69},{6,198},{7,71},{8,200... | collective-permute-start | bytes 491528 | tf_op jit(solution)/shard_map/ppermute | solution.py:42
  123.8 18.4 %collective-permute-start.23 = (bf16[16,16,1280]{2,1,0:T(8,128)(2,1)S(1)}, bf16[16,16,1280]{2,1,0:T(8,128)(2,1)S(1)}, u32[]{:S(2)}, u32[]{:S(2)}) collective-permute-start(bf16[16,16,1280]{2,1,0:T(8,128)(2,1)S(1)} %all_to_all.16.got.mine), channel_id=1, source_target_pairs={{0,1},{1,0},{2,3},{3,2},{4,5},{5,4},{6,7},{7,6},{8,9},{9,8},{10,11... | collective-permute-start | bytes 1966088 | tf_op jit(solution)/shard_map/ppermute | solution.py:42

commit v6 on v5

--- a/solution.py
+++ b/solution.py
@@ -532,14 +532,13 @@
     sum_x, sum_y = terms(True, 0, lows), terms(False, 0, highs)
     normed_own, normed_send = normed_grad(spots, (*lows[1:], *highs[1:]), pieces)
     normed_came = swap(normed_send, other_core)
-    came_x, sum_x, sum_y, normed_own = lax.optimization_barrier((came_x, sum_x, sum_y, normed_own))
+    normed_came, sum_x, sum_y = lax.optimization_barrier((normed_came, sum_x, sum_y))
+    d_tokens = tokens_grad(normed_own, normed_came, tokens, scale_r)
+    came_x, sum_x, sum_y, d_tokens = lax.optimization_barrier((came_x, sum_x, sum_y, d_tokens))
     first, second = add([(sum_x, 4, 4), (came_x, 4, 4)], [(2, 2), (0, 2)])
     pass_x, keep_x = swap(first, x_2), swap(second, x_2)
     first, second = add([(sum_y, 4, 4), (came_y, 4, 4)], [(2, 2), (0, 2)])
     pass_y, keep_y = swap(first, y_2), swap(second, y_2)
-    first, normed_came = lax.optimization_barrier((first, normed_came))
-    d_tokens = tokens_grad(normed_own, normed_came, tokens, scale_r)
-    pass_x, d_tokens = lax.optimization_barrier((pass_x, d_tokens))
     (sent,) = add([(sum_x, 2, 2), (came_x, 2, 2), (pass_x, 0, 2)], [(0, 2)])
     pass_x = swap(sent, y_1)
     (sent,) = add([(sum_y, 2, 2), (came_y, 2, 2), (pass_y, 0, 2)], [(0, 2)])

time: 144 us -> 145 us (level)
  starting transfers between devices: 39.4 us -> 36.8 us
  waiting for transfers between devices: 36.3 us -> 38.1 us
  blocking collectives: 43.4 us -> 44.9 us
    ppermute x24, starting transfers between devices: 39.4 us -> 36.8 us  [swap(): return lax.ppermute(value, AXES, pairs)]
    all_to_all x1, blocking collectives: 9.78 us -> 11.9 us  [on_device(): parts = lax.all_to_all(squares(got), ('x', 'y_lo', 'core'), 0, 0)]
    ppermute x24, waiting for transfers between devices: 36.3 us -> 38.1 us  [swap(): return lax.ppermute(value, AXES, pairs)]
  transfers between devices with their start and end apart: 24 -> 24, of which waited for: 17 -> 18; matrix products, arithmetic and copies ran while one was open for 0% -> 0% of each run, Pallas kernels for 11% -> 11%
where the time goes in v6:
time: 145 us; the launch traced here: 144 us
  blocking collectives  44.9 us (31%)
  waiting for transfers between devices  38.1 us (26%)
  starting transfers between devices  36.8 us (25%)
  Pallas kernels  20.5 us (14%)
  local copies, waits for them, and re-layouts  2.98 us (2%)
    ppermute x24, waiting for transfers between devices, swap(): return lax.ppermute(value, AXES, pairs)  38.1 us
    ppermute x24, starting transfers between devices, swap(): return lax.ppermute(value, AXES, pairs)  36.8 us
    all_to_all x1, blocking collectives, on_device(): got = lax.all_to_all(got, ('y_hi', 'z'), 0, 0)  17.2 us
    all_to_all x1, blocking collectives, on_device(): got = finish(lax.all_to_all(total, 'z', 0, 0))  15.7 us
    all_to_all x1, blocking collectives, on_device(): parts = lax.all_to_all(squares(got), ('x', 'y_lo', 'core'), 0, 0)  11.9 us
    pallas_call x4, Pallas kernels, terms(): pl.pallas_call(lambda *refs: term_body(along_x, level, *refs), out_shape=...  3.91 us
    pallas_call x1, Pallas kernels, normed_grad(): pl.pallas_call(lambda *refs: normed_body(spots, *refs), out_shape=(jax.Sh...  2.98 us
    unnamed x14, local copies, waits for them, and re-layouts  2.93 us
  transfers between devices with their start and end apart: 24, of which 18 were waited for; matrix products, arithmetic and copies ran while one was open for 0% of the time, Pallas kernels for 11%

profile of v6, /device:TPU:1, one launch (start us, length us, event | category | flops | bytes accessed | tf_op | source)
XLA Modules:
  0.0 144.4 jit_solution(188305275765945139)
XLA Ops:
  0.6 1.3 copy-done
  2.0 3.7 %collective-permute-start.1 = (bf16[256,1280]{1,0:T(8,128)(2,1)S(1)}, bf16[256,1280]{1,0:T(8,128)(2,1)S(1)}, u32[]{:S(2)}, u32[]{:S(2)}) collective-permute-start(bf16[256,1280]{1,0:T(8,128)(2,1)S(1)} %constant_dynamic-slice_fusion.refs_3_.refs_4_), channel_id=1, source_target_pairs={{0,32},{1,49},{2,34},{3,51},{4,36},{5,53},{6,38},{7,55},{8,40},{9,... | collective-permute-start | bytes 1966088 | tf_op jit(solution)/shard_map/ppermute | solution.py:42
  5.6 2.5 %collective-permute-start = (bf16[256,1280]{1,0:T(8,128)(2,1)S(1)}, bf16[256,1280]{1,0:T(8,128)(2,1)S(1)}, u32[]{:S(2)}, u32[]{:S(2)}) collective-permute-start(bf16[256,1280]{1,0:T(8,128)(2,1)S(1)} %constant_dynamic-slice_fusion.refs_3_.refs_4_), channel_id=1, source_target_pairs={{0,64},{1,193},{2,194},{3,67},{4,68},{5,197},{6,198},{7,71},{8,72}... | collective-permute-start | bytes 1966088 | tf_op jit(solution)/shard_map/ppermute | solution.py:42
  8.1 1.6 %copy-done.1 = bf16[256,4096]{1,0:T(8,128)(2,1)S(1)} copy-done((bf16[256,4096]{1,0:T(8,128)(2,1)S(1)}, bf16[256,4096]{1,0:T(8,128)(2,1)}, u32[]{:S(2)}) %copy-start.1) | copy-done | bytes 2097176
  11.4 1.4 collective-permute-done.2.refs_1_.low.refs_0_
  13.6 2.7 %collective-permute-done.refs_5_.refs_6_ = bf16[256,1280]{1,0:T(8,128)(2,1)S(1)} collective-permute-done((bf16[256,1280]{1,0:T(8,128)(2,1)S(1)}, bf16[256,1280]{1,0:T(8,128)(2,1)S(1)}, u32[]{:S(2)}, u32[]{:S(2)}) %collective-permute-start) | collective-permute-done | bytes 655392 | tf_op jit(solution)/shard_map/ppermute | solution.py:42
  17.5 7.1 %collective-permute-start.8 = (bf16[256,1280]{1,0:T(8,128)(2,1)S(1)}, bf16[256,1280]{1,0:T(8,128)(2,1)S(1)}, u32[]{:S(2)}, u32[]{:S(2)}) collective-permute-start(bf16[256,1280]{1,0:T(8,128)(2,1)S(1)} %collective-permute-done.refs_5_.refs_6_), channel_id=1, source_target_pairs={{0,2},{1,15},{2,0},{3,5},{4,6},{5,3},{6,4},{7,9},{8,10},{9,7},{10,... | collective-permute-start | bytes 1966088 | tf_op jit(solution)/shard_map/ppermute | solution.py:42
  25.3 1.2 project.2
  27.2 1.5 %collective-permute-start.6 = (bf16[256,1280]{1,0:T(8,128)(2,1)S(1)}, bf16[256,1280]{1,0:T(8,128)(2,1)S(1)}, u32[]{:S(2)}, u32[]{:S(2)}) collective-permute-start(bf16[256,1280]{1,0:T(8,128)(2,1)S(1)} %collective-permute-done.4.refs_3_.refs_7_), channel_id=1, source_target_pairs={{0,32},{1,49},{2,34},{3,51},{4,36},{5,53},{6,38},{7,55},{8,40},{9,... | collective-permute-start | bytes 1966088 | tf_op jit(solution)/shard_map/ppermute | solution.py:42
  28.7 5.6 %collective-permute-start.7 = (bf16[256,1280]{1,0:T(8,128)(2,1)S(1)}, bf16[256,1280]{1,0:T(8,128)(2,1)S(1)}, u32[]{:S(2)}, u32[]{:S(2)}) collective-permute-start(bf16[256,1280]{1,0:T(8,128)(2,1)S(1)} %collective-permute-done.5.refs_4_.refs_8_), channel_id=1, source_target_pairs={{0,2},{1,15},{2,0},{3,5},{4,6},{5,3},{6,4},{7,9},{8,10},{9,7},{10,... | collective-permute-start | bytes 1966088 | tf_op jit(solution)/shard_map/ppermute | solution.py:42
  35.5 2.4 %collective-permute-done.6.refs_2_.refs_1_.refs_10_ = bf16[256,1280]{1,0:T(8,128)(2,1)S(1)} collective-permute-done((bf16[256,1280]{1,0:T(8,128)(2,1)S(1)}, bf16[256,1280]{1,0:T(8,128)(2,1)S(1)}, u32[]{:S(2)}, u32[]{:S(2)}) %collective-permute-start.6) | collective-permute-done | bytes 655392 | tf_op jit(solution)/shard_map/ppermute | solution.py:42
  37.9 4.4 %collective-permute-done.7.refs_3_.refs_2_.refs_11_ = bf16[256,1280]{1,0:T(8,128)(2,1)S(1)} collective-permute-done((bf16[256,1280]{1,0:T(8,128)(2,1)S(1)}, bf16[256,1280]{1,0:T(8,128)(2,1)S(1)}, u32[]{:S(2)}, u32[]{:S(2)}) %collective-permute-start.7) | collective-permute-done | bytes 655392 | tf_op jit(solution)/shard_map/ppermute | solution.py:42
  43.5 1.6 %collective-permute-done.9.came = bf16[256,1280]{1,0:T(8,128)(2,1)S(1)} collective-permute-done((bf16[256,1280]{1,0:T(8,128)(2,1)S(1)}, bf16[256,1280]{1,0:T(8,128)(2,1)S(1)}, u32[]{:S(2)}, u32[]{:S(2)}) %collective-permute-start.9) | collective-permute-done | bytes 655392 | tf_op jit(solution)/shard_map/ppermute | solution.py:42
  45.0 2.1 %attend_low.1 = (bf16[256,640]{1,0:T(8,128)(2,1)S(1)}, bf16[256,640]{1,0:T(8,128)(2,1)S(1)}, f32[256,128]{1,0:T(8,128)S(1)}, f32[256,128]{1,0:T(8,128)S(1)}) custom-call(f32[256,1280]{1,0:T(8,128)S(1)} %project_late.3.own, bf16[256,1280]{1,0:T(8,128)(2,1)S(1)} %collective-permute-done.9.came, bf16[256,1024]{1,0:T(8,128)(2,1)S(1)} %copy-done.3, ...), custom_call_target="tpu_custom_call" | custom-call | flops 419430400 | bytes 4194304 | tf_op jit(solution)/shard_map/attend_low/pallas_call | solution.py:273
  47.6 1.2 attend_high.1.refs_1_.refs_2_
  50.3 2.6 %collective-permute-start.11 = (bf16[8,128,640]{2,1,0:T(8,128)(2,1)S(1)}, bf16[8,128,640]{2,1,0:T(8,128)(2,1)S(1)}, u32[]{:S(2)}, u32[]{:S(2)}) collective-permute-start(bf16[8,128,640]{2,1,0:T(8,128)(2,1)S(1)} %terms.4), channel_id=1, source_target_pairs={{0,64},{1,193},{2,66},{3,195},{4,68},{5,197},{6,70},{7,199},{8,72}... | collective-permute-start | bytes 3932168 | tf_op jit(solution)/shard_map/ppermute | solution.py:42
  53.8 1.3 collective-permute-start.18
  55.1 3.0 %normed_grad.1 = (f32[256,2048]{1,0:T(8,128)S(1)}, bf16[256,2048]{1,0:T(8,128)(2,1)S(1)}) custom-call(bf16[256,640]{1,0:T(8,128)(2,1)S(1)} %get-tuple-element.86.refs_1_.refs_0_, bf16[256,640]{1,0:T(8,128)(2,1)S(1)} %collective-permute-done.10.refs_2_.refs_1_, bf16[256,640]{1,0:T(8,128)(2,1)S(1)} %attend_high.1.refs_1_.refs_2_, ...), custom_call_target="tpu_custom_call" | custom-call | flops 2684354560 | bytes 8388608 | tf_op jit(solution)/shard_map/normed_grad/pallas_call | solution.py:308
  60.8 2.7 %tokens_grad.1 = bf16[256,4096]{1,0:T(8,128)(2,1)} custom-call(f32[256,2048]{1,0:T(8,128)S(1)} %get-tuple-element.95.own, bf16[256,2048]{1,0:T(8,128)(2,1)S(1)} %collective-permute-done.13.came, bf16[256,4096]{1,0:T(8,128)(2,1)S(1)} %copy-done.2, f32[256,1]{1,0:T(8,128)S(1)} %get-tuple-element.97.scale_r), custom_call_target="tpu_custom_call" | custom-call | flops 10485760 | bytes 8388608 | tf_op jit(solution)/shard_map/tokens_grad/pallas_call | solution.py:339
  63.6 4.4 %collective-permute-done.11.refs_1_ = bf16[8,128,640]{2,1,0:T(8,128)(2,1)S(1)} collective-permute-done((bf16[8,128,640]{2,1,0:T(8,128)(2,1)S(1)}, bf16[8,128,640]{2,1,0:T(8,128)(2,1)S(1)}, u32[]{:S(2)}, u32[]{:S(2)}) %collective-permute-start.11) | collective-permute-done | bytes 1310752 | tf_op jit(solution)/shard_map/ppermute | solution.py:42
  68.3 3.3 %collective-permute-done.18.refs_1_ = bf16[8,128,640]{2,1,0:T(8,128)(2,1)S(1)} collective-permute-done((bf16[8,128,640]{2,1,0:T(8,128)(2,1)S(1)}, bf16[8,128,640]{2,1,0:T(8,128)(2,1)S(1)}, u32[]{:S(2)}, u32[]{:S(2)}) %collective-permute-start.18) | collective-permute-done | bytes 1310752 | tf_op jit(solution)/shard_map/ppermute | solution.py:42
  72.1 2.3 %collective-permute-done.15.refs_2_ = bf16[2,128,640]{2,1,0:T(8,128)(2,1)S(1)} collective-permute-done((bf16[2,128,640]{2,1,0:T(8,128)(2,1)S(1)}, bf16[2,128,640]{2,1,0:T(8,128)(2,1)S(1)}, u32[]{:S(2)}, u32[]{:S(2)}) %collective-permute-start.15) | collective-permute-done | bytes 327712 | tf_op jit(solution)/shard_map/ppermute | solution.py:42
  74.6 1.3 collective-permute-start.16
  75.9 2.1 %collective-permute-done.20.refs_2_ = bf16[2,128,640]{2,1,0:T(8,128)(2,1)S(1)} collective-permute-done((bf16[2,128,640]{2,1,0:T(8,128)(2,1)S(1)}, bf16[2,128,640]{2,1,0:T(8,128)(2,1)S(1)}, u32[]{:S(2)}, u32[]{:S(2)}) %collective-permute-start.20) | collective-permute-done | bytes 327712 | tf_op jit(solution)/shard_map/ppermute | solution.py:42
  78.6 5.7 %collective-permute-done.16.refs_3_ = bf16[2,128,640]{2,1,0:T(8,128)(2,1)S(1)} collective-permute-done((bf16[2,128,640]{2,1,0:T(8,128)(2,1)S(1)}, bf16[2,128,640]{2,1,0:T(8,128)(2,1)S(1)}, u32[]{:S(2)}, u32[]{:S(2)}) %collective-permute-start.16) | collective-permute-done | bytes 327712 | tf_op jit(solution)/shard_map/ppermute | solution.py:42
  85.9 2.8 %collective-permute-done.17.came_x = bf16[1,128,640]{2,1,0:T(8,128)(2,1)S(1)} collective-permute-done((bf16[1,128,640]{2,1,0:T(8,128)(2,1)S(1)}, bf16[1,128,640]{2,1,0:T(8,128)(2,1)S(1)}, u32[]{:S(2)}, u32[]{:S(2)}) %collective-permute-start.17) | collective-permute-done | bytes 163872 | tf_op jit(solution)/shard_map/ppermute | solution.py:42
  88.7 1.4 collective-permute-done.22.came_y
  90.2 15.7 %all_to_all.15.parts = bf16[8,16,1280]{2,1,0:T(8,128)(2,1)S(1)} all-to-all(bf16[8,16,1280]{2,1,0:T(8,128)(2,1)S(1)} %join.1), channel_id=1, replica_groups=mesh['x'=4,'y_lo'=2,'y_hi'=2,'z'=8,'core'=2] {'z'}, dimensions={0} | all-to-all | bytes 655360 | tf_op jit(solution)/shard_map/all_to_all | solution.py:552
  106.0 17.2 %all_to_all.16.got.mine = bf16[16,16,1280]{2,1,0:T(8,128)(2,1)S(1)} all-to-all(bf16[16,16,1280]{2,1,0:T(8,128)(2,1)S(1)} %finish.1), channel_id=1, replica_groups=mesh['x'=4,'y_lo'=2,'y_hi'=2,'z'=8,'core'=2] {'y_hi','z'}, dimensions={0} | all-to-all | bytes 1310720 | tf_op jit(solution)/shard_map/all_to_all | solution.py:553
  123.2 7.6 %collective-permute-start.23 = (bf16[16,16,1280]{2,1,0:T(8,128)(2,1)S(1)}, bf16[16,16,1280]{2,1,0:T(8,128)(2,1)S(1)}, u32[]{:S(2)}, u32[]{:S(2)}) collective-permute-start(bf16[16,16,1280]{2,1,0:T(8,128)(2,1)S(1)} %all_to_all.16.got.mine), channel_id=1, source_target_pairs={{0,1},{1,0},{2,3},{3,2},{4,5},{5,4},{6,7},{7,6},{8,9},{9,8},{10,11... | collective-permute-start | bytes 1966088 | tf_op jit(solution)/shard_map/ppermute | solution.py:42
  131.0 11.9 %all_to_all.17.parts = f32[16,8,128]{2,1,0:T(8,128)S(1)} all-to-all(f32[16,8,128]{2,1,0:T(8,128)S(1)} %squares.1), channel_id=1, replica_groups=mesh['x'=4,'y_lo'=2,'y_hi'=2,'z'=8,'core'=2] {'x','y_lo','core'}, dimensions={0} | all-to-all | bytes 131072 | tf_op jit(solution)/shard_map/all_to_all | solution.py:556
  142.9 1.3 rescale.1
  (58 shorter events, 16.5 us)
Async XLA Ops:
  0.6 1.3 copy-start
  2.0 11.6 %collective-permute-start.1 = (bf16[256,1280]{1,0:T(8,128)(2,1)S(1)}, bf16[256,1280]{1,0:T(8,128)(2,1)S(1)}, u32[]{:S(2)}, u32[]{:S(2)}) collective-permute-start(bf16[256,1280]{1,0:T(8,128)(2,1)S(1)} %constant_dynamic-slice_fusion.refs_3_.refs_4_), channel_id=1, source_target_pairs={{0,32},{1,49},{2,34},{3,51},{4,36},{5,53},{6,38},{7,55},{8,40},{9,... | collective-permute-start | bytes 1966088 | tf_op jit(solution)/shard_map/ppermute | solution.py:42
  5.6 10.6 %collective-permute-start = (bf16[256,1280]{1,0:T(8,128)(2,1)S(1)}, bf16[256,1280]{1,0:T(8,128)(2,1)S(1)}, u32[]{:S(2)}, u32[]{:S(2)}) collective-permute-start(bf16[256,1280]{1,0:T(8,128)(2,1)S(1)} %constant_dynamic-slice_fusion.refs_3_.refs_4_), channel_id=1, source_target_pairs={{0,64},{1,193},{2,194},{3,67},{4,68},{5,197},{6,198},{7,71},{8,72}... | collective-permute-start | bytes 1966088 | tf_op jit(solution)/shard_map/ppermute | solution.py:42
  8.1 1.6 %copy-start.1 = (bf16[256,4096]{1,0:T(8,128)(2,1)S(1)}, bf16[256,4096]{1,0:T(8,128)(2,1)}, u32[]{:S(2)}) copy-start(bf16[256,4096]{1,0:T(8,128)(2,1)} %tokens.1) | copy-start | bytes 6291460
  10.8 2.0 %collective-permute-start.2 = (bf16[128,2048]{1,0:T(8,128)(2,1)S(1)}, bf16[128,2048]{1,0:T(8,128)(2,1)S(1)}, u32[]{:S(2)}, u32[]{:S(2)}) collective-permute-start(bf16[128,2048]{1,0:T(8,128)(2,1)S(1)} %get-tuple-element.59), channel_id=1, source_target_pairs={{0,1},{1,0},{2,3},{3,2},{4,5},{5,4},{6,7},{7,6},{8,9},{9,8},{10,11... | collective-permute-start | bytes 1572872 | tf_op jit(solution)/shard_map/ppermute | solution.py:42
  10.9 2.6 %collective-permute-start.3 = (bf16[128,2048]{1,0:T(8,128)(2,1)S(1)}, bf16[128,2048]{1,0:T(8,128)(2,1)S(1)}, u32[]{:S(2)}, u32[]{:S(2)}) collective-permute-start(bf16[128,2048]{1,0:T(8,128)(2,1)S(1)} %get-tuple-element.60), channel_id=1, source_target_pairs={{0,1},{1,0},{2,3},{3,2},{4,5},{5,4},{6,7},{7,6},{8,9},{9,8},{10,11... | collective-permute-start | bytes 1572872 | tf_op jit(solution)/shard_map/ppermute | solution.py:42
  16.3 10.9 %collective-permute-start.5 = (bf16[256,1280]{1,0:T(8,128)(2,1)S(1)}, bf16[256,1280]{1,0:T(8,128)(2,1)S(1)}, u32[]{:S(2)}, u32[]{:S(2)}) collective-permute-start(bf16[256,1280]{1,0:T(8,128)(2,1)S(1)} %collective-permute-done.refs_5_.refs_6_), channel_id=1, source_target_pairs={{0,32},{1,49},{2,34},{3,51},{4,36},{5,53},{6,38},{7,55},{8,40},{9,... | collective-permute-start | bytes 1966088 | tf_op jit(solution)/shard_map/ppermute | solution.py:42
  16.4 10.8 %collective-permute-start.4 = (bf16[256,1280]{1,0:T(8,128)(2,1)S(1)}, bf16[256,1280]{1,0:T(8,128)(2,1)S(1)}, u32[]{:S(2)}, u32[]{:S(2)}) collective-permute-start(bf16[256,1280]{1,0:T(8,128)(2,1)S(1)} %collective-permute-done.refs_5_.refs_6_), channel_id=1, source_target_pairs={{0,192},{1,65},{2,66},{3,195},{4,196},{5,69},{6,70},{7,199},{8,200... | collective-permute-start | bytes 1966088 | tf_op jit(solution)/shard_map/ppermute | solution.py:42
  17.5 16.8 %collective-permute-start.8 = (bf16[256,1280]{1,0:T(8,128)(2,1)S(1)}, bf16[256,1280]{1,0:T(8,128)(2,1)S(1)}, u32[]{:S(2)}, u32[]{:S(2)}) collective-permute-start(bf16[256,1280]{1,0:T(8,128)(2,1)S(1)} %collective-permute-done.refs_5_.refs_6_), channel_id=1, source_target_pairs={{0,2},{1,15},{2,0},{3,5},{4,6},{5,3},{6,4},{7,9},{8,10},{9,7},{10,... | collective-permute-start | bytes 1966088 | tf_op jit(solution)/shard_map/ppermute | solution.py:42
  27.2 10.6 %collective-permute-start.6 = (bf16[256,1280]{1,0:T(8,128)(2,1)S(1)}, bf16[256,1280]{1,0:T(8,128)(2,1)S(1)}, u32[]{:S(2)}, u32[]{:S(2)}) collective-permute-start(bf16[256,1280]{1,0:T(8,128)(2,1)S(1)} %collective-permute-done.4.refs_3_.refs_7_), channel_id=1, source_target_pairs={{0,32},{1,49},{2,34},{3,51},{4,36},{5,53},{6,38},{7,55},{8,40},{9,... | collective-permute-start | bytes 1966088 | tf_op jit(solution)/shard_map/ppermute | solution.py:42
  28.7 13.5 %collective-permute-start.7 = (bf16[256,1280]{1,0:T(8,128)(2,1)S(1)}, bf16[256,1280]{1,0:T(8,128)(2,1)S(1)}, u32[]{:S(2)}, u32[]{:S(2)}) collective-permute-start(bf16[256,1280]{1,0:T(8,128)(2,1)S(1)} %collective-permute-done.5.refs_4_.refs_8_), channel_id=1, source_target_pairs={{0,2},{1,15},{2,0},{3,5},{4,6},{5,3},{6,4},{7,9},{8,10},{9,7},{10,... | collective-permute-start | bytes 1966088 | tf_op jit(solution)/shard_map/ppermute | solution.py:42
  42.8 2.2 %copy-start.3 = (bf16[256,1024]{1,0:T(8,128)(2,1)S(1)}, bf16[256,1024]{1,0:T(8,128)(2,1)}, u32[]{:S(2)}) copy-start(bf16[256,1024]{1,0:T(8,128)(2,1)} %grad.3) | copy-start | bytes 1572868
  42.8 2.2 %copy-start.4 = (f32[256,128]{1,0:T(8,128)S(1)}, f32[256,128]{1,0:T(8,128)}, u32[]{:S(2)}) copy-start(f32[256,128]{1,0:T(8,128)} %constant.15.clone.sine) | copy-start | bytes 393220
  42.8 2.2 %copy-start.5 = (f32[256,128]{1,0:T(8,128)S(1)}, f32[256,128]{1,0:T(8,128)}, u32[]{:S(2)}) copy-start(f32[256,128]{1,0:T(8,128)} %constant.14.clone.cosine) | copy-start | bytes 393220
  42.8 2.2 %copy-start.6 = (s32[1,256]{1,0:T(1,128)S(1)}, s32[1,256]{1,0:T(1,128)}, u32[]{:S(2)}) copy-start(s32[1,256]{1,0:T(1,128)} %doc.3) | copy-start | bytes 3076
  42.8 2.2 %collective-permute-start.9 = (bf16[256,1280]{1,0:T(8,128)(2,1)S(1)}, bf16[256,1280]{1,0:T(8,128)(2,1)S(1)}, u32[]{:S(2)}, u32[]{:S(2)}) collective-permute-start(bf16[256,1280]{1,0:T(8,128)(2,1)S(1)} %project_late.2), channel_id=1, source_target_pairs={{0,1},{1,0},{2,3},{3,2},{4,5},{5,4},{6,7},{7,6},{8,9},{9,8},{10,11... | collective-permute-start | bytes 1966088 | tf_op jit(solution)/shard_map/ppermute | solution.py:42
  47.2 1.9 %collective-permute-start.10 = (bf16[256,640]{1,0:T(8,128)(2,1)S(1)}, bf16[256,640]{1,0:T(8,128)(2,1)S(1)}, u32[]{:S(2)}, u32[]{:S(2)}) collective-permute-start(bf16[256,640]{1,0:T(8,128)(2,1)S(1)} %get-tuple-element.86.refs_1_.refs_0_), channel_id=1, source_target_pairs={{0,1},{1,0},{2,3},{3,2},{4,5},{5,4},{6,7},{7,6},{8,9},{9,8},{10,11... | collective-permute-start | bytes 983048 | tf_op jit(solution)/shard_map/ppermute | solution.py:42
  49.1 3.7 %collective-permute-start.12 = (bf16[256,640]{1,0:T(8,128)(2,1)S(1)}, bf16[256,640]{1,0:T(8,128)(2,1)S(1)}, u32[]{:S(2)}, u32[]{:S(2)}) collective-permute-start(bf16[256,640]{1,0:T(8,128)(2,1)S(1)} %attend_high.1.refs_1_.refs_2_), channel_id=1, source_target_pairs={{0,1},{1,0},{2,3},{3,2},{4,5},{5,4},{6,7},{7,6},{8,9},{9,8},{10,11... | collective-permute-start | bytes 983048 | tf_op jit(solution)/shard_map/ppermute | solution.py:42
  50.3 17.8 %collective-permute-start.11 = (bf16[8,128,640]{2,1,0:T(8,128)(2,1)S(1)}, bf16[8,128,640]{2,1,0:T(8,128)(2,1)S(1)}, u32[]{:S(2)}, u32[]{:S(2)}) collective-permute-start(bf16[8,128,640]{2,1,0:T(8,128)(2,1)S(1)} %terms.4), channel_id=1, source_target_pairs={{0,64},{1,193},{2,66},{3,195},{4,68},{5,197},{6,70},{7,199},{8,72}... | collective-permute-start | bytes 3932168 | tf_op jit(solution)/shard_map/ppermute | solution.py:42
  53.8 17.8 %collective-permute-start.18 = (bf16[8,128,640]{2,1,0:T(8,128)(2,1)S(1)}, bf16[8,128,640]{2,1,0:T(8,128)(2,1)S(1)}, u32[]{:S(2)}, u32[]{:S(2)}) collective-permute-start(bf16[8,128,640]{2,1,0:T(8,128)(2,1)S(1)} %terms.5), channel_id=1, source_target_pairs={{0,32},{1,49},{2,34},{3,51},{4,36},{5,53},{6,38},{7,55},{8,40},{9,... | collective-permute-start | bytes 3932168 | tf_op jit(solution)/shard_map/ppermute | solution.py:42
  58.1 2.7 %collective-permute-start.13 = (bf16[256,2048]{1,0:T(8,128)(2,1)S(1)}, bf16[256,2048]{1,0:T(8,128)(2,1)S(1)}, u32[]{:S(2)}, u32[]{:S(2)}) collective-permute-start(bf16[256,2048]{1,0:T(8,128)(2,1)S(1)} %get-tuple-element.90), channel_id=1, source_target_pairs={{0,1},{1,0},{2,3},{3,2},{4,5},{5,4},{6,7},{7,6},{8,9},{9,8},{10,11... | collective-permute-start | bytes 3145736 | tf_op jit(solution)/shard_map/ppermute | solution.py:42
  59.2 1.7 %copy-start.2 = (bf16[256,4096]{1,0:T(8,128)(2,1)S(1)}, bf16[256,4096]{1,0:T(8,128)(2,1)}, u32[]{:S(2)}) copy-start(bf16[256,4096]{1,0:T(8,128)(2,1)} %tokens.1) | copy-start | bytes 6291460
  68.2 6.3 %collective-permute-start.15 = (bf16[2,128,640]{2,1,0:T(8,128)(2,1)S(1)}, bf16[2,128,640]{2,1,0:T(8,128)(2,1)S(1)}, u32[]{:S(2)}, u32[]{:S(2)}) collective-permute-start(bf16[2,128,640]{2,1,0:T(8,128)(2,1)S(1)} %get-tuple-element.102), channel_id=1, source_target_pairs={{0,192},{1,65},{2,194},{3,67},{4,196},{5,69},{6,198},{7,71},{8,200... | collective-permute-start | bytes 983048 | tf_op jit(solution)/shard_map/ppermute | solution.py:42
  71.7 6.3 %collective-permute-start.20 = (bf16[2,128,640]{2,1,0:T(8,128)(2,1)S(1)}, bf16[2,128,640]{2,1,0:T(8,128)(2,1)S(1)}, u32[]{:S(2)}, u32[]{:S(2)}) collective-permute-start(bf16[2,128,640]{2,1,0:T(8,128)(2,1)S(1)} %get-tuple-element.107), channel_id=1, source_target_pairs={{0,48},{1,33},{2,50},{3,35},{4,52},{5,37},{6,54},{7,39},{8,56},{9,... | collective-permute-start | bytes 983048 | tf_op jit(solution)/shard_map/ppermute | solution.py:42
  71.8 6.8 %collective-permute-start.14 = (bf16[2,128,640]{2,1,0:T(8,128)(2,1)S(1)}, bf16[2,128,640]{2,1,0:T(8,128)(2,1)S(1)}, u32[]{:S(2)}, u32[]{:S(2)}) collective-permute-start(bf16[2,128,640]{2,1,0:T(8,128)(2,1)S(1)} %get-tuple-element.101), channel_id=1, source_target_pairs={{0,192},{1,65},{2,194},{3,67},{4,196},{5,69},{6,198},{7,71},{8,200... | collective-permute-start | bytes 983048 | tf_op jit(solution)/shard_map/ppermute | solution.py:42
  74.6 9.7 %collective-permute-start.16 = (bf16[2,128,640]{2,1,0:T(8,128)(2,1)S(1)}, bf16[2,128,640]{2,1,0:T(8,128)(2,1)S(1)}, u32[]{:S(2)}, u32[]{:S(2)}) collective-permute-start(bf16[2,128,640]{2,1,0:T(8,128)(2,1)S(1)} %add.11), channel_id=1, source_target_pairs={{0,32},{1,49},{2,34},{3,51},{4,36},{5,53},{6,38},{7,55},{8,40},{9,... | collective-permute-start | bytes 983048 | tf_op jit(solution)/shard_map/ppermute | solution.py:42
  75.9 8.6 %collective-permute-start.19 = (bf16[2,128,640]{2,1,0:T(8,128)(2,1)S(1)}, bf16[2,128,640]{2,1,0:T(8,128)(2,1)S(1)}, u32[]{:S(2)}, u32[]{:S(2)}) collective-permute-start(bf16[2,128,640]{2,1,0:T(8,128)(2,1)S(1)} %get-tuple-element.106), channel_id=1, source_target_pairs={{0,48},{1,33},{2,50},{3,35},{4,52},{5,37},{6,54},{7,39},{8,56},{9,... | collective-permute-start | bytes 983048 | tf_op jit(solution)/shard_map/ppermute | solution.py:42
  78.2 7.5 %collective-permute-start.21 = (bf16[2,128,640]{2,1,0:T(8,128)(2,1)S(1)}, bf16[2,128,640]{2,1,0:T(8,128)(2,1)S(1)}, u32[]{:S(2)}, u32[]{:S(2)}) collective-permute-start(bf16[2,128,640]{2,1,0:T(8,128)(2,1)S(1)} %add.14), channel_id=1, source_target_pairs={{0,64},{1,193},{2,66},{3,195},{4,68},{5,197},{6,70},{7,199},{8,72}... | collective-permute-start | bytes 983048 | tf_op jit(solution)/shard_map/ppermute | solution.py:42
  84.4 4.3 %collective-permute-start.17 = (bf16[1,128,640]{2,1,0:T(8,128)(2,1)S(1)}, bf16[1,128,640]{2,1,0:T(8,128)(2,1)S(1)}, u32[]{:S(2)}, u32[]{:S(2)}) collective-permute-start(bf16[1,128,640]{2,1,0:T(8,128)(2,1)S(1)} %get-tuple-element.104), channel_id=1, source_target_pairs={{0,48},{1,33},{2,50},{3,35},{4,52},{5,37},{6,54},{7,39},{8,56},{9,... | collective-permute-start | bytes 491528 | tf_op jit(solution)/shard_map/ppermute | solution.py:42
  85.8 4.3 %collective-permute-start.22 = (bf16[1,128,640]{2,1,0:T(8,128)(2,1)S(1)}, bf16[1,128,640]{2,1,0:T(8,128)(2,1)S(1)}, u32[]{:S(2)}, u32[]{:S(2)}) collective-permute-start(bf16[1,128,640]{2,1,0:T(8,128)(2,1)S(1)} %get-tuple-element.109), channel_id=1, source_target_pairs={{0,192},{1,65},{2,194},{3,67},{4,196},{5,69},{6,198},{7,71},{8,200... | collective-permute-start | bytes 491528 | tf_op jit(solution)/shard_map/ppermute | solution.py:42
  123.2 19.7 %collective-permute-start.23 = (bf16[16,16,1280]{2,1,0:T(8,128)(2,1)S(1)}, bf16[16,16,1280]{2,1,0:T(8,128)(2,1)S(1)}, u32[]{:S(2)}, u32[]{:S(2)}) collective-permute-start(bf16[16,16,1280]{2,1,0:T(8,128)(2,1)S(1)} %all_to_all.16.got.mine), channel_id=1, source_target_pairs={{0,1},{1,0},{2,3},{3,2},{4,5},{5,4},{6,7},{7,6},{8,9},{9,8},{10,11... | collective-permute-start | bytes 1966088 | tf_op jit(solution)/shard_map/ppermute | solution.py:42

commit v7 on v6

--- a/solution.py
+++ b/solution.py
@@ -158,11 +158,11 @@
 def product(spots, feats, pieces):
     cols = [aligned(block(*spot) * HALF, HALF) for spot in spots]
     lhs = jnp.concatenate([jnp.concatenate([ref[:, k] for k in cols], axis=1) for ref in feats], axis=0)
-    return dot(lhs, jnp.concatenate([p[...] for p in pieces], axis=0), ((1,), (0,)))
+    return dot(lhs, jnp.concatenate([piece[...] for piece in pieces], axis=0), ((1,), (0,)))
 
 
 def part_body(spots, own, low, high, *refs):
-    count = len(spots)
+    count = 2 * len(spots)
     pieces, old, outs = refs[:count], refs[count:-2], refs[-2:]
     part = product(spots, (own, low, high), pieces)
     for k, half in enumerate((part[:TOK], part[TOK:])):
@@ -295,23 +295,23 @@
 
 
 def normed_body(spots, low, low_other, high, high_other, *refs):
-    pieces, own, send = refs[: len(spots)], refs[-2], refs[-1]
+    count = 2 * len(spots)
+    pieces, own, send = refs[:count], refs[-2], refs[-1]
     for lower, higher, out in ((low_other, high_other, send), (low, high, own)):
         d_qkv = jnp.concatenate([lower[...], higher[...]], axis=1)
-        for spot, piece in zip(spots, pieces):
-            part = dot(d_qkv, piece[...], ((1,), (1,)))
-            out[:, aligned(block(*spot) * HALF, HALF)] = part.astype(out.dtype)
+        for i, spot in enumerate(spots):
+            piece = jnp.concatenate([pieces[2 * i][...], pieces[2 * i + 1][...]], axis=0)
+            out[:, aligned(block(*spot) * HALF, HALF)] = dot(d_qkv, piece, ((1,), (1,))).astype(out.dtype)
 
 
 def normed_grad(spots, grads, pieces):
-    count = len(pieces)
     return pl.pallas_call(
         lambda *refs: normed_body(spots, *refs),
         out_shape=(
             jax.ShapeDtypeStruct((TOK, D // 2), F32),
             jax.ShapeDtypeStruct((TOK, D // 2), BF16),
         ),
-        in_specs=[VM] * (4 + count),
+        in_specs=[VM] * (4 + len(pieces)),
         out_specs=(VM, VM),
         compiler_params=pltpu.CompilerParams(vmem_limit_bytes=12 << 20),
         cost_estimate=pl.CostEstimate(flops=2 * TOK * D * QKV, bytes_accessed=8 << 20, transcendentals=0),
@@ -492,27 +492,23 @@
 TABLES = tables()
 
 def on_device(tokens, grad_attended, doc_ids, w_own):
-    w00 = lax.dynamic_slice_in_dim(w_own, lax.axis_index("core") * HALF, HALF, 0)
+    start = lax.axis_index("core") * HALF
+    w00 = [lax.dynamic_slice_in_dim(w_own, start + k, QUART, 0) for k in (0, QUART)]
     w00, tokens = lax.optimization_barrier((w00, tokens))
-    wa0 = swap(w00, gather_x1)
-    w01 = swap(w00, flip_y)
+    round_one = [lax.optimization_barrier((swap(part, gather_x1), swap(part, flip_y))) for part in w00]
+    wa0, w01 = zip(*round_one)
+    wb0, wo0, wa1 = zip(*[(swap(part, pair_z), swap(part, gather_x2), swap(part, flip_y)) for part in wa0])
     scale_r, own, send_low, send_high = norm(tokens)
     other = [swap(send, other_core) for send in (send_low, send_high)]
-    wa0, w01, own, other = lax.optimization_barrier((wa0, w01, own, other))
     both = (own, *other)
-    wo0 = swap(wa0, gather_x2)
-    wa1 = swap(wa0, flip_y)
-    wb0 = swap(wa0, pair_z)
-    early, early_spots = [w00, w01, wa0], [("0", 0), ("0", 1), ("a", 0)]
-    part_own, part_other = project(early_spots, both, early)
+    wb1 = [swap(part, pair_z) for part in wa1]
+    wo1 = [swap(wo0[0], flip_y), swap(wa1[1], gather_x2)]
+    early, early_spots = [*w00, *w01, *wa0], [("0", 0), ("0", 1), ("a", 0)]
+    middle, middle_spots = [*wo0, *wa1, *wb0], [("o", 0), ("a", 1), ("b", 0)]
+    part_own, part_other = project(early_spots + middle_spots, both, early + middle)
     feats = transpose(*both)
-    wo0, wa1, part_own, part_other, feats = lax.optimization_barrier((wo0, wa1, part_own, part_other, feats))
-    wo1 = swap(wo0, flip_y)
-    wb1 = swap(wa1, pair_z)
-    middle, middle_spots = [wo0, wa1, wb0], [("o", 0), ("a", 1), ("b", 0)]
-    part_own, part_other = project(middle_spots, both, middle, part_own, part_other)
     wo1, wb1, part_own, part_other = lax.optimization_barrier((wo1, wb1, part_own, part_other))
-    late, late_spots = [wo1, wb1], [("o", 1), ("b", 1)]
+    late, late_spots = [*wo1, *wb1], [("o", 1), ("b", 1)]
     late_other = project_late(late_spots, other, late, part_other, BF16)
     came = swap(late_other, other_core)
     late_other, part_own = lax.optimization_barrier((late_other, part_own))

time: 145 us -> 142 us (0.979)
  starting transfers between devices: 36.8 us -> 49.2 us
  waiting for transfers between devices: 38.1 us -> 28.3 us
  blocking collectives: 44.9 us -> 40.2 us
    ppermute x24 -> x31, starting transfers between devices: 36.8 us -> 49.2 us  [swap(): return lax.ppermute(value, AXES, pairs)]
    ppermute x24 -> x31, waiting for transfers between devices: 38.1 us -> 28.3 us  [swap(): return lax.ppermute(value, AXES, pairs)]
    all_to_all x1, blocking collectives: 11.9 us -> 8.71 us  [on_device(): parts = lax.all_to_all(squares(got), ('x', 'y_lo', 'core'), 0, 0)]
    unnamed x14 -> x12, local copies, waits for them, and re-layouts: 2.93 us -> 1.62 us
  transfers between devices with their start and end apart: 24 -> 31, of which waited for: 18 -> 14; matrix products, arithmetic and copies ran while one was open for 0% -> 0% of each run, Pallas kernels for 11% -> 11%
where the time goes in v7:
time: 142 us
  starting transfers between devices  49.2 us (35%)
  blocking collectives  40.2 us (28%)
  waiting for transfers between devices  28.3 us (20%)
  Pallas kernels  20.3 us (14%)
  local copies, waits for them, and re-layouts  2.74 us (2%)
    ppermute x31, starting transfers between devices, swap(): return lax.ppermute(value, AXES, pairs)  49.2 us
    ppermute x31, waiting for transfers between devices, swap(): return lax.ppermute(value, AXES, pairs)  28.3 us
    all_to_all x1, blocking collectives, on_device(): got = lax.all_to_all(got, ('y_hi', 'z'), 0, 0)  17 us
    all_to_all x1, blocking collectives, on_device(): got = finish(lax.all_to_all(total, 'z', 0, 0))  14.5 us
    all_to_all x1, blocking collectives, on_device(): parts = lax.all_to_all(squares(got), ('x', 'y_lo', 'core'), 0, 0)  8.71 us
    pallas_call x4, Pallas kernels, terms(): pl.pallas_call(lambda *refs: term_body(along_x, level, *refs), out_shape=...  3.91 us
    pallas_call x1, Pallas kernels, normed_grad(): pl.pallas_call(lambda *refs: normed_body(spots, *refs), out_shape=(jax.Sh...  2.98 us
  transfers between devices with their start and end apart: 31, of which 14 were waited for; matrix products, arithmetic and copies ran while one was open for 0% of the time, Pallas kernels for 11%

profile of v7, /device:TPU:1, one launch (start us, length us, event | category | flops | bytes accessed | tf_op | source)
XLA Modules:
  0.0 141.8 jit_solution(11595973628114363693)
XLA Ops:
  1.8 3.7 %collective-permute-start.3 = (bf16[128,1280]{1,0:T(8,128)(2,1)S(1)}, bf16[128,1280]{1,0:T(8,128)(2,1)S(1)}, u32[]{:S(2)}, u32[]{:S(2)}) collective-permute-start(bf16[128,1280]{1,0:T(8,128)(2,1)S(1)} %get-tuple-element.55.refs_3_.refs_4_), channel_id=1, source_target_pairs={{0,32},{1,49},{2,34},{3,51},{4,36},{5,53},{6,38},{7,55},{8,40},{9,... | collective-permute-start | bytes 983048 | tf_op jit(solution)/shard_map/ppermute | solution.py:42
  5.4 2.5 %collective-permute-start.2 = (bf16[128,1280]{1,0:T(8,128)(2,1)S(1)}, bf16[128,1280]{1,0:T(8,128)(2,1)S(1)}, u32[]{:S(2)}, u32[]{:S(2)}) collective-permute-start(bf16[128,1280]{1,0:T(8,128)(2,1)S(1)} %get-tuple-element.55.refs_3_.refs_4_), channel_id=1, source_target_pairs={{0,64},{1,193},{2,194},{3,67},{4,68},{5,197},{6,198},{7,71},{8,72}... | collective-permute-start | bytes 983048 | tf_op jit(solution)/shard_map/ppermute | solution.py:42
  7.9 1.6 %copy-done = bf16[256,4096]{1,0:T(8,128)(2,1)S(1)} copy-done((bf16[256,4096]{1,0:T(8,128)(2,1)S(1)}, bf16[256,4096]{1,0:T(8,128)(2,1)}, u32[]{:S(2)}) %copy-start) | copy-done | bytes 2097176
  11.2 1.7 %collective-permute-start.6 = (bf16[128,1280]{1,0:T(8,128)(2,1)S(1)}, bf16[128,1280]{1,0:T(8,128)(2,1)S(1)}, u32[]{:S(2)}, u32[]{:S(2)}) collective-permute-start(bf16[128,1280]{1,0:T(8,128)(2,1)S(1)} %get-tuple-element.57.refs_4_.refs_5_), channel_id=1, source_target_pairs={{0,64},{1,193},{2,194},{3,67},{4,68},{5,197},{6,198},{7,71},{8,72}... | collective-permute-start | bytes 983048 | tf_op jit(solution)/shard_map/ppermute | solution.py:42
  13.0 5.1 %collective-permute-start.14 = (bf16[128,1280]{1,0:T(8,128)(2,1)S(1)}, bf16[128,1280]{1,0:T(8,128)(2,1)S(1)}, u32[]{:S(2)}, u32[]{:S(2)}) collective-permute-start(bf16[128,1280]{1,0:T(8,128)(2,1)S(1)} %collective-permute-done.2.refs_7_.refs_8_), channel_id=1, source_target_pairs={{0,2},{1,15},{2,0},{3,5},{4,6},{5,3},{6,4},{7,9},{8,10},{9,7},{10,... | collective-permute-start | bytes 983048 | tf_op jit(solution)/shard_map/ppermute | solution.py:42
  18.4 2.6 %collective-permute-start.8 = (bf16[128,1280]{1,0:T(8,128)(2,1)S(1)}, bf16[128,1280]{1,0:T(8,128)(2,1)S(1)}, u32[]{:S(2)}, u32[]{:S(2)}) collective-permute-start(bf16[128,1280]{1,0:T(8,128)(2,1)S(1)} %collective-permute-done.6.refs_8_.refs_9_), channel_id=1, source_target_pairs={{0,32},{1,49},{2,34},{3,51},{4,36},{5,53},{6,38},{7,55},{8,40},{9,... | collective-permute-start | bytes 983048 | tf_op jit(solution)/shard_map/ppermute | solution.py:42
  22.2 5.2 %collective-permute-start.15 = (bf16[128,1280]{1,0:T(8,128)(2,1)S(1)}, bf16[128,1280]{1,0:T(8,128)(2,1)S(1)}, u32[]{:S(2)}, u32[]{:S(2)}) collective-permute-start(bf16[128,1280]{1,0:T(8,128)(2,1)S(1)} %collective-permute-done.6.refs_8_.refs_9_), channel_id=1, source_target_pairs={{0,2},{1,15},{2,0},{3,5},{4,6},{5,3},{6,4},{7,9},{8,10},{9,7},{10,... | collective-permute-start | bytes 983048 | tf_op jit(solution)/shard_map/ppermute | solution.py:42
  27.4 4.0 %collective-permute-start.12 = (bf16[128,1280]{1,0:T(8,128)(2,1)S(1)}, bf16[128,1280]{1,0:T(8,128)(2,1)S(1)}, u32[]{:S(2)}, u32[]{:S(2)}) collective-permute-start(bf16[128,1280]{1,0:T(8,128)(2,1)S(1)} %collective-permute-done.8.refs_12_.refs_13_), channel_id=1, source_target_pairs={{0,2},{1,15},{2,0},{3,5},{4,6},{5,3},{6,4},{7,9},{8,10},{9,7},{10,... | collective-permute-start | bytes 983048 | tf_op jit(solution)/shard_map/ppermute | solution.py:42
  31.4 4.0 %collective-permute-start.11 = (bf16[128,1280]{1,0:T(8,128)(2,1)S(1)}, bf16[128,1280]{1,0:T(8,128)(2,1)S(1)}, u32[]{:S(2)}, u32[]{:S(2)}) collective-permute-start(bf16[128,1280]{1,0:T(8,128)(2,1)S(1)} %collective-permute-done.10.refs_11_.refs_12_), channel_id=1, source_target_pairs={{0,2},{1,15},{2,0},{3,5},{4,6},{5,3},{6,4},{7,9},{8,10},{9,7},{10,... | collective-permute-start | bytes 983048 | tf_op jit(solution)/shard_map/ppermute | solution.py:42
  35.4 2.4 %collective-permute-start.5 = (bf16[128,1280]{1,0:T(8,128)(2,1)S(1)}, bf16[128,1280]{1,0:T(8,128)(2,1)S(1)}, u32[]{:S(2)}, u32[]{:S(2)}) collective-permute-start(bf16[128,1280]{1,0:T(8,128)(2,1)S(1)} %collective-permute-done.4.refs_9_.refs_10_), channel_id=1, source_target_pairs={{0,32},{1,49},{2,34},{3,51},{4,36},{5,53},{6,38},{7,55},{8,40},{9,... | collective-permute-start | bytes 983048 | tf_op jit(solution)/shard_map/ppermute | solution.py:42
  37.8 2.2 %project.1 = (f32[256,1280]{1,0:T(8,128)S(1)}, f32[256,1280]{1,0:T(8,128)S(1)}) custom-call(bf16[256,2048]{1,0:T(8,128)(2,1)S(1)} %get-tuple-element.52.own.refs_0_, bf16[128,2048]{1,0:T(8,128)(2,1)S(1)} %collective-permute-done.low.refs_1_.refs_0_, bf16[128,2048]{1,0:T(8,128)(2,1)S(1)} %collective-permute-done.1.high.refs_2_.refs_1_, ...), custom_call_target="tpu_custom_call" | custom-call | flops 4026531840 | bytes 6291456 | tf_op jit(solution)/shard_map/project/pallas_call | solution.py:174
  40.0 2.5 %collective-permute-done.5.refs_2_.refs_1_.refs_16_ = bf16[128,1280]{1,0:T(8,128)(2,1)S(1)} collective-permute-done((bf16[128,1280]{1,0:T(8,128)(2,1)S(1)}, bf16[128,1280]{1,0:T(8,128)(2,1)S(1)}, u32[]{:S(2)}, u32[]{:S(2)}) %collective-permute-start.5) | collective-permute-done | bytes 327712 | tf_op jit(solution)/shard_map/ppermute | solution.py:42
  43.9 1.6 %collective-permute-done.16.came = bf16[256,1280]{1,0:T(8,128)(2,1)S(1)} collective-permute-done((bf16[256,1280]{1,0:T(8,128)(2,1)S(1)}, bf16[256,1280]{1,0:T(8,128)(2,1)S(1)}, u32[]{:S(2)}, u32[]{:S(2)}) %collective-permute-start.16) | collective-permute-done | bytes 655392 | tf_op jit(solution)/shard_map/ppermute | solution.py:42
  45.5 2.1 %attend_low.1 = (bf16[256,640]{1,0:T(8,128)(2,1)S(1)}, bf16[256,640]{1,0:T(8,128)(2,1)S(1)}, f32[256,128]{1,0:T(8,128)S(1)}, f32[256,128]{1,0:T(8,128)S(1)}) custom-call(f32[256,1280]{1,0:T(8,128)S(1)} %project_late.3.own, bf16[256,1280]{1,0:T(8,128)(2,1)S(1)} %collective-permute-done.16.came, bf16[256,1024]{1,0:T(8,128)(2,1)S(1)} %copy-done.2, ...), custom_call_target="tpu_custom_call" | custom-call | flops 419430400 | bytes 4194304 | tf_op jit(solution)/shard_map/attend_low/pallas_call | solution.py:273
  47.8 1.2 attend_high.1.refs_1_.refs_2_
  51.1 2.3 %collective-permute-start.18 = (bf16[8,128,640]{2,1,0:T(8,128)(2,1)S(1)}, bf16[8,128,640]{2,1,0:T(8,128)(2,1)S(1)}, u32[]{:S(2)}, u32[]{:S(2)}) collective-permute-start(bf16[8,128,640]{2,1,0:T(8,128)(2,1)S(1)} %terms.4), channel_id=1, source_target_pairs={{0,64},{1,193},{2,66},{3,195},{4,68},{5,197},{6,70},{7,199},{8,72}... | collective-permute-start | bytes 3932168 | tf_op jit(solution)/shard_map/ppermute | solution.py:42
  54.4 1.3 collective-permute-start.25
  55.7 3.0 %normed_grad.1 = (f32[256,2048]{1,0:T(8,128)S(1)}, bf16[256,2048]{1,0:T(8,128)(2,1)S(1)}) custom-call(bf16[256,640]{1,0:T(8,128)(2,1)S(1)} %get-tuple-element.76.refs_1_.refs_0_, bf16[256,640]{1,0:T(8,128)(2,1)S(1)} %collective-permute-done.17.refs_2_.refs_1_, bf16[256,640]{1,0:T(8,128)(2,1)S(1)} %attend_high.1.refs_1_.refs_2_, ...), custom_call_target="tpu_custom_call" | custom-call | flops 2684354560 | bytes 8388608 | tf_op jit(solution)/shard_map/normed_grad/pallas_call | solution.py:308
  61.6 2.7 %tokens_grad.1 = bf16[256,4096]{1,0:T(8,128)(2,1)} custom-call(f32[256,2048]{1,0:T(8,128)S(1)} %get-tuple-element.85.own, bf16[256,2048]{1,0:T(8,128)(2,1)S(1)} %collective-permute-done.20.came, bf16[256,4096]{1,0:T(8,128)(2,1)S(1)} %copy-done.1, f32[256,1]{1,0:T(8,128)S(1)} %get-tuple-element.87.scale_r), custom_call_target="tpu_custom_call" | custom-call | flops 10485760 | bytes 8388608 | tf_op jit(solution)/shard_map/tokens_grad/pallas_call | solution.py:339
  64.4 4.5 %collective-permute-done.18.refs_1_ = bf16[8,128,640]{2,1,0:T(8,128)(2,1)S(1)} collective-permute-done((bf16[8,128,640]{2,1,0:T(8,128)(2,1)S(1)}, bf16[8,128,640]{2,1,0:T(8,128)(2,1)S(1)}, u32[]{:S(2)}, u32[]{:S(2)}) %collective-permute-start.18) | collective-permute-done | bytes 1310752 | tf_op jit(solution)/shard_map/ppermute | solution.py:42
  69.1 3.0 %collective-permute-done.25.refs_1_ = bf16[8,128,640]{2,1,0:T(8,128)(2,1)S(1)} collective-permute-done((bf16[8,128,640]{2,1,0:T(8,128)(2,1)S(1)}, bf16[8,128,640]{2,1,0:T(8,128)(2,1)S(1)}, u32[]{:S(2)}, u32[]{:S(2)}) %collective-permute-start.25) | collective-permute-done | bytes 1310752 | tf_op jit(solution)/shard_map/ppermute | solution.py:42
  72.5 2.8 %collective-permute-done.22.refs_2_ = bf16[2,128,640]{2,1,0:T(8,128)(2,1)S(1)} collective-permute-done((bf16[2,128,640]{2,1,0:T(8,128)(2,1)S(1)}, bf16[2,128,640]{2,1,0:T(8,128)(2,1)S(1)}, u32[]{:S(2)}, u32[]{:S(2)}) %collective-permute-start.22) | collective-permute-done | bytes 327712 | tf_op jit(solution)/shard_map/ppermute | solution.py:42
  75.5 2.5 %collective-permute-start.23 = (bf16[2,128,640]{2,1,0:T(8,128)(2,1)S(1)}, bf16[2,128,640]{2,1,0:T(8,128)(2,1)S(1)}, u32[]{:S(2)}, u32[]{:S(2)}) collective-permute-start(bf16[2,128,640]{2,1,0:T(8,128)(2,1)S(1)} %add.21), channel_id=1, source_target_pairs={{0,32},{1,49},{2,34},{3,51},{4,36},{5,53},{6,38},{7,55},{8,40},{9,... | collective-permute-start | bytes 983048 | tf_op jit(solution)/shard_map/ppermute | solution.py:42
  79.3 5.3 %collective-permute-done.23.refs_3_ = bf16[2,128,640]{2,1,0:T(8,128)(2,1)S(1)} collective-permute-done((bf16[2,128,640]{2,1,0:T(8,128)(2,1)S(1)}, bf16[2,128,640]{2,1,0:T(8,128)(2,1)S(1)}, u32[]{:S(2)}, u32[]{:S(2)}) %collective-permute-start.23) | collective-permute-done | bytes 327712 | tf_op jit(solution)/shard_map/ppermute | solution.py:42
  84.9 2.5 %collective-permute-done.26.refs_2_ = bf16[2,128,640]{2,1,0:T(8,128)(2,1)S(1)} collective-permute-done((bf16[2,128,640]{2,1,0:T(8,128)(2,1)S(1)}, bf16[2,128,640]{2,1,0:T(8,128)(2,1)S(1)}, u32[]{:S(2)}, u32[]{:S(2)}) %collective-permute-start.26) | collective-permute-done | bytes 327712 | tf_op jit(solution)/shard_map/ppermute | solution.py:42
  87.7 1.5 %collective-permute-done.24.came_x = bf16[1,128,640]{2,1,0:T(8,128)(2,1)S(1)} collective-permute-done((bf16[1,128,640]{2,1,0:T(8,128)(2,1)S(1)}, bf16[1,128,640]{2,1,0:T(8,128)(2,1)S(1)}, u32[]{:S(2)}, u32[]{:S(2)}) %collective-permute-start.24) | collective-permute-done | bytes 163872 | tf_op jit(solution)/shard_map/ppermute | solution.py:42
  89.1 2.7 %collective-permute-done.29.came_y = bf16[1,128,640]{2,1,0:T(8,128)(2,1)S(1)} collective-permute-done((bf16[1,128,640]{2,1,0:T(8,128)(2,1)S(1)}, bf16[1,128,640]{2,1,0:T(8,128)(2,1)S(1)}, u32[]{:S(2)}, u32[]{:S(2)}) %collective-permute-start.29) | collective-permute-done | bytes 163872 | tf_op jit(solution)/shard_map/ppermute | solution.py:42
  91.9 14.5 %all_to_all.15.parts = bf16[8,16,1280]{2,1,0:T(8,128)(2,1)S(1)} all-to-all(bf16[8,16,1280]{2,1,0:T(8,128)(2,1)S(1)} %join.1), channel_id=1, replica_groups=mesh['x'=4,'y_lo'=2,'y_hi'=2,'z'=8,'core'=2] {'z'}, dimensions={0} | all-to-all | bytes 655360 | tf_op jit(solution)/shard_map/all_to_all | solution.py:548
  106.4 17.0 %all_to_all.16.got.mine = bf16[16,16,1280]{2,1,0:T(8,128)(2,1)S(1)} all-to-all(bf16[16,16,1280]{2,1,0:T(8,128)(2,1)S(1)} %finish.1), channel_id=1, replica_groups=mesh['x'=4,'y_lo'=2,'y_hi'=2,'z'=8,'core'=2] {'y_hi','z'}, dimensions={0} | all-to-all | bytes 1310720 | tf_op jit(solution)/shard_map/all_to_all | solution.py:549
  123.4 8.0 %collective-permute-start.30 = (bf16[16,16,1280]{2,1,0:T(8,128)(2,1)S(1)}, bf16[16,16,1280]{2,1,0:T(8,128)(2,1)S(1)}, u32[]{:S(2)}, u32[]{:S(2)}) collective-permute-start(bf16[16,16,1280]{2,1,0:T(8,128)(2,1)S(1)} %all_to_all.16.got.mine), channel_id=1, source_target_pairs={{0,1},{1,0},{2,3},{3,2},{4,5},{5,4},{6,7},{7,6},{8,9},{9,8},{10,11... | collective-permute-start | bytes 1966088 | tf_op jit(solution)/shard_map/ppermute | solution.py:42
  131.6 8.7 %all_to_all.17.parts = f32[16,8,128]{2,1,0:T(8,128)S(1)} all-to-all(f32[16,8,128]{2,1,0:T(8,128)S(1)} %squares.1), channel_id=1, replica_groups=mesh['x'=4,'y_lo'=2,'y_hi'=2,'z'=8,'core'=2] {'x','y_lo','core'}, dimensions={0} | all-to-all | bytes 131072 | tf_op jit(solution)/shard_map/all_to_all | solution.py:552
  140.3 1.3 rescale.1
  (69 shorter events, 14.8 us)
Async XLA Ops:
  1.8 9.5 %collective-permute-start.3 = (bf16[128,1280]{1,0:T(8,128)(2,1)S(1)}, bf16[128,1280]{1,0:T(8,128)(2,1)S(1)}, u32[]{:S(2)}, u32[]{:S(2)}) collective-permute-start(bf16[128,1280]{1,0:T(8,128)(2,1)S(1)} %get-tuple-element.55.refs_3_.refs_4_), channel_id=1, source_target_pairs={{0,32},{1,49},{2,34},{3,51},{4,36},{5,53},{6,38},{7,55},{8,40},{9,... | collective-permute-start | bytes 983048 | tf_op jit(solution)/shard_map/ppermute | solution.py:42
  5.4 7.6 %collective-permute-start.2 = (bf16[128,1280]{1,0:T(8,128)(2,1)S(1)}, bf16[128,1280]{1,0:T(8,128)(2,1)S(1)}, u32[]{:S(2)}, u32[]{:S(2)}) collective-permute-start(bf16[128,1280]{1,0:T(8,128)(2,1)S(1)} %get-tuple-element.55.refs_3_.refs_4_), channel_id=1, source_target_pairs={{0,64},{1,193},{2,194},{3,67},{4,68},{5,197},{6,198},{7,71},{8,72}... | collective-permute-start | bytes 983048 | tf_op jit(solution)/shard_map/ppermute | solution.py:42
  10.5 10.5 %collective-permute-start = (bf16[128,2048]{1,0:T(8,128)(2,1)S(1)}, bf16[128,2048]{1,0:T(8,128)(2,1)S(1)}, u32[]{:S(2)}, u32[]{:S(2)}) collective-permute-start(bf16[128,2048]{1,0:T(8,128)(2,1)S(1)} %get-tuple-element.53), channel_id=1, source_target_pairs={{0,1},{1,0},{2,3},{3,2},{4,5},{5,4},{6,7},{7,6},{8,9},{9,8},{10,11... | collective-permute-start | bytes 1572872 | tf_op jit(solution)/shard_map/ppermute | solution.py:42
  10.6 11.5 %collective-permute-start.1 = (bf16[128,2048]{1,0:T(8,128)(2,1)S(1)}, bf16[128,2048]{1,0:T(8,128)(2,1)S(1)}, u32[]{:S(2)}, u32[]{:S(2)}) collective-permute-start(bf16[128,2048]{1,0:T(8,128)(2,1)S(1)} %get-tuple-element.54), channel_id=1, source_target_pairs={{0,1},{1,0},{2,3},{3,2},{4,5},{5,4},{6,7},{7,6},{8,9},{9,8},{10,11... | collective-permute-start | bytes 1572872 | tf_op jit(solution)/shard_map/ppermute | solution.py:42
  11.1 7.1 %collective-permute-start.7 = (bf16[128,1280]{1,0:T(8,128)(2,1)S(1)}, bf16[128,1280]{1,0:T(8,128)(2,1)S(1)}, u32[]{:S(2)}, u32[]{:S(2)}) collective-permute-start(bf16[128,1280]{1,0:T(8,128)(2,1)S(1)} %get-tuple-element.57.refs_4_.refs_5_), channel_id=1, source_target_pairs={{0,32},{1,49},{2,34},{3,51},{4,36},{5,53},{6,38},{7,55},{8,40},{9,... | collective-permute-start | bytes 983048 | tf_op jit(solution)/shard_map/ppermute | solution.py:42
  11.2 7.1 %collective-permute-start.6 = (bf16[128,1280]{1,0:T(8,128)(2,1)S(1)}, bf16[128,1280]{1,0:T(8,128)(2,1)S(1)}, u32[]{:S(2)}, u32[]{:S(2)}) collective-permute-start(bf16[128,1280]{1,0:T(8,128)(2,1)S(1)} %get-tuple-element.57.refs_4_.refs_5_), channel_id=1, source_target_pairs={{0,64},{1,193},{2,194},{3,67},{4,68},{5,197},{6,198},{7,71},{8,72}... | collective-permute-start | bytes 983048 | tf_op jit(solution)/shard_map/ppermute | solution.py:42
  13.0 14.4 %collective-permute-start.14 = (bf16[128,1280]{1,0:T(8,128)(2,1)S(1)}, bf16[128,1280]{1,0:T(8,128)(2,1)S(1)}, u32[]{:S(2)}, u32[]{:S(2)}) collective-permute-start(bf16[128,1280]{1,0:T(8,128)(2,1)S(1)} %collective-permute-done.2.refs_7_.refs_8_), channel_id=1, source_target_pairs={{0,2},{1,15},{2,0},{3,5},{4,6},{5,3},{6,4},{7,9},{8,10},{9,7},{10,... | collective-permute-start | bytes 983048 | tf_op jit(solution)/shard_map/ppermute | solution.py:42
  18.4 9.0 %collective-permute-start.8 = (bf16[128,1280]{1,0:T(8,128)(2,1)S(1)}, bf16[128,1280]{1,0:T(8,128)(2,1)S(1)}, u32[]{:S(2)}, u32[]{:S(2)}) collective-permute-start(bf16[128,1280]{1,0:T(8,128)(2,1)S(1)} %collective-permute-done.6.refs_8_.refs_9_), channel_id=1, source_target_pairs={{0,32},{1,49},{2,34},{3,51},{4,36},{5,53},{6,38},{7,55},{8,40},{9,... | collective-permute-start | bytes 983048 | tf_op jit(solution)/shard_map/ppermute | solution.py:42
  21.0 10.4 %collective-permute-start.10 = (bf16[128,1280]{1,0:T(8,128)(2,1)S(1)}, bf16[128,1280]{1,0:T(8,128)(2,1)S(1)}, u32[]{:S(2)}, u32[]{:S(2)}) collective-permute-start(bf16[128,1280]{1,0:T(8,128)(2,1)S(1)} %collective-permute-done.2.refs_7_.refs_8_), channel_id=1, source_target_pairs={{0,32},{1,49},{2,34},{3,51},{4,36},{5,53},{6,38},{7,55},{8,40},{9,... | collective-permute-start | bytes 983048 | tf_op jit(solution)/shard_map/ppermute | solution.py:42
  21.1 10.3 %collective-permute-start.4 = (bf16[128,1280]{1,0:T(8,128)(2,1)S(1)}, bf16[128,1280]{1,0:T(8,128)(2,1)S(1)}, u32[]{:S(2)}, u32[]{:S(2)}) collective-permute-start(bf16[128,1280]{1,0:T(8,128)(2,1)S(1)} %collective-permute-done.2.refs_7_.refs_8_), channel_id=1, source_target_pairs={{0,192},{1,65},{2,66},{3,195},{4,196},{5,69},{6,70},{7,199},{8,200... | collective-permute-start | bytes 983048 | tf_op jit(solution)/shard_map/ppermute | solution.py:42
  22.2 13.2 %collective-permute-start.15 = (bf16[128,1280]{1,0:T(8,128)(2,1)S(1)}, bf16[128,1280]{1,0:T(8,128)(2,1)S(1)}, u32[]{:S(2)}, u32[]{:S(2)}) collective-permute-start(bf16[128,1280]{1,0:T(8,128)(2,1)S(1)} %collective-permute-done.6.refs_8_.refs_9_), channel_id=1, source_target_pairs={{0,2},{1,15},{2,0},{3,5},{4,6},{5,3},{6,4},{7,9},{8,10},{9,7},{10,... | collective-permute-start | bytes 983048 | tf_op jit(solution)/shard_map/ppermute | solution.py:42
  27.4 10.4 %collective-permute-start.13 = (bf16[128,1280]{1,0:T(8,128)(2,1)S(1)}, bf16[128,1280]{1,0:T(8,128)(2,1)S(1)}, u32[]{:S(2)}, u32[]{:S(2)}) collective-permute-start(bf16[128,1280]{1,0:T(8,128)(2,1)S(1)} %collective-permute-done.6.refs_8_.refs_9_), channel_id=1, source_target_pairs={{0,192},{1,65},{2,66},{3,195},{4,196},{5,69},{6,70},{7,199},{8,200... | collective-permute-start | bytes 983048 | tf_op jit(solution)/shard_map/ppermute | solution.py:42
  27.4 15.1 %collective-permute-start.12 = (bf16[128,1280]{1,0:T(8,128)(2,1)S(1)}, bf16[128,1280]{1,0:T(8,128)(2,1)S(1)}, u32[]{:S(2)}, u32[]{:S(2)}) collective-permute-start(bf16[128,1280]{1,0:T(8,128)(2,1)S(1)} %collective-permute-done.8.refs_12_.refs_13_), channel_id=1, source_target_pairs={{0,2},{1,15},{2,0},{3,5},{4,6},{5,3},{6,4},{7,9},{8,10},{9,7},{10,... | collective-permute-start | bytes 983048 | tf_op jit(solution)/shard_map/ppermute | solution.py:42
  31.4 11.1 %collective-permute-start.9 = (bf16[128,1280]{1,0:T(8,128)(2,1)S(1)}, bf16[128,1280]{1,0:T(8,128)(2,1)S(1)}, u32[]{:S(2)}, u32[]{:S(2)}) collective-permute-start(bf16[128,1280]{1,0:T(8,128)(2,1)S(1)} %collective-permute-done.8.refs_12_.refs_13_), channel_id=1, source_target_pairs={{0,192},{1,65},{2,66},{3,195},{4,196},{5,69},{6,70},{7,199},{8,200... | collective-permute-start | bytes 983048 | tf_op jit(solution)/shard_map/ppermute | solution.py:42
  31.4 8.6 %collective-permute-start.11 = (bf16[128,1280]{1,0:T(8,128)(2,1)S(1)}, bf16[128,1280]{1,0:T(8,128)(2,1)S(1)}, u32[]{:S(2)}, u32[]{:S(2)}) collective-permute-start(bf16[128,1280]{1,0:T(8,128)(2,1)S(1)} %collective-permute-done.10.refs_11_.refs_12_), channel_id=1, source_target_pairs={{0,2},{1,15},{2,0},{3,5},{4,6},{5,3},{6,4},{7,9},{8,10},{9,7},{10,... | collective-permute-start | bytes 983048 | tf_op jit(solution)/shard_map/ppermute | solution.py:42
  35.4 7.1 %collective-permute-start.5 = (bf16[128,1280]{1,0:T(8,128)(2,1)S(1)}, bf16[128,1280]{1,0:T(8,128)(2,1)S(1)}, u32[]{:S(2)}, u32[]{:S(2)}) collective-permute-start(bf16[128,1280]{1,0:T(8,128)(2,1)S(1)} %collective-permute-done.4.refs_9_.refs_10_), channel_id=1, source_target_pairs={{0,32},{1,49},{2,34},{3,51},{4,36},{5,53},{6,38},{7,55},{8,40},{9,... | collective-permute-start | bytes 983048 | tf_op jit(solution)/shard_map/ppermute | solution.py:42
  43.0 2.4 %copy-start.2 = (bf16[256,1024]{1,0:T(8,128)(2,1)S(1)}, bf16[256,1024]{1,0:T(8,128)(2,1)}, u32[]{:S(2)}) copy-start(bf16[256,1024]{1,0:T(8,128)(2,1)} %grad.3) | copy-start | bytes 1572868
  43.1 2.4 %collective-permute-start.16 = (bf16[256,1280]{1,0:T(8,128)(2,1)S(1)}, bf16[256,1280]{1,0:T(8,128)(2,1)S(1)}, u32[]{:S(2)}, u32[]{:S(2)}) collective-permute-start(bf16[256,1280]{1,0:T(8,128)(2,1)S(1)} %project_late.2), channel_id=1, source_target_pairs={{0,1},{1,0},{2,3},{3,2},{4,5},{5,4},{6,7},{7,6},{8,9},{9,8},{10,11... | collective-permute-start | bytes 1966088 | tf_op jit(solution)/shard_map/ppermute | solution.py:42
  47.6 1.7 %collective-permute-start.17 = (bf16[256,640]{1,0:T(8,128)(2,1)S(1)}, bf16[256,640]{1,0:T(8,128)(2,1)S(1)}, u32[]{:S(2)}, u32[]{:S(2)}) collective-permute-start(bf16[256,640]{1,0:T(8,128)(2,1)S(1)} %get-tuple-element.76.refs_1_.refs_0_), channel_id=1, source_target_pairs={{0,1},{1,0},{2,3},{3,2},{4,5},{5,4},{6,7},{7,6},{8,9},{9,8},{10,11... | collective-permute-start | bytes 983048 | tf_op jit(solution)/shard_map/ppermute | solution.py:42
  49.3 4.1 %collective-permute-start.19 = (bf16[256,640]{1,0:T(8,128)(2,1)S(1)}, bf16[256,640]{1,0:T(8,128)(2,1)S(1)}, u32[]{:S(2)}, u32[]{:S(2)}) collective-permute-start(bf16[256,640]{1,0:T(8,128)(2,1)S(1)} %attend_high.1.refs_1_.refs_2_), channel_id=1, source_target_pairs={{0,1},{1,0},{2,3},{3,2},{4,5},{5,4},{6,7},{7,6},{8,9},{9,8},{10,11... | collective-permute-start | bytes 983048 | tf_op jit(solution)/shard_map/ppermute | solution.py:42
  51.1 17.8 %collective-permute-start.18 = (bf16[8,128,640]{2,1,0:T(8,128)(2,1)S(1)}, bf16[8,128,640]{2,1,0:T(8,128)(2,1)S(1)}, u32[]{:S(2)}, u32[]{:S(2)}) collective-permute-start(bf16[8,128,640]{2,1,0:T(8,128)(2,1)S(1)} %terms.4), channel_id=1, source_target_pairs={{0,64},{1,193},{2,66},{3,195},{4,68},{5,197},{6,70},{7,199},{8,72}... | collective-permute-start | bytes 3932168 | tf_op jit(solution)/shard_map/ppermute | solution.py:42
  54.4 17.8 %collective-permute-start.25 = (bf16[8,128,640]{2,1,0:T(8,128)(2,1)S(1)}, bf16[8,128,640]{2,1,0:T(8,128)(2,1)S(1)}, u32[]{:S(2)}, u32[]{:S(2)}) collective-permute-start(bf16[8,128,640]{2,1,0:T(8,128)(2,1)S(1)} %terms.5), channel_id=1, source_target_pairs={{0,32},{1,49},{2,34},{3,51},{4,36},{5,53},{6,38},{7,55},{8,40},{9,... | collective-permute-start | bytes 3932168 | tf_op jit(solution)/shard_map/ppermute | solution.py:42
  58.7 3.0 %collective-permute-start.20 = (bf16[256,2048]{1,0:T(8,128)(2,1)S(1)}, bf16[256,2048]{1,0:T(8,128)(2,1)S(1)}, u32[]{:S(2)}, u32[]{:S(2)}) collective-permute-start(bf16[256,2048]{1,0:T(8,128)(2,1)S(1)} %get-tuple-element.80), channel_id=1, source_target_pairs={{0,1},{1,0},{2,3},{3,2},{4,5},{5,4},{6,7},{7,6},{8,9},{9,8},{10,11... | collective-permute-start | bytes 3145736 | tf_op jit(solution)/shard_map/ppermute | solution.py:42
  69.0 6.3 %collective-permute-start.22 = (bf16[2,128,640]{2,1,0:T(8,128)(2,1)S(1)}, bf16[2,128,640]{2,1,0:T(8,128)(2,1)S(1)}, u32[]{:S(2)}, u32[]{:S(2)}) collective-permute-start(bf16[2,128,640]{2,1,0:T(8,128)(2,1)S(1)} %get-tuple-element.92), channel_id=1, source_target_pairs={{0,192},{1,65},{2,194},{3,67},{4,196},{5,69},{6,198},{7,71},{8,200... | collective-permute-start | bytes 983048 | tf_op jit(solution)/shard_map/ppermute | solution.py:42
  72.3 6.3 %collective-permute-start.27 = (bf16[2,128,640]{2,1,0:T(8,128)(2,1)S(1)}, bf16[2,128,640]{2,1,0:T(8,128)(2,1)S(1)}, u32[]{:S(2)}, u32[]{:S(2)}) collective-permute-start(bf16[2,128,640]{2,1,0:T(8,128)(2,1)S(1)} %get-tuple-element.97), channel_id=1, source_target_pairs={{0,48},{1,33},{2,50},{3,35},{4,52},{5,37},{6,54},{7,39},{8,56},{9,... | collective-permute-start | bytes 983048 | tf_op jit(solution)/shard_map/ppermute | solution.py:42
  72.4 6.9 %collective-permute-start.21 = (bf16[2,128,640]{2,1,0:T(8,128)(2,1)S(1)}, bf16[2,128,640]{2,1,0:T(8,128)(2,1)S(1)}, u32[]{:S(2)}, u32[]{:S(2)}) collective-permute-start(bf16[2,128,640]{2,1,0:T(8,128)(2,1)S(1)} %get-tuple-element.91), channel_id=1, source_target_pairs={{0,192},{1,65},{2,194},{3,67},{4,196},{5,69},{6,198},{7,71},{8,200... | collective-permute-start | bytes 983048 | tf_op jit(solution)/shard_map/ppermute | solution.py:42
  75.5 9.1 %collective-permute-start.23 = (bf16[2,128,640]{2,1,0:T(8,128)(2,1)S(1)}, bf16[2,128,640]{2,1,0:T(8,128)(2,1)S(1)}, u32[]{:S(2)}, u32[]{:S(2)}) collective-permute-start(bf16[2,128,640]{2,1,0:T(8,128)(2,1)S(1)} %add.21), channel_id=1, source_target_pairs={{0,32},{1,49},{2,34},{3,51},{4,36},{5,53},{6,38},{7,55},{8,40},{9,... | collective-permute-start | bytes 983048 | tf_op jit(solution)/shard_map/ppermute | solution.py:42
  78.0 9.4 %collective-permute-start.26 = (bf16[2,128,640]{2,1,0:T(8,128)(2,1)S(1)}, bf16[2,128,640]{2,1,0:T(8,128)(2,1)S(1)}, u32[]{:S(2)}, u32[]{:S(2)}) collective-permute-start(bf16[2,128,640]{2,1,0:T(8,128)(2,1)S(1)} %get-tuple-element.96), channel_id=1, source_target_pairs={{0,48},{1,33},{2,50},{3,35},{4,52},{5,37},{6,54},{7,39},{8,56},{9,... | collective-permute-start | bytes 983048 | tf_op jit(solution)/shard_map/ppermute | solution.py:42
  78.7 8.7 %collective-permute-start.28 = (bf16[2,128,640]{2,1,0:T(8,128)(2,1)S(1)}, bf16[2,128,640]{2,1,0:T(8,128)(2,1)S(1)}, u32[]{:S(2)}, u32[]{:S(2)}) collective-permute-start(bf16[2,128,640]{2,1,0:T(8,128)(2,1)S(1)} %add.24), channel_id=1, source_target_pairs={{0,64},{1,193},{2,66},{3,195},{4,68},{5,197},{6,70},{7,199},{8,72}... | collective-permute-start | bytes 983048 | tf_op jit(solution)/shard_map/ppermute | solution.py:42
  84.8 4.4 %collective-permute-start.24 = (bf16[1,128,640]{2,1,0:T(8,128)(2,1)S(1)}, bf16[1,128,640]{2,1,0:T(8,128)(2,1)S(1)}, u32[]{:S(2)}, u32[]{:S(2)}) collective-permute-start(bf16[1,128,640]{2,1,0:T(8,128)(2,1)S(1)} %get-tuple-element.94), channel_id=1, source_target_pairs={{0,48},{1,33},{2,50},{3,35},{4,52},{5,37},{6,54},{7,39},{8,56},{9,... | collective-permute-start | bytes 491528 | tf_op jit(solution)/shard_map/ppermute | solution.py:42
  87.6 4.3 %collective-permute-start.29 = (bf16[1,128,640]{2,1,0:T(8,128)(2,1)S(1)}, bf16[1,128,640]{2,1,0:T(8,128)(2,1)S(1)}, u32[]{:S(2)}, u32[]{:S(2)}) collective-permute-start(bf16[1,128,640]{2,1,0:T(8,128)(2,1)S(1)} %get-tuple-element.99), channel_id=1, source_target_pairs={{0,192},{1,65},{2,194},{3,67},{4,196},{5,69},{6,198},{7,71},{8,200... | collective-permute-start | bytes 491528 | tf_op jit(solution)/shard_map/ppermute | solution.py:42
  123.4 16.9 %collective-permute-start.30 = (bf16[16,16,1280]{2,1,0:T(8,128)(2,1)S(1)}, bf16[16,16,1280]{2,1,0:T(8,128)(2,1)S(1)}, u32[]{:S(2)}, u32[]{:S(2)}) collective-permute-start(bf16[16,16,1280]{2,1,0:T(8,128)(2,1)S(1)} %all_to_all.16.got.mine), channel_id=1, source_target_pairs={{0,1},{1,0},{2,3},{3,2},{4,5},{5,4},{6,7},{7,6},{8,9},{9,8},{10,11... | collective-permute-start | bytes 1966088 | tf_op jit(solution)/shard_map/ppermute | solution.py:42
  (5 other events, 10.5 us)
